TPU v7x, 256 devices: a whole 4x4x8 slice. The times are simulated.
256 devices in a mesh: grp: 4 (over x), seq: 16 (over z, core), tp: 4 (over y).
Axes of the slice: x: 4, y: 4, z: 8, core: 2. Of those that a mesh axis runs over, the one named last changes fastest.
Arguments:
- queries: bfloat16 [6144, 4096], P('seq', ('grp', 'tp')), may hold values from -5.5 to 5.5
- neighbour_states: bfloat16 [2, 96, 128, 4096], P(None, 'seq', None, ('grp', 'tp')), may hold values from -5.5 to 5.5
- retrieved: int32 [96, 2], P('seq'), may hold values from 0 to 95, as said below
- valid_blocks: int32 [96, 2], P('seq'), may hold values 0 or 1
- output_weight: bfloat16 [4096, 8192], P(('grp', 'tp')), may hold values from -0.75 to 0.75
- attention_cotangent: bfloat16 [6144, 4096], P('seq', ('grp', 'tp')), may hold values from -48 to 48
Outputs:
- layer_output: bfloat16 [6144, 8192], P('seq', ('grp', 'tp'))
- neighbour_gradient: bfloat16 [2, 96, 128, 4096], P(None, 'seq', None, ('grp', 'tp'))
Inputs may be any that keep to these rules, and one draw needn't show every extreme that they name: `retrieved`: entries are store rows; row n is held by owner n // 6. Among the 12 entries of the spans of one index of seq, at most 2 name rows of one owner, and one owner, drawn from the seed, is named exactly 2 times by the spans of every index of seq.
All inputs are finite; a program needn't handle non-finite values. No bound on the sum of `valid_blocks` on one device may be relied on, other than what follows from the above.
Results may differ from a plain program's by a relative error of at most 0.019.
Values may be sent and summed in bfloat16 or wider, within the bound.
No kernel may reach another device: no remote copies, remote signals or barrier semaphores. Data moves between devices by JAX's collectives and lax.ppermute only.
A program may use at most 128 MiB of HBM per device.

v0:
```python
import jax
import jax.numpy as jnp
from jax import lax
from jax.sharding import PartitionSpec as P

HDIM = 128
SPAN = 64
NTOK = 128
KNB = 2


def passed_along(value, axis, steps):
    count = lax.axis_size(axis)
    initial, last = (max(0, -steps), min(count, count - steps))
    return lax.ppermute(value, axis, [(source, source + steps) for source in range(initial, last)])


def block_attention(query_blocks, cotangent_blocks, states, live_table):
    blocks, row_count, feature_count = query_blocks.shape
    heads_here = feature_count // HDIM
    score_scale = HDIM ** (-0.5)
    query_heads = query_blocks.reshape(blocks, row_count, heads_here, HDIM)
    cotangent_heads = cotangent_blocks.reshape(blocks, row_count, heads_here, HDIM)
    key_heads = states[0].reshape(blocks, KNB * NTOK, heads_here, HDIM)
    value_heads = states[1].reshape(blocks, KNB * NTOK, heads_here, HDIM)
    live_keys = (jnp.repeat(live_table, NTOK, axis=1) > 0)[:, None, None, :]
    scores = (
        jnp.einsum("bqhd,bkhd->bhqk", query_heads, key_heads, preferred_element_type=jnp.float32)
        * score_scale
    )
    row_max = jnp.max(jnp.where(live_keys, scores, -1e30), axis=-1, keepdims=True)
    unnormed = jnp.where(live_keys, jnp.exp(scores - row_max), 0.0)
    soft_weights = unnormed / jnp.maximum(jnp.sum(unnormed, axis=-1, keepdims=True), 1.0)
    rounded_weights = soft_weights.astype(jnp.bfloat16)
    attended = jnp.einsum(
        "bhqk,bkhd->bqhd", rounded_weights, value_heads, preferred_element_type=jnp.float32
    )
    attended = attended.astype(jnp.bfloat16).reshape(blocks, row_count, feature_count)
    weight_grads = jnp.einsum(
        "bqhd,bkhd->bhqk", cotangent_heads, value_heads, preferred_element_type=jnp.float32
    )
    row_delta = jnp.sum(soft_weights * weight_grads, axis=-1, keepdims=True)
    score_grads = (soft_weights * (weight_grads - row_delta)).astype(jnp.bfloat16)
    key_grad = (
        jnp.einsum("bhqk,bqhd->bkhd", score_grads, query_heads, preferred_element_type=jnp.float32)
        * score_scale
    )
    value_grad = jnp.einsum(
        "bhqk,bqhd->bkhd", rounded_weights, cotangent_heads, preferred_element_type=jnp.float32
    )
    pair_grads = jnp.stack([key_grad, value_grad]).reshape(2, blocks, KNB, NTOK, feature_count)
    return (attended, pair_grads)


def local(queries, neighbour_states, retrieved, valid_blocks, output_weight, attention_cotangent):
    owners = lax.axis_size("seq")
    tok_rows, feature_count = queries.shape
    span_count = tok_rows // SPAN
    request_count = span_count * KNB
    store_rows = neighbour_states.shape[1]
    capacity = max(2, (request_count + owners - 1) // owners + request_count // (4 * owners))
    slot_count = owners * capacity
    flat_ids = retrieved.reshape(request_count)
    owner_of = flat_ids // store_rows
    local_row = flat_ids % store_rows
    request_index = jnp.arange(request_count, dtype=jnp.int32)
    same_owner = owner_of[:, None] == owner_of[None, :]
    earlier = request_index[None, :] < request_index[:, None]
    position = jnp.sum(same_owner & earlier, axis=1)
    slot_of = owner_of * capacity + position
    slot_hits = slot_of[:, None] == jnp.arange(slot_count, dtype=jnp.int32)[None, :]
    requested = jnp.sum(jnp.where(slot_hits, local_row[:, None] + 1, 0), axis=0) - 1
    sender_of = jnp.sum(jnp.where(slot_hits, request_index[:, None] + 1, 0), axis=0) - 1
    incoming = lax.all_to_all(requested, "seq", split_axis=0, concat_axis=0, tiled=True)
    present = incoming >= 0
    picked = jnp.take(neighbour_states, jnp.maximum(incoming, 0), axis=1)
    picked = jnp.where(present[None, :, None, None], picked, jnp.zeros_like(picked))
    arrived = lax.all_to_all(picked, "seq", split_axis=1, concat_axis=1, tiled=True)
    fetched = jnp.take(arrived, slot_of, axis=1).reshape(2, span_count, KNB, NTOK, feature_count)
    lead_rows = SPAN - 1
    last_states = fetched[:, span_count - 1]
    last_live = valid_blocks[span_count - 1].astype(jnp.bfloat16)
    prior_states, prior_live = passed_along((last_states, last_live), "seq", 1)
    states = jnp.concatenate([prior_states[:, None], fetched], axis=1)
    live_table = jnp.concatenate(
        [(prior_live > 0).astype(jnp.int32)[None, :], valid_blocks], axis=0
    )
    front_pad = jnp.zeros((1, feature_count), jnp.bfloat16)
    back_pad = jnp.zeros((lead_rows, feature_count), jnp.bfloat16)
    query_blocks = jnp.concatenate([front_pad, queries, back_pad]).reshape(
        span_count + 1, SPAN, feature_count
    )
    cotangent_blocks = jnp.concatenate([front_pad, attention_cotangent, back_pad]).reshape(
        span_count + 1, SPAN, feature_count
    )
    attended, block_grads = block_attention(query_blocks, cotangent_blocks, states, live_table)
    attention = attended.reshape((span_count + 1) * SPAN, feature_count)[1 : tok_rows + 1]
    returned = passed_along(block_grads[:, 0].astype(jnp.bfloat16), "seq", -1).astype(jnp.float32)
    pair_grads = block_grads[:, 1:].at[:, span_count - 1].add(returned)
    request_grads = pair_grads.reshape(2, request_count, NTOK, feature_count).astype(jnp.bfloat16)
    outgoing = jnp.take(request_grads, jnp.maximum(sender_of, 0), axis=1)
    outgoing = jnp.where((sender_of >= 0)[None, :, None, None], outgoing, jnp.zeros_like(outgoing))
    returned_grads = lax.all_to_all(outgoing, "seq", split_axis=1, concat_axis=1, tiled=True)
    owner_hits = (incoming[None, :] == jnp.arange(store_rows, dtype=jnp.int32)[:, None]).astype(
        jnp.bfloat16
    )
    neighbour_gradient = jnp.einsum(
        "ns,kstw->kntw", owner_hits, returned_grads, preferred_element_type=jnp.float32
    ).astype(jnp.bfloat16)
    partial_value = jnp.dot(attention, output_weight, preferred_element_type=jnp.float32)
    layer_output = lax.psum_scatter(
        partial_value.astype(jnp.bfloat16), ("grp", "tp"), scatter_dimension=1, tiled=True
    )
    return (layer_output, neighbour_gradient)


def solution(mesh):
    placed = (
        P("seq", ("grp", "tp")),
        P(None, "seq", None, ("grp", "tp")),
        P("seq", None),
        P("seq", None),
        P(("grp", "tp"), None),
        P("seq", ("grp", "tp")),
    )
    return jax.shard_map(
        local,
        mesh=mesh,
        in_specs=placed,
        out_specs=(P("seq", ("grp", "tp")), P(None, "seq", None, ("grp", "tp"))),
        check_vma=False,
    )
```

profile of v0, /device:TPU:1, one launch (start us, length us, event | category | flops | bytes accessed | tf_op | source)
XLA Modules:
  0.0 312.2 jit_solution(3308251000143309297)
XLA Ops:
  8.7 16.8 %all_to_all.19 = s32[16,2,1]{1,2,0:T(1,128)S(1)} all-to-all(s32[16,2,1]{1,2,0:T(1,128)S(1)} %bitcast.73), channel_id=1, replica_groups=mesh['grp'=4,'seq'=16,'tp'=4] {'seq'}, dimensions={0} | all-to-all | bytes 256 | tf_op jit(solution)/shard_map/all_to_all | solution.py:74
  26.9 2.8 gather_fusion
  29.7 4.7 %select_bitcast_fusion.1 = bf16[2,32,128,256]{3,2,0,1:T(8,128)(2,1)} fusion(bf16[32,2,128,256]{3,2,1,0:T(8,128)(2,1)} %gather_fusion, pred[32]{0:T(512)(128)(4,1)S(1)} %get-tuple-element.37, pred[32]{0:T(512)(128)(4,1)S(1)} %get-tuple-element.36), kind=kLoop, calls=%fused_computation.12 | loop fusion | flops 4194304 | bytes 8388672 | tf_op jit(solution)/shard_map/jit(_where)/select_n | solution.py:77
  34.4 5.0 %all-to-all-start.1 = ((bf16[2,32,128,256]{3,2,0,1:T(8,128)(2,1)}), bf16[2,32,128,256]{3,2,0,1:T(8,128)(2,1)}, u32[]{:S(2)}, u32[]{:S(2)}) async-start(bf16[2,32,128,256]{3,2,0,1:T(8,128)(2,1)} %select_bitcast_fusion.1), calls=%async_computation.1 | async-start | bytes 8388608 | tf_op jit(solution)/shard_map/all_to_all | solution.py:78
  39.7 3.5 %collective-permute-start.1 = (bf16[2]{0:T(256)(128)(2,1)S(1)}, bf16[2]{0:T(256)(128)(2,1)S(1)}, u32[]{:S(2)}, u32[]{:S(2)}) collective-permute-start(bf16[2]{0:T(256)(128)(2,1)S(1)} %slice_reduce_fusion), channel_id=1, source_target_pairs={{0,4},{4,8},{8,12},{12,16},{16,20},{20,24},{24,28},{28,32},{32,36}... | collective-permute-start | bytes 20 | tf_op jit(solution)/shard_map/ppermute | solution.py:15
  43.9 86.2 %collective-permute-done.1 = bf16[2]{0:T(256)(128)(2,1)S(1)} collective-permute-done((bf16[2]{0:T(256)(128)(2,1)S(1)}, bf16[2]{0:T(256)(128)(2,1)S(1)}, u32[]{:S(2)}, u32[]{:S(2)}) %collective-permute-start.1) | collective-permute-done | bytes 36 | tf_op jit(solution)/shard_map/ppermute | solution.py:15
  130.2 2.9 all-to-all-done.1
  133.1 4.7 %copy.65 = bf16[2,32,128,256]{3,2,1,0:T(8,128)(2,1)} copy(bf16[2,32,128,256]{3,2,0,1:T(8,128)(2,1)} %all-to-all-done.1) | data formatting | bytes 8388608 | tf_op jit(solution)/shard_map/all_to_all | solution.py:78
  137.8 2.8 gather_fusion.1
  141.0 2.5 collective-permute-start
  143.7 3.0 collective-permute-done
  146.8 1.2 reshape_squeeze.7
  148.0 1.1 reshape_squeeze.6
  149.7 1.4 fusion.61
  151.1 2.3 fusion.14
  153.5 1.2 copy.72
  154.7 6.7 %convolution_convert_fusion = bf16[384,8192]{1,0:T(8,128)(2,1)} fusion(bf16[256,8192]{1,0:T(8,128)(2,1)} %param.12, bf16[448,256]{1,0:T(8,128)(2,1)S(1)} %bitcast.71), kind=kOutput, calls=%fused_computation.4 | convolution fusion | flops 1613758464 | bytes 10682368 | tf_op jit(solution)/shard_map/dot_general | solution.py:110
  161.4 1.4 multiply_reduce_fusion
  162.8 3.2 %multiply_bitcast_fusion = f32[7,256,2,128]{1,3,2,0:T(8,128)S(1)} fusion(f32[7,2,64,256]{3,2,1,0:T(8,128)} %get-tuple-element.43, f32[7,2,64]{2,1,0:T(2,128)S(1)} %get-tuple-element.42, bf16[7,64,2,128]{3,2,1,0:T(2,128)(2,1)S(1)} %reshape_reshape.9, f32[7,2,64]{2,1,0:T(2,128)S(1)} %broadcast_maximum_fusion, ...), kind=kOutput, calls=%fused_computation.16 | convolution fusion | flops 60785792 | bytes 3908352 | tf_op jit(solution)/shard_map/bhqk,bqhd->bkhd/dot_general | solution.py:45
  166.0 2.1 stack.9
  168.1 2.8 copy.77
  171.0 3.2 %convolution_bitcast_fusion = f32[7,256,2,128]{1,3,2,0:T(8,128)} fusion(bf16[7,64,2,128]{3,2,1,0:T(2,128)(2,1)S(1)} %reshape_reshape.11, f32[7,2,64]{2,1,0:T(2,128)S(1)} %broadcast_maximum_fusion, f32[7,2,64,256]{3,2,1,0:T(8,128)S(1)} %convolution_multiply_fusion, pred[7,256]{1,0:T(8,128)(4,1)S(1)} %broadcast_bitcast_fusion), kind=kOutput, calls=%fused_computation.18 | convolution fusion | flops 59868288 | bytes 2987264 | tf_op jit(solution)/shard_map/bhqk,bqhd->bkhd/dot_general | solution.py:48
  174.1 3.0 stack.10
  177.2 4.0 %copy.78 = f32[1,7,2,128,256]{4,3,2,0,1:T(8,128)} copy(f32[1,7,2,128,256]{3,2,4,1,0:T(2,128)} %stack.10) | data formatting | bytes 3670016 | tf_op jit(solution)/shard_map/stack | solution.py:51
  181.2 1.1 fusion.28
  182.3 1.9 collective-permute-start.2
  184.6 6.2 %collective-permute-done.2 = bf16[2,2,128,256]{3,2,1,0:T(8,128)(2,1)S(1)} collective-permute-done((bf16[2,2,128,256]{3,2,1,0:T(8,128)(2,1)S(1)}, bf16[2,2,128,256]{3,2,1,0:T(8,128)(2,1)S(1)}, u32[]{:S(2)}, u32[]{:S(2)}) %collective-permute-start.2) | collective-permute-done | bytes 262176 | tf_op jit(solution)/shard_map/ppermute | solution.py:15
  190.9 1.1 copy-done.3
  192.0 4.3 %gather_fusion.2 = bf16[32,2,128,256]{3,2,1,0:T(8,128)(2,1)} fusion(bf16[2,12,128,256]{3,2,1,0:T(8,128)(2,1)} %bitcast.67, s32[1024]{0:T(1024)S(1)} %pad_clamp_fusion), kind=kCustom, calls=%fused_computation.2 | custom fusion | bytes 8388736 | tf_op jit(solution)/shard_map/jit(_take)/gather | solution.py:101
  196.3 3.0 select_bitcast_fusion
  199.3 102.6 %all_to_all.20 = bf16[2,32,128,256]{3,2,0,1:T(8,128)(2,1)S(1)} all-to-all(bf16[2,32,128,256]{3,2,0,1:T(8,128)(2,1)S(1)} %select_bitcast_fusion), channel_id=1, replica_groups=mesh['grp'=4,'seq'=16,'tp'=4] {'seq'}, dimensions={1} | all-to-all | bytes 8388608 | tf_op jit(solution)/shard_map/all_to_all | solution.py:103
  301.9 2.4 fusion.7
  (70 shorter events, 6.8 us)
Async XLA Ops:
  7.2 19.7 %copy-start = (bf16[2,6,128,256]{3,2,1,0:T(8,128)(2,1)S(1)}, bf16[2,6,128,256]{3,2,1,0:T(8,128)(2,1)}, u32[]{:S(2)}) copy-start(bf16[2,6,128,256]{3,2,1,0:T(8,128)(2,1)} %param.9) | copy-start | bytes 2359300
  34.4 5.1 %copy-start.8 = (s32[6,2]{0,1:T(2,128)S(1)}, s32[6,2]{0,1:T(2,128)}, u32[]{:S(2)}) copy-start(s32[6,2]{0,1:T(2,128)} %param.11) | copy-start | bytes 148
  34.4 9.2 %copy-start.6 = (bf16[384,256]{1,0:T(8,128)(2,1)S(1)}, bf16[384,256]{1,0:T(8,128)(2,1)}, u32[]{:S(2)}) copy-start(bf16[384,256]{1,0:T(8,128)(2,1)} %param.13) | copy-start | bytes 589828
  34.4 9.2 %copy-start.7 = (bf16[384,256]{1,0:T(8,128)(2,1)S(1)}, bf16[384,256]{1,0:T(8,128)(2,1)}, u32[]{:S(2)}) copy-start(bf16[384,256]{1,0:T(8,128)(2,1)} %param.8) | copy-start | bytes 589828
  34.4 98.7 %all-to-all-start.1 = ((bf16[2,32,128,256]{3,2,0,1:T(8,128)(2,1)}), bf16[2,32,128,256]{3,2,0,1:T(8,128)(2,1)}, u32[]{:S(2)}, u32[]{:S(2)}) async-start(bf16[2,32,128,256]{3,2,0,1:T(8,128)(2,1)} %select_bitcast_fusion.1), calls=%async_computation.1 | async-start | bytes 8388608 | tf_op jit(solution)/shard_map/all_to_all | solution.py:78
  39.4 265.9 %reduce-scatter.2.cloned.1.call-start = ((), (), s32[]{:S(2)}) async-start(), calls=%async_computation.4 | async-start | bytes 6684672 | tf_op jit(solution)/shard_map/reduce_scatter | solution.py:111
  39.7 90.4 %collective-permute-start.1 = (bf16[2]{0:T(256)(128)(2,1)S(1)}, bf16[2]{0:T(256)(128)(2,1)S(1)}, u32[]{:S(2)}, u32[]{:S(2)}) collective-permute-start(bf16[2]{0:T(256)(128)(2,1)S(1)} %slice_reduce_fusion), channel_id=1, source_target_pairs={{0,4},{4,8},{8,12},{12,16},{16,20},{20,24},{24,28},{28,32},{32,36}... | collective-permute-start | bytes 20 | tf_op jit(solution)/shard_map/ppermute | solution.py:15
  141.0 5.6 %collective-permute-start = (bf16[2,2,128,256]{3,2,1,0:T(8,128)(2,1)S(1)}, bf16[2,2,128,256]{3,2,1,0:T(8,128)(2,1)S(1)}, u32[]{:S(2)}, u32[]{:S(2)}) collective-permute-start(bf16[2,2,128,256]{3,2,1,0:T(8,128)(2,1)S(1)} %slice_bitcast_fusion), channel_id=1, source_target_pairs={{0,4},{4,8},{8,12},{12,16},{16,20},{20,24},{24,28},{28,32},{32,36}... | collective-permute-start | bytes 786440 | tf_op jit(solution)/shard_map/ppermute | solution.py:15
  148.0 1.3 copy-start.4
  149.3 1.8 copy-start.5
  181.2 3.1 copy-start.2
  182.3 8.5 %collective-permute-start.2 = (bf16[2,2,128,256]{3,2,1,0:T(8,128)(2,1)S(1)}, bf16[2,2,128,256]{3,2,1,0:T(8,128)(2,1)S(1)}, u32[]{:S(2)}, u32[]{:S(2)}) collective-permute-start(bf16[2,2,128,256]{3,2,1,0:T(8,128)(2,1)S(1)} %fusion.28), channel_id=1, source_target_pairs={{4,0},{8,4},{12,8},{16,12},{20,16},{24,20},{28,24},{32,28},{36,32}... | collective-permute-start | bytes 786440 | tf_op jit(solution)/shard_map/ppermute | solution.py:15
  190.9 1.1 copy-start.3
  301.9 3.5 %copy-start.1 = (bf16[2,6,128,256]{3,2,1,0:T(8,128)(2,1)S(1)}, bf16[2,6,128,256]{3,2,1,0:T(8,128)(2,1)}, u32[]{:S(2)}) copy-start(bf16[2,6,128,256]{3,2,1,0:T(8,128)(2,1)} %param.9) | copy-start | bytes 2359300
Sparse Core Ops, SparseCore 0:
  161.5 87.7 reduce-scatter.1
where the time goes:
time: 313 us; the launch traced here: 312 us
  blocking collectives  119 us (38%)
  waiting for transfers between devices  98.2 us (31%)
  local copies, waits for them, and re-layouts  35.4 us (11%)
  matrix products  19.6 us (6%)
  between operations  14.3 us (5%)
  starting transfers between devices  13 us (4%)
  other arithmetic  12.2 us (4%)
    all_to_all x1, blocking collectives, local(): lax.all_to_all(outgoing, 'seq', split_axis=1, concat_axis=1, tiled=True)  103 us
    ppermute x3, waiting for transfers between devices, passed_along(): lax.ppermute(value, axis, [(source, source + steps) for source in range(i...  95.3 us
    all_to_all x1, blocking collectives, local(): lax.all_to_all(requested, 'seq', split_axis=0, concat_axis=0, tiled=True)  16.8 us
    another operation x4, local copies, waits for them, and re-layouts, block_attention(): jnp.stack([key_grad, value_grad])  12 us
    ppermute x3, starting transfers between devices, passed_along(): lax.ppermute(value, axis, [(source, source + steps) for source in range(i...  7.96 us
    dot_general x1, matrix products, local(): jnp.dot(attention, output_weight, preferred_element_type=jnp.float32)  6.67 us
  transfers between devices with their start and end apart: 5, of which 4 were waited for; matrix products, arithmetic and copies ran while one was open for 11% of the time, Pallas kernels for 0%

commit v1 on v0

v1 whole, which is shorter than its diff:
```python
import functools

import jax
import jax.numpy as jnp
from jax import lax
from jax.experimental import pallas as pl
from jax.experimental.pallas import tpu as pltpu
from jax.sharding import PartitionSpec as P

HDIM = 128
SPAN = 64
NTOK = 128
KNB = 2
CAP = 2
LEAD = SPAN - 1
FEATS = ("grp", "tp")
NT = (((1,), (1,)), ((), ()))
NN = (((1,), (0,)), ((), ()))
TN = (((0,), (0,)), ((), ()))
VMEM = pl.BlockSpec(memory_space=pltpu.VMEM)
SMEM = pl.BlockSpec(memory_space=pltpu.SMEM)
ANY = pl.BlockSpec(memory_space=pl.ANY)
LIMIT = pltpu.CompilerParams(vmem_limit_bytes=48 * 1024 * 1024)


def dot(a, b, dims):
    return lax.dot_general(a, b, dims, preferred_element_type=jnp.float32)


def three_parts(x):
    high = x.astype(jnp.bfloat16).astype(jnp.float32)
    middle = (x - high).astype(jnp.bfloat16).astype(jnp.float32)
    return [high, middle, x - high - middle]


def fill_window(rows_hbm, rows, sem):
    count = rows_hbm.shape[0]
    copy = pltpu.make_async_copy(rows_hbm, rows.at[pl.ds(0, count)], sem)
    copy.start()
    rows[pl.ds(count, SPAN), :] = jnp.zeros((SPAN, rows.shape[1]), rows.dtype)
    copy.wait()


def decode_slot(code):
    return code % 128, (code // 128) % 8, code // 1024


def pair_forward(slots, rows_hbm, states, out, rows, sem):
    fill_window(rows_hbm, rows, sem)
    width = states.shape[3]
    scale = HDIM ** (-0.5)

    def one_target(target, carry):
        stat_rows = []
        for place in range(CAP):
            span, row, _ = decode_slot(slots[target * CAP + place])
            tokens = rows[pl.ds(pl.multiple_of(span * SPAN, SPAN), 2 * SPAN), :]
            lse_heads, delta_heads, attended = [], [], []
            for at in range(0, width, HDIM):
                q = tokens[:, at : at + HDIM]
                g = tokens[:, width + at : width + at + HDIM]
                k = states[0, row, :, at : at + HDIM]
                v = states[1, row, :, at : at + HDIM]
                scores = dot(k, q, NT) * scale
                grads = dot(v, g, NT)
                top = jnp.max(scores, axis=0, keepdims=True)
                weights = jnp.exp(scores - top)
                total = jnp.sum(weights, axis=0, keepdims=True)
                weights = weights * (1.0 / total)
                lse_heads.append(top + jnp.log(total))
                delta_heads.append(jnp.sum(weights * grads, axis=0, keepdims=True))
                mixed = dot(weights.astype(jnp.bfloat16), v, TN)
                attended.append(mixed[LEAD : LEAD + SPAN])
            out[target, pl.ds(place * SPAN, SPAN), :] = jnp.concatenate(attended, 1).astype(out.dtype)
            stat_rows += three_parts(jnp.concatenate(lse_heads, 1))
            stat_rows += three_parts(jnp.concatenate(delta_heads, 1))
            stat_rows += [jnp.zeros((2, width), jnp.float32)]
        out[target, pl.ds(CAP * SPAN, 16), :] = jnp.concatenate(stat_rows, 0).astype(out.dtype)
        return carry

    lax.fori_loop(0, out.shape[0], one_target, 0)


def merge_pairs(requests, arrived, attention, stats):
    width = arrived.shape[2]
    for span in range(stats.shape[0]):
        lse, delta, live, parts = [], [], [], []
        for k in range(KNB):
            code = requests[span * KNB + k]
            owner, place, valid = code % 16, (code // 16) % 2, code // 32 > 0
            both = arrived[owner, pl.ds(CAP * SPAN, 16), :].astype(jnp.float32)
            mine = jnp.where(place == 0, both[0:8], both[8:16])
            lse.append(jnp.where(valid, mine[0:1] + (mine[1:2] + mine[2:3]), -1e30))
            delta.append(jnp.where(valid, mine[3:4] + (mine[4:5] + mine[5:6]), 0.0))
            live.append(valid)
            rows = arrived[owner, pl.ds(pl.multiple_of(place * SPAN, SPAN), SPAN), :]
            parts.append(jnp.where(valid, rows.astype(jnp.float32), 0.0))
        top = jnp.maximum(lse[0], lse[1])
        share = [jnp.where(live[k], jnp.exp(lse[k] - top), 0.0) for k in range(KNB)]
        total = jnp.maximum(share[0] + share[1], 1.0)
        share = [each / total for each in share]
        lse_all = top + jnp.log(total)
        delta_all = share[0] * delta[0] + share[1] * delta[1]
        heads = range(0, width, HDIM)
        stats[span] = jnp.concatenate(
            [lse_all[:, at : at + HDIM] for at in heads] + [delta_all[:, at : at + HDIM] for at in heads], 0
        )
        lines = [each[:, at : at + HDIM] for each in share for at in heads]
        square = jnp.concatenate(lines + [jnp.zeros((HDIM - len(lines), HDIM), jnp.float32)], 0).T
        columns = square[LEAD : LEAD + SPAN]
        count = len(heads)
        mixed = [
            parts[0][:, at : at + HDIM] * columns[:, h : h + 1]
            + parts[1][:, at : at + HDIM] * columns[:, count + h : count + h + 1]
            for h, at in enumerate(heads)
        ]
        attention[pl.ds(span * SPAN, SPAN), :] = jnp.concatenate(mixed, 1).astype(attention.dtype)


def pair_backward(slots, rows_hbm, states, stats, out, rows, total, sem):
    fill_window(rows_hbm, rows, sem)
    total[...] = jnp.zeros_like(total)
    width = states.shape[3]
    heads = width // HDIM
    scale = HDIM ** (-0.5)
    lane = lax.broadcasted_iota(jnp.int32, (NTOK, 2 * SPAN), 1)
    inside = (lane >= LEAD) & (lane < LEAD + SPAN)

    def one_target(target, carry):
        for place in range(CAP):
            span, row, live = decode_slot(slots[target * CAP + place])
            tokens = rows[pl.ds(pl.multiple_of(span * SPAN, SPAN), 2 * SPAN), :]
            lines = stats[span]
            seen = inside & (live > 0)
            for h in range(heads):
                at = h * HDIM
                q = tokens[:, at : at + HDIM]
                g = tokens[:, width + at : width + at + HDIM]
                k = states[0, row, :, at : at + HDIM]
                v = states[1, row, :, at : at + HDIM]
                scores = dot(k, q, NT) * scale
                weights = jnp.where(seen, jnp.exp(scores - lines[h : h + 1]), 0.0)
                grads = weights * (dot(v, g, NT) - lines[heads + h : heads + h + 1])
                total[0, row, :, at : at + HDIM] += dot(grads.astype(jnp.bfloat16), q, NN) * scale
                total[1, row, :, at : at + HDIM] += dot(weights.astype(jnp.bfloat16), g, NN)
        return carry

    lax.fori_loop(0, slots.shape[0] // CAP, one_target, 0)
    out[...] = total[...].astype(out.dtype)


def local(queries, neighbour_states, retrieved, valid_blocks, output_weight, attention_cotangent):
    owners = lax.axis_size("seq")
    me = lax.axis_index("seq")
    tok_rows, width = queries.shape
    span_count = tok_rows // SPAN
    request_count = span_count * KNB
    store_rows = neighbour_states.shape[1]

    gathered = lax.all_gather(
        jnp.concatenate([queries, attention_cotangent], axis=1), "seq", axis=0, tiled=True
    )
    weight_columns = lax.all_to_all(output_weight, FEATS, split_axis=1, concat_axis=0, tiled=True)
    table = lax.all_gather(
        jnp.stack([retrieved.reshape(request_count), valid_blocks.reshape(request_count)]), "seq", axis=0
    )
    owner_of = table[:, 0] // store_rows
    same_owner = owner_of[:, :, None] == owner_of[:, None, :]
    order = jnp.arange(request_count, dtype=jnp.int32)
    earlier = order[None, :] < order[:, None]
    position = jnp.sum((same_owner & earlier[None]).astype(jnp.int32), axis=2)
    span_of = jnp.arange(owners, dtype=jnp.int32)[:, None] * span_count + order[None, :] // KNB
    code = span_of + 128 * (table[:, 0] % store_rows) + 1024 * (table[:, 1] > 0).astype(jnp.int32)
    hit = (owner_of == me)[:, None, :] & (
        position[:, None, :] == jnp.arange(CAP, dtype=jnp.int32)[None, :, None]
    )
    slots = jnp.sum(jnp.where(hit, code[:, None, :], 0), axis=2).reshape(owners * CAP)
    mine = owner_of + 16 * position + 32 * (table[:, 1] > 0).astype(jnp.int32)
    requests = lax.dynamic_index_in_dim(mine, me, 0, keepdims=False)

    window = pltpu.VMEM((owners * tok_rows + SPAN, 2 * width), jnp.bfloat16)
    outgoing = pl.pallas_call(
        pair_forward,
        out_shape=jax.ShapeDtypeStruct((owners, CAP * SPAN + 16, width), jnp.bfloat16),
        in_specs=[SMEM, ANY, VMEM],
        out_specs=VMEM,
        scratch_shapes=[window, pltpu.SemaphoreType.DMA],
        compiler_params=LIMIT,
    )(slots, gathered, neighbour_states)
    arrived = lax.all_to_all(outgoing, "seq", split_axis=0, concat_axis=0, tiled=True)
    span_rows, stats = pl.pallas_call(
        merge_pairs,
        out_shape=(
            jax.ShapeDtypeStruct((tok_rows, width), jnp.bfloat16),
            jax.ShapeDtypeStruct((span_count, 2 * width // HDIM, HDIM), jnp.float32),
        ),
        in_specs=[SMEM, VMEM],
        out_specs=(VMEM, VMEM),
        compiler_params=LIMIT,
    )(requests, arrived)

    onward = [(source, source + 1) for source in range(owners - 1)]
    before = lax.ppermute(span_rows[tok_rows - SPAN :], "seq", onward)
    attention = jnp.concatenate([before[1:], span_rows[: tok_rows - LEAD]])
    all_heads = lax.all_gather(attention, FEATS, axis=1, tiled=True)
    layer_output = jnp.dot(all_heads, weight_columns, preferred_element_type=jnp.float32).astype(jnp.bfloat16)

    all_stats = lax.all_gather(stats, "seq", axis=0, tiled=True)
    neighbour_gradient = pl.pallas_call(
        pair_backward,
        out_shape=jax.ShapeDtypeStruct(neighbour_states.shape, jnp.bfloat16),
        in_specs=[SMEM, ANY, VMEM, VMEM],
        out_specs=VMEM,
        scratch_shapes=[
            window,
            pltpu.VMEM(neighbour_states.shape, jnp.float32),
            pltpu.SemaphoreType.DMA,
        ],
        compiler_params=LIMIT,
    )(slots, gathered, neighbour_states, all_stats)
    return (layer_output, neighbour_gradient)


def solution(mesh):
    placed = (
        P("seq", FEATS),
        P(None, "seq", None, FEATS),
        P("seq", None),
        P("seq", None),
        P(FEATS, None),
        P("seq", FEATS),
    )
    return jax.shard_map(
        local,
        mesh=mesh,
        in_specs=placed,
        out_specs=(P("seq", FEATS), P(None, "seq", None, FEATS)),
        check_vma=False,
    )
```

time: 313 us -> 239 us (0.76)
  waiting for transfers between devices: 98.2 us -> 59.2 us
  Pallas kernels: 0 us -> 36.1 us
  blocking collectives: 119 us -> 97.6 us
  local copies, waits for them, and re-layouts: 35.4 us -> 16.2 us
  matrix products: 19.6 us -> 5.68 us
  other arithmetic: 12.2 us -> 3.22 us
  starting transfers between devices: 13 us -> 6.62 us
    ppermute x3 -> x1, waiting for transfers between devices: 95.3 us -> 1.15 us  [local(): before = lax.ppermute(span_rows[tok_rows - SPAN:], 'seq', onward)]
    all_to_all x2 -> x1, blocking collectives: 119 us -> 60.2 us  [local(): lax.all_to_all(output_weight, FEATS, split_axis=1, concat_axis=0, tiled=T...]
    all_gather x0 -> x2, blocking collectives: none -> 37.4 us  [the longest x1 21.3 us: local(): lax.all_gather(jnp.stack([retrieved.reshape(request_count), valid_blocks....]
    pallas_call x0 -> x3, Pallas kernels: none -> 36.1 us  [the longest x1 17.7 us: local(): pl.pallas_call(pair_backward, out_shape=jax.ShapeDtypeStruct(neighbour_st...]
    all_gather x0 -> x2, waiting for transfers between devices: none -> 27.7 us  [the longest x1 27.7 us: local(): lax.all_gather(jnp.concatenate([queries, attention_cotangent], axis=1), '...]
    all_to_all x1, waiting for transfers between devices: 2.93 us -> 30.3 us  [local(): lax.all_to_all(outgoing, 'seq', split_axis=0, concat_axis=0, tiled=True)]
    another operation x8 -> x2, local copies, waits for them, and re-layouts: 14.4 us -> 0.16 us  [local(): jnp.stack([retrieved.reshape(request_count), valid_blocks.reshape(request...]
    dot_general x7 -> x1, matrix products: 19.6 us -> 5.68 us  [local(): jnp.dot(all_heads, weight_columns, preferred_element_type=jnp.float32)]
  transfers between devices with their start and end apart: 5 -> 4, of which waited for: 4 -> 3; matrix products, arithmetic and copies ran while one was open for 11% -> 7% of each run, Pallas kernels for 0% -> 7%
where the time goes in v1:
time: 239 us
  blocking collectives  97.6 us (41%)
  waiting for transfers between devices  59.2 us (25%)
  Pallas kernels  36.1 us (15%)
  local copies, waits for them, and re-layouts  16.2 us (7%)
  between operations  14.1 us (6%)
  starting transfers between devices  6.62 us (3%)
  matrix products  5.68 us (2%)
  other arithmetic  3.22 us (1%)
    all_to_all x1, blocking collectives, local(): lax.all_to_all(output_weight, FEATS, split_axis=1, concat_axis=0, tiled=T...  60.2 us
    all_to_all x1, waiting for transfers between devices, local(): lax.all_to_all(outgoing, 'seq', split_axis=0, concat_axis=0, tiled=True)  30.3 us
    all_gather x1, waiting for transfers between devices, local(): lax.all_gather(jnp.concatenate([queries, attention_cotangent], axis=1), '...  27.7 us
    all_gather x1, blocking collectives, local(): lax.all_gather(jnp.stack([retrieved.reshape(request_count), valid_blocks....  21.3 us
    pallas_call x1, Pallas kernels, local(): pl.pallas_call(pair_backward, out_shape=jax.ShapeDtypeStruct(neighbour_st...  17.7 us
    pallas_call x1, Pallas kernels, local(): pl.pallas_call(pair_forward, out_shape=jax.ShapeDtypeStruct((owners, CAP...  17.1 us
    all_gather x1, blocking collectives, local(): all_stats = lax.all_gather(stats, 'seq', axis=0, tiled=True)  16.1 us
    unnamed x9, local copies, waits for them, and re-layouts  9.26 us
  transfers between devices with their start and end apart: 4, of which 3 were waited for; matrix products, arithmetic and copies ran while one was open for 7% of the time, Pallas kernels for 7%

profile of v1, /device:TPU:1, one launch (start us, length us, event | category | flops | bytes accessed | tf_op | source)
XLA Modules:
  0.0 238.7 jit_solution(7882686074480840484)
XLA Ops:
  7.2 0.0 all-gather.5.cloned.1.call-start
  7.2 1.8 pad_maximum_fusion
  9.0 0.8 copy.38
  9.8 0.1 stack_reshape.6
  9.9 0.8 copy.39
  10.6 0.1 stack_reshape.7
  10.7 21.3 %all-gather.1 = s32[16,2,12]{2,1,0:T(2,128)S(1)} all-gather(s32[1,2,12]{2,1,0:T(2,128)S(1)} %add_bitcast_fusion), channel_id=2, replica_groups=mesh['grp'=4,'seq'=16,'tp'=4] {'seq'}, dimensions={0}, use_global_device_ids=true | all-gather | bytes 1632 | tf_op jit(solution)/shard_map/all_gather | solution.py:164
  32.1 0.1 copy.53
  32.1 0.1 copy.52
  32.2 0.1 fusion.4
  32.3 0.1 copy.43
  32.4 0.4 convert_reduce_fusion
  32.8 0.1 copy.47
  32.9 0.1 reshape.137.slots
  33.0 27.7 %all-gather.5.cloned.1.call-done.rows_hbm = bf16[6144,512]{1,0:T(8,128)(2,1)} async-done(((bf16[384,512]{1,0:T(8,128)(2,1)}), bf16[6144,512]{1,0:T(8,128)(2,1)}) %all-gather.5.cloned.1.call-update) | async-done | bytes 6291472 | tf_op jit(solution)/shard_map/all_gather | solution.py:160
  60.7 1.1 copy-done
  61.8 17.1 %shard_map.77 = bf16[16,144,256]{2,1,0:T(8,128)(2,1)} custom-call(s32[32]{0:T(128)S(1)} %reshape.137.slots, bf16[6144,512]{1,0:T(8,128)(2,1)} %all-gather.5.cloned.1.call-done.rows_hbm, bf16[2,6,128,256]{3,2,1,0:T(8,128)(2,1)S(1)} %copy-done), custom_call_target="tpu_custom_call" | custom-call | tf_op jit(solution)/shard_map/pallas_call | solution.py:182
  78.9 4.6 %all-to-all-start = ((bf16[16,144,256]{2,1,0:T(8,128)(2,1)}), bf16[16,144,256]{2,1,0:T(8,128)(2,1)S(1)}, u32[]{:S(2)}, u32[]{:S(2)}) async-start(bf16[16,144,256]{2,1,0:T(8,128)(2,1)} %shard_map.77), calls=%async_computation | async-start | bytes 2359296 | tf_op jit(solution)/shard_map/all_to_all | solution.py:190
  83.6 0.0 all-gather.7.cloned.1.call-start
  83.6 0.2 fusion.5.requests
  83.8 30.3 %all-to-all-done.arrived = bf16[16,144,256]{2,1,0:T(8,128)(2,1)S(1)} async-done(((bf16[16,144,256]{2,1,0:T(8,128)(2,1)}), bf16[16,144,256]{2,1,0:T(8,128)(2,1)S(1)}, u32[]{:S(2)}, u32[]{:S(2)}) %all-to-all-start) | async-done | bytes 1179680 | tf_op jit(solution)/shard_map/all_to_all | solution.py:190
  114.1 1.2 shard_map.78
  115.4 1.9 collective-permute-start
  117.3 1.2 collective-permute-done
  118.5 0.7 pad_maximum_fusion.1
  119.2 6.4 %copy.48 = bf16[256,8192]{0,1:T(8,128)(2,1)} copy(bf16[256,8192]{1,0:T(8,128)(2,1)} %param.10) | data formatting | bytes 8388608 | tf_op args[4]
  125.7 60.2 %all_to_all.24 = bf16[256,16,512]{0,2,1:T(8,128)(2,1)} all-to-all(bf16[256,16,512]{0,2,1:T(8,128)(2,1)} %bitcast.20), channel_id=1, replica_groups=mesh['grp'=4,'seq'=16,'tp'=4] {'grp','tp'}, dimensions={1} | all-to-all | bytes 8388608 | tf_op jit(solution)/shard_map/all_to_all | solution.py:163
  185.9 6.5 %copy.49 = bf16[16,256,512]{2,1,0:T(8,128)(2,1)} copy(bf16[16,256,512]{1,2,0:T(8,128)(2,1)} %bitcast.19) | data formatting | bytes 8388608 | tf_op jit(solution)/shard_map/all_to_all | solution.py:163
  192.4 16.1 %all_gather.19.stats = f32[96,4,128]{2,1,0:T(4,128)S(1)} all-gather(f32[6,4,128]{2,1,0:T(4,128)S(1)} %get-tuple-element.5), channel_id=1, replica_groups=mesh['grp'=4,'seq'=16,'tp'=4] {'seq'}, dimensions={0}, use_global_device_ids=true | all-gather | bytes 208896 | tf_op jit(solution)/shard_map/all_gather | solution.py:208
  208.5 17.7 %shard_map.79 = bf16[2,6,128,256]{3,2,1,0:T(8,128)(2,1)} custom-call(s32[32]{0:T(128)S(1)} %reshape.137.slots, bf16[6144,512]{1,0:T(8,128)(2,1)} %all-gather.5.cloned.1.call-done.rows_hbm, bf16[2,6,128,256]{3,2,1,0:T(8,128)(2,1)S(1)} %copy-done.1, f32[96,4,128]{2,1,0:T(4,128)S(1)} %all_gather.19.stats), custom_call_target="tpu_custom_call" | custom-call | tf_op jit(solution)/shard_map/pallas_call | solution.py:209
  226.2 0.0 all-gather.7.cloned.1.call-done
  226.2 5.7 %convolution_convert_fusion = bf16[384,512]{1,0:T(8,128)(2,1)} fusion(bf16[384,4096]{1,0:T(8,128)(2,1)} %all-gather.7.cloned.1.call-done, bf16[4096,512]{1,0:T(8,128)(2,1)} %bitcast.21), kind=kOutput, calls=%fused_computation | convolution fusion | flops 1610809344 | bytes 7733248 | tf_op jit(solution)/shard_map/dot_general | solution.py:206
  (17 shorter events, 0.2 us)
Async XLA Ops:
  7.2 53.5 %all-gather.5.cloned.1.call-start = ((), (), s32[]{:S(2)}) async-start(), calls=%async_computation.2 | async-start | bytes 6684672 | tf_op jit(solution)/shard_map/all_gather | solution.py:160
  60.7 1.1 copy-start
  78.9 35.2 %all-to-all-start = ((bf16[16,144,256]{2,1,0:T(8,128)(2,1)}), bf16[16,144,256]{2,1,0:T(8,128)(2,1)S(1)}, u32[]{:S(2)}, u32[]{:S(2)}) async-start(bf16[16,144,256]{2,1,0:T(8,128)(2,1)} %shard_map.77), calls=%async_computation | async-start | bytes 2359296 | tf_op jit(solution)/shard_map/all_to_all | solution.py:190
  83.6 142.7 %all-gather.7.cloned.1.call-start = ((), (), s32[]{:S(2)}) async-start(), calls=%async_computation.3 | async-start | bytes 3342336 | tf_op jit(solution)/shard_map/all_gather | solution.py:205
  115.4 3.1 %collective-permute-start = (bf16[64,256]{1,0:T(8,128)(2,1)S(1)}, bf16[64,256]{1,0:T(8,128)(2,1)S(1)}, u32[]{:S(2)}, u32[]{:S(2)}) collective-permute-start(bf16[64,256]{1,0:T(8,128)(2,1)S(1)} %slice.19), channel_id=1, source_target_pairs={{0,4},{4,8},{8,12},{12,16},{16,20},{20,24},{24,28},{28,32},{32,36}... | collective-permute-start | bytes 98312 | tf_op jit(solution)/shard_map/ppermute | solution.py:203
  185.9 22.6 %copy-start.1 = (bf16[2,6,128,256]{3,2,1,0:T(8,128)(2,1)S(1)}, bf16[2,6,128,256]{3,2,1,0:T(8,128)(2,1)}, u32[]{:S(2)}) copy-start(bf16[2,6,128,256]{3,2,1,0:T(8,128)(2,1)} %states.3) | copy-start | bytes 2359300
Sparse Core Ops, SparseCore 0:
  10.4 50.2 all-gather.4
  119.4 84.6 all-gather.6

commit v2 on v1

v2 whole, which is shorter than its diff:
```python
import jax
import jax.numpy as jnp
from jax import lax
from jax.experimental import pallas as pl
from jax.experimental.pallas import tpu as pltpu
from jax.sharding import PartitionSpec as P

HDIM = 128
SPAN = 64
NTOK = 128
KNB = 2
CAP = 2
FEATS = ("grp", "tp")
NT = (((1,), (1,)), ((), ()))
NN = (((1,), (0,)), ((), ()))
TN = (((0,), (0,)), ((), ()))
VMEM = pl.BlockSpec(memory_space=pltpu.VMEM)
SMEM = pl.BlockSpec(memory_space=pltpu.SMEM)
ANY = pl.BlockSpec(memory_space=pl.ANY)
LIMIT = pltpu.CompilerParams(vmem_limit_bytes=48 * 1024 * 1024)


def cost(gigaflops):
    return pl.CostEstimate(flops=int(gigaflops * 1e9), bytes_accessed=8 * 1024 * 1024, transcendentals=0)


def dot(a, b, dims):
    return lax.dot_general(a, b, dims, preferred_element_type=jnp.float32)


def three_parts(x):
    high = x.astype(jnp.bfloat16).astype(jnp.float32)
    middle = (x - high).astype(jnp.bfloat16).astype(jnp.float32)
    return [high, middle, x - high - middle]


def decode_slot(code):
    return code % 128, (code // 128) % 8, code // 1024


def span_tokens(rows, span):
    block = jnp.minimum(span + 1, rows.shape[0] // SPAN - 1)
    main = rows[pl.ds(pl.multiple_of(block * SPAN, SPAN), SPAN), :]
    before = rows[pl.ds(pl.multiple_of(span * SPAN + SPAN - 16, 16), 16), :]
    place = lax.broadcasted_iota(jnp.int32, before.shape, 0)
    return jnp.concatenate([main[: SPAN - 16], jnp.where(place == 15, before, main[SPAN - 16 :])], 0)


def diagonal(first, second):
    zero = jnp.zeros_like(first)
    return jnp.concatenate(
        [jnp.concatenate([first, zero], 1), jnp.concatenate([zero, second], 1)], 0
    )


def pair_forward(slots, rows, states, out):
    width = states.shape[3]
    scale = HDIM ** (-0.5)

    def one_target(target, carry):
        span_0, row_0, _ = decode_slot(slots[target * CAP])
        span_1, row_1, _ = decode_slot(slots[target * CAP + 1])
        tokens_0, tokens_1 = span_tokens(rows, span_0), span_tokens(rows, span_1)
        lse_heads, delta_heads, attended_0, attended_1 = [], [], [], []
        for at in range(0, width, HDIM):
            q = diagonal(tokens_0[:, at : at + HDIM], tokens_1[:, at : at + HDIM])
            g = diagonal(
                tokens_0[:, width + at : width + at + HDIM], tokens_1[:, width + at : width + at + HDIM]
            )
            k = jnp.concatenate([states[0, row_0, :, at : at + HDIM], states[0, row_1, :, at : at + HDIM]], 1)
            v = jnp.concatenate([states[1, row_0, :, at : at + HDIM], states[1, row_1, :, at : at + HDIM]], 1)
            scores = dot(k, q, NT) * scale
            grads = dot(v, g, NT)
            top = jnp.max(scores, axis=0, keepdims=True)
            weights = jnp.exp(scores - top)
            total = jnp.sum(weights, axis=0, keepdims=True)
            weights = weights * (1.0 / total)
            lse_heads.append(top + jnp.log(total))
            delta_heads.append(jnp.sum(weights * grads, axis=0, keepdims=True))
            mixed = dot(weights.astype(jnp.bfloat16), v, TN)
            attended_0.append(mixed[:SPAN, :HDIM])
            attended_1.append(mixed[SPAN:, HDIM:])
        out[target, pl.ds(0, SPAN), :] = jnp.concatenate(attended_0, 1).astype(out.dtype)
        out[target, pl.ds(SPAN, SPAN), :] = jnp.concatenate(attended_1, 1).astype(out.dtype)
        lines = three_parts(jnp.concatenate(lse_heads, 1)) + three_parts(jnp.concatenate(delta_heads, 1))
        lines.append(jnp.zeros((16 - len(lines), width), jnp.float32))
        out[target, pl.ds(CAP * SPAN, 16), :] = jnp.concatenate(lines, 0).astype(out.dtype)
        return carry

    lax.fori_loop(0, out.shape[0], one_target, 0)


def merge_pairs(requests, arrived, *rest):
    attention, last, stats = rest[-3:]
    width = arrived.shape[2]
    heads = range(0, width, HDIM)
    count = len(heads)
    early = lax.broadcasted_iota(jnp.int32, (8, HDIM), 1) < SPAN
    final_row = lax.broadcasted_iota(jnp.int32, (SPAN, width), 0) == SPAN - 1
    previous = jnp.zeros((SPAN, width), jnp.float32)
    for span in range(stats.shape[0]):
        lse, delta, live, parts = [], [], [], []
        for k in range(KNB):
            code = requests[span * KNB + k]
            owner, place, valid = code % 16, (code // 16) % 2, code // 32 > 0
            both = arrived[owner, pl.ds(CAP * SPAN, 16), :].astype(jnp.float32)[:8]
            sides = []
            for at in heads:
                side = both[:, at : at + HDIM]
                sides.append(jnp.where(early == (place == 0), side, pltpu.roll(side, SPAN, 1)))
            mine = jnp.concatenate(sides, 1)
            lse.append(jnp.where(valid, mine[0:1] + (mine[1:2] + mine[2:3]), -1e30))
            delta.append(jnp.where(valid, mine[3:4] + (mine[4:5] + mine[5:6]), 0.0))
            live.append(valid)
            rows = arrived[owner, pl.ds(pl.multiple_of(place * SPAN, SPAN), SPAN), :]
            parts.append(jnp.where(valid, rows.astype(jnp.float32), 0.0))
        top = jnp.maximum(lse[0], lse[1])
        share = [jnp.where(live[k], jnp.exp(lse[k] - top), 0.0) for k in range(KNB)]
        total = jnp.maximum(share[0] + share[1], 1.0)
        share = [each / total for each in share]
        lse_all = top + jnp.log(total)
        delta_all = share[0] * delta[0] + share[1] * delta[1]
        stats[span] = jnp.concatenate(
            [lse_all[:, at : at + HDIM] for at in heads] + [delta_all[:, at : at + HDIM] for at in heads], 0
        )
        lines = [each[:, at : at + HDIM] for each in share for at in heads]
        columns = jnp.concatenate(lines + [jnp.zeros((HDIM - len(lines), HDIM), jnp.float32)], 0).T[:SPAN]
        mixed = jnp.concatenate(
            [
                parts[0][:, at : at + HDIM] * columns[:, h : h + 1]
                + parts[1][:, at : at + HDIM] * columns[:, count + h : count + h + 1]
                for h, at in enumerate(heads)
            ],
            1,
        )
        block = jnp.where(final_row, mixed, previous)
        attention[pl.ds(span * SPAN, SPAN), :] = block.astype(attention.dtype)
        previous = mixed
    last[...] = previous.astype(last.dtype)


def pair_backward(slots, rows, states, stats, out, total):
    total[...] = jnp.zeros_like(total)
    width = states.shape[3]
    heads = width // HDIM
    scale = HDIM ** (-0.5)
    lane = lax.broadcasted_iota(jnp.int32, (1, 2 * SPAN), 1)
    early = lane < SPAN
    first_token = lane % SPAN == SPAN - 1
    last_span = rows.shape[0] // SPAN - 1

    def one_target(target, carry):
        span_0, row_0, live_0 = decode_slot(slots[target * CAP])
        span_1, row_1, live_1 = decode_slot(slots[target * CAP + 1])
        tokens_0, tokens_1 = span_tokens(rows, span_0), span_tokens(rows, span_1)
        span = jnp.where(early, span_0, span_1)
        seen = (jnp.where(early, live_0, live_1) > 0) & (first_token | (span < last_span))
        lines = jnp.where(early, stats[span_0], stats[span_1])
        for h in range(heads):
            at = h * HDIM
            q = diagonal(tokens_0[:, at : at + HDIM], tokens_1[:, at : at + HDIM])
            g = diagonal(
                tokens_0[:, width + at : width + at + HDIM], tokens_1[:, width + at : width + at + HDIM]
            )
            k = jnp.concatenate([states[0, row_0, :, at : at + HDIM], states[0, row_1, :, at : at + HDIM]], 1)
            v = jnp.concatenate([states[1, row_0, :, at : at + HDIM], states[1, row_1, :, at : at + HDIM]], 1)
            scores = dot(k, q, NT) * scale
            weights = jnp.where(seen, jnp.exp(scores - lines[h : h + 1]), 0.0)
            grads = weights * (dot(v, g, NT) - lines[heads + h : heads + h + 1])
            key_part = dot(grads.astype(jnp.bfloat16), q, NN) * scale
            value_part = dot(weights.astype(jnp.bfloat16), g, NN)
            total[0, row_0, :, at : at + HDIM] += key_part[:, :HDIM]
            total[0, row_1, :, at : at + HDIM] += key_part[:, HDIM:]
            total[1, row_0, :, at : at + HDIM] += value_part[:, :HDIM]
            total[1, row_1, :, at : at + HDIM] += value_part[:, HDIM:]
        return carry

    lax.fori_loop(0, slots.shape[0] // CAP, one_target, 0)
    out[...] = total[...].astype(out.dtype)


def cut_weight(weight, *rest):
    pieces, sems = rest[:-1], rest[-1]
    grps, tps = lax.axis_size("grp"), lax.axis_size("tp")
    columns = pieces[0].shape[1]
    copies = []
    for i, piece in enumerate(pieces):
        g = lax.rem(lax.axis_index("grp") + i // tps, grps)
        t = lax.rem(lax.axis_index("tp") + i % tps, tps)
        start = pl.multiple_of((g * tps + t) * columns, 128)
        copies.append(pltpu.make_async_copy(weight.at[:, pl.ds(start, columns)], piece, sems.at[i]))
        copies[-1].start()
    for copy in copies:
        copy.wait()


def shifted(value, axis, steps):
    count = lax.axis_size(axis)
    return lax.ppermute(value, axis, [(source, (source + steps) % count) for source in range(count)])


def shifted_both(value, steps_grp, steps_tp):
    grps, tps = lax.axis_size("grp"), lax.axis_size("tp")
    pairs = [
        (g * tps + t, ((g + steps_grp) % grps) * tps + (t + steps_tp) % tps)
        for g in range(grps)
        for t in range(tps)
    ]
    return lax.ppermute(value, FEATS, pairs)


def halves_round(first, second, axis):
    half = first.shape[1] // 2
    count = lax.axis_size(axis)
    return [shifted(first[:, :half], axis, 1), shifted(second[:, half:], axis, count - 1)]


def project_near(*refs):
    blocks, weights, out = refs[:6], refs[6:-1], refs[-1]
    side = int(len(weights) ** 0.5)
    rows, width = blocks[0].shape[0], weights[0].shape[0]
    for half in range(2):
        total = None
        for block, step in zip(blocks[half * 3 : half * 3 + 3], (0, 1, side - 1)):
            for inner in range(side):
                weight = weights[inner * side + step] if half == 0 else weights[step * side + inner]
                term = dot(block[:, inner * width : (inner + 1) * width], weight[...], NN)
                total = term if total is None else total + term
        out[pl.ds(half * rows, rows), :] = total


def project_far(*refs):
    blocks, weights, partial, out = refs[:4], refs[4:-2], refs[-2], refs[-1]
    side = int(len(weights) ** 0.5)
    rows, width = blocks[0].shape[0], weights[0].shape[0]
    for half in range(2):
        total = partial[pl.ds(half * rows, rows), :]
        for inner in range(side):
            block = blocks[half * 2 + inner // (side // 2)]
            at = inner % (side // 2) * width
            weight = weights[inner * side + side // 2] if half == 0 else weights[side // 2 * side + inner]
            total = total + dot(block[:, at : at + width], weight[...], NN)
        out[pl.ds(half * rows, rows), :] = total.astype(out.dtype)


def local(queries, neighbour_states, retrieved, valid_blocks, output_weight, attention_cotangent):
    owners = lax.axis_size("seq")
    grps, tps = lax.axis_size("grp"), lax.axis_size("tp")
    me = lax.axis_index("seq")
    tok_rows, width = queries.shape
    span_count = tok_rows // SPAN
    request_count = span_count * KNB
    store_rows = neighbour_states.shape[1]
    out_columns = output_weight.shape[1] // (grps * tps)

    gathered = lax.all_gather(
        jnp.concatenate([queries, attention_cotangent], axis=1), "seq", axis=0, tiled=True
    )

    steps = [(dg, dt) for dg in range(grps) for dt in range(tps)]
    cut = pl.pallas_call(
        cut_weight,
        out_shape=[jax.ShapeDtypeStruct((width, out_columns), jnp.bfloat16)] * len(steps),
        in_specs=[ANY],
        out_specs=[ANY] * len(steps),
        scratch_shapes=[pltpu.SemaphoreType.DMA((len(steps),))],
    )(output_weight)
    weights = [shifted_both(piece, dg, dt) if dg or dt else piece for (dg, dt), piece in zip(steps, cut)]

    table = lax.all_gather(
        jnp.stack([retrieved.reshape(request_count), valid_blocks.reshape(request_count)]), "seq", axis=0
    )
    owner_of = table[:, 0] // store_rows
    same_owner = owner_of[:, :, None] == owner_of[:, None, :]
    order = jnp.arange(request_count, dtype=jnp.int32)
    earlier = order[None, :] < order[:, None]
    position = jnp.sum((same_owner & earlier[None]).astype(jnp.int32), axis=2)
    span_of = jnp.arange(owners, dtype=jnp.int32)[:, None] * span_count + order[None, :] // KNB
    code = span_of + 128 * (table[:, 0] % store_rows) + 1024 * (table[:, 1] > 0).astype(jnp.int32)
    hit = (owner_of == me)[:, None, :] & (
        position[:, None, :] == jnp.arange(CAP, dtype=jnp.int32)[None, :, None]
    )
    slots = jnp.sum(jnp.where(hit, code[:, None, :], 0), axis=2).reshape(owners * CAP)
    mine = owner_of + 16 * position + 32 * (table[:, 1] > 0).astype(jnp.int32)
    requests = lax.dynamic_index_in_dim(mine, me, 0, keepdims=False)

    outgoing = pl.pallas_call(
        pair_forward,
        cost_estimate=cost(9),
        out_shape=jax.ShapeDtypeStruct((owners, CAP * SPAN + 16, width), jnp.bfloat16),
        in_specs=[SMEM, VMEM, VMEM],
        out_specs=VMEM,
        compiler_params=LIMIT,
    )(slots, gathered, neighbour_states)
    arrived = lax.all_to_all(outgoing, "seq", split_axis=0, concat_axis=0, tiled=True)
    attention, last, stats = pl.pallas_call(
        merge_pairs,
        cost_estimate=cost(1),
        out_shape=(
            jax.ShapeDtypeStruct((tok_rows, width), jnp.bfloat16),
            jax.ShapeDtypeStruct((SPAN, width), jnp.bfloat16),
            jax.ShapeDtypeStruct((span_count, 2 * width // HDIM, HDIM), jnp.float32),
        ),
        in_specs=[SMEM, VMEM] + [ANY] * len(weights),
        out_specs=(VMEM, VMEM, VMEM),
        compiler_params=LIMIT,
    )(requests, arrived, *weights)

    middle = tok_rows // 2
    lower = attention[middle:]
    lower = jnp.concatenate([lower] + [shifted(lower, "tp", i) for i in range(1, tps)], 1)
    before = lax.ppermute(last, "seq", [(source, source + 1) for source in range(owners - 1)])
    final_row = lax.broadcasted_iota(jnp.int32, before.shape, 0) == SPAN - 1
    upper = jnp.concatenate([jnp.where(final_row, attention[:SPAN], before), attention[SPAN:middle]])
    upper = jnp.concatenate([upper] + [shifted(upper, "grp", i) for i in range(1, grps)], 1)
    upper = [upper, shifted(upper, "tp", 1), shifted(upper, "tp", tps - 1)]
    lower = [lower, shifted(lower, "grp", 1), shifted(lower, "grp", grps - 1)]
    far = halves_round(upper[1], upper[2], "tp") + halves_round(lower[1], lower[2], "grp")
    total = pl.pallas_call(
        project_near,
        cost_estimate=cost(3),
        out_shape=jax.ShapeDtypeStruct((tok_rows, out_columns), jnp.float32),
        in_specs=[VMEM] * (6 + len(weights)),
        out_specs=VMEM,
        compiler_params=LIMIT,
    )(*upper, *lower, *weights)
    layer_output = pl.pallas_call(
        project_far,
        cost_estimate=cost(2),
        out_shape=jax.ShapeDtypeStruct((tok_rows, out_columns), jnp.bfloat16),
        in_specs=[VMEM] * (5 + len(weights)),
        out_specs=VMEM,
        compiler_params=LIMIT,
    )(*far, *weights, total)

    all_stats = lax.all_gather(stats, "seq", axis=0, tiled=True)
    neighbour_gradient = pl.pallas_call(
        pair_backward,
        cost_estimate=cost(10),
        out_shape=jax.ShapeDtypeStruct(neighbour_states.shape, jnp.bfloat16),
        in_specs=[SMEM, VMEM, VMEM, VMEM],
        out_specs=VMEM,
        scratch_shapes=[pltpu.VMEM(neighbour_states.shape, jnp.float32)],
        compiler_params=LIMIT,
    )(slots, gathered, neighbour_states, all_stats)
    return (layer_output, neighbour_gradient)


def solution(mesh):
    placed = (
        P("seq", FEATS),
        P(None, "seq", None, FEATS),
        P("seq", None),
        P("seq", None),
        P(FEATS, None),
        P("seq", FEATS),
    )
    return jax.shard_map(
        local,
        mesh=mesh,
        in_specs=placed,
        out_specs=(P("seq", FEATS), P(None, "seq", None, FEATS)),
        check_vma=False,
    )
```

time: 239 us -> 364 us (1.52)
  Pallas kernels: 36.1 us -> 160 us
  blocking collectives: 97.6 us -> 37.4 us
  starting transfers between devices: 6.62 us -> 46.7 us
  waiting for transfers between devices: 59.2 us -> 85 us
  matrix products: 5.68 us -> 0 us
    pallas_call x3 -> x6, Pallas kernels: 36.1 us -> 160 us  [the longest x1 128 us: local(): pl.pallas_call(cut_weight, out_shape=[jax.ShapeDtypeStruct((width, out_co...]
    all_to_all x1 -> x0, blocking collectives: 60.2 us -> none  [local(): lax.all_to_all(output_weight, FEATS, split_axis=1, concat_axis=0, tiled=T...]
    ppermute x1 -> x30, waiting for transfers between devices: 1.15 us -> 57.9 us  [the longest x15 52.2 us: shifted_both(): return lax.ppermute(value, FEATS, pairs)]
    ppermute x1 -> x30, starting transfers between devices: 1.92 us -> 42 us  [the longest x15 20.6 us: shifted_both(): return lax.ppermute(value, FEATS, pairs)]
    all_to_all x1, waiting for transfers between devices: 30.3 us -> 0.01 us  [local(): lax.all_to_all(outgoing, 'seq', split_axis=0, concat_axis=0, tiled=True)]
    all_to_all x1 -> x0, local copies, waits for them, and re-layouts: 6.48 us -> none  [local(): lax.all_to_all(output_weight, FEATS, split_axis=1, concat_axis=0, tiled=T...]
    dot_general x1 -> x0, matrix products: 5.68 us -> none  [local(): jnp.dot(all_heads, weight_columns, preferred_element_type=jnp.float32)]
    unnamed x9 -> x48, local copies, waits for them, and re-layouts: 9.26 us -> 13.9 us
  transfers between devices with their start and end apart: 4 -> 32, of which waited for: 3 -> 13; matrix products, arithmetic and copies ran while one was open for 7% -> 1% of each run, Pallas kernels for 7% -> 40%
where the time goes in v2:
time: 364 us; the launch traced here: 361 us
  Pallas kernels  160 us (44%)
  waiting for transfers between devices  85 us (23%)
  starting transfers between devices  46.7 us (13%)
  blocking collectives  37.4 us (10%)
  local copies, waits for them, and re-layouts  14.3 us (4%)
  between operations  14.3 us (4%)
    pallas_call x1, Pallas kernels, local(): pl.pallas_call(cut_weight, out_shape=[jax.ShapeDtypeStruct((width, out_co...  128 us
    ppermute x15, waiting for transfers between devices, shifted_both(): return lax.ppermute(value, FEATS, pairs)  52.2 us
    all_gather x1, waiting for transfers between devices, local(): lax.all_gather(jnp.concatenate([queries, attention_cotangent], axis=1), '...  27.1 us
    all_gather x1, blocking collectives, local(): lax.all_gather(jnp.stack([retrieved.reshape(request_count), valid_blocks....  21.3 us
    ppermute x15, starting transfers between devices, shifted_both(): return lax.ppermute(value, FEATS, pairs)  20.6 us
    all_gather x1, blocking collectives, local(): all_stats = lax.all_gather(stats, 'seq', axis=0, tiled=True)  16.1 us
    ppermute x14, starting transfers between devices, shifted(): lax.ppermute(value, axis, [(source, (source + steps) % count) for source...  15.9 us
    unnamed x48, local copies, waits for them, and re-layouts  13.9 us
  transfers between devices with their start and end apart: 32, of which 13 were waited for; matrix products, arithmetic and copies ran while one was open for 1% of the time, Pallas kernels for 40%

profile of v2, /device:TPU:1, one launch (start us, length us, event | category | flops | bytes accessed | tf_op | source)
XLA Modules:
  0.0 361.1 jit_solution(1285177423388932387)
XLA Ops:
  10.7 21.3 %all-gather.1 = s32[16,2,12]{2,1,0:T(2,128)S(1)} all-gather(s32[1,2,12]{2,1,0:T(2,128)S(1)} %add_bitcast_fusion), channel_id=2, replica_groups=mesh['grp'=4,'seq'=16,'tp'=4] {'seq'}, dimensions={0}, use_global_device_ids=true | all-gather | bytes 1632 | tf_op jit(solution)/shard_map/all_gather | solution.py:270
  33.6 27.1 %all-gather.4.cloned.1.call-done.rows = bf16[6144,512]{1,0:T(8,128)(2,1)} async-done(((bf16[384,512]{1,0:T(8,128)(2,1)}), bf16[6144,512]{1,0:T(8,128)(2,1)}) %all-gather.4.cloned.1.call-update) | async-done | bytes 6291472 | tf_op jit(solution)/shard_map/all_gather | solution.py:256
  61.8 11.9 %shard_map.77 = bf16[16,144,256]{2,1,0:T(8,128)(2,1)} custom-call(s32[32]{0:T(128)S(1)} %reshape.134.slots, bf16[6144,512]{1,0:T(8,128)(2,1)} %all-gather.4.cloned.1.call-done.rows, bf16[2,6,128,256]{3,2,1,0:T(8,128)(2,1)S(1)} %copy-done.17), custom_call_target="tpu_custom_call" | custom-call | flops 8999999488 | bytes 8388608 | tf_op jit(solution)/shard_map/pallas_call | solution.py:287
  73.8 4.6 %all-to-all-start = ((bf16[16,144,256]{2,1,0:T(8,128)(2,1)}), bf16[16,144,256]{2,1,0:T(8,128)(2,1)S(1)}, u32[]{:S(2)}, u32[]{:S(2)}) async-start(bf16[16,144,256]{2,1,0:T(8,128)(2,1)} %shard_map.77), calls=%async_computation | async-start | bytes 2359296 | tf_op jit(solution)/shard_map/all_to_all | solution.py:295
  78.4 128.3 %shard_map.78 = (bf16[256,512]{1,0:T(8,128)(2,1)}, bf16[256,512]{1,0:T(8,128)(2,1)}, bf16[256,512]{1,0:T(8,128)(2,1)}, bf16[256,512]{1,0:T(8,128)(2,1)}, bf16[25...) custom-call(bf16[256,8192]{1,0:T(8,128)(2,1)} %weight.1), custom_call_target="tpu_custom_call" | custom-call | tf_op jit(solution)/shard_map/pallas_call | solution.py:261
  208.0 2.4 collective-permute-start.1
  214.0 2.0 collective-permute-done.rest_1_.refs_7_.refs_5_
  215.9 2.5 collective-permute-start.5
  218.5 15.3 %collective-permute-done.1.rest_2_.refs_8_.refs_6_ = bf16[256,512]{1,0:T(8,128)(2,1)S(1)} collective-permute-done((bf16[256,512]{1,0:T(8,128)(2,1)}, bf16[256,512]{1,0:T(8,128)(2,1)S(1)}, u32[]{:S(2)}, u32[]{:S(2)}) %collective-permute-start.1) | collective-permute-done | bytes 262176 | tf_op jit(solution)/shard_map/ppermute | solution.py:209
  233.8 2.7 collective-permute-start.7
  236.5 2.4 collective-permute-start.8
  238.8 2.6 collective-permute-start.9
  241.5 2.0 collective-permute-start.10
  244.6 3.3 collective-permute-done.7.rest_8_.refs_14_.refs_12_
  248.0 6.5 %collective-permute-done.8.rest_9_.refs_15_.refs_13_ = bf16[256,512]{1,0:T(8,128)(2,1)S(1)} collective-permute-done((bf16[256,512]{1,0:T(8,128)(2,1)}, bf16[256,512]{1,0:T(8,128)(2,1)S(1)}, u32[]{:S(2)}, u32[]{:S(2)}) %collective-permute-start.8) | collective-permute-done | bytes 262176 | tf_op jit(solution)/shard_map/ppermute | solution.py:209
  254.4 5.8 %collective-permute-done.9.rest_10_.refs_16_.refs_14_ = bf16[256,512]{1,0:T(8,128)(2,1)} collective-permute-done((bf16[256,512]{1,0:T(8,128)(2,1)}, bf16[256,512]{1,0:T(8,128)(2,1)}, u32[]{:S(2)}, u32[]{:S(2)}) %collective-permute-start.9) | collective-permute-done | bytes 262176 | tf_op jit(solution)/shard_map/ppermute | solution.py:209
  261.1 5.2 %collective-permute-done.10.rest_11_.refs_17_.refs_15_ = bf16[256,512]{1,0:T(8,128)(2,1)S(1)} collective-permute-done((bf16[256,512]{1,0:T(8,128)(2,1)}, bf16[256,512]{1,0:T(8,128)(2,1)S(1)}, u32[]{:S(2)}, u32[]{:S(2)}) %collective-permute-start.10) | collective-permute-done | bytes 262176 | tf_op jit(solution)/shard_map/ppermute | solution.py:209
  267.7 3.2 collective-permute-done.12.rest_13_.refs_19_.refs_17_
  271.6 5.0 %collective-permute-done.13.rest_14_.refs_20_.refs_18_ = bf16[256,512]{1,0:T(8,128)(2,1)S(1)} collective-permute-done((bf16[256,512]{1,0:T(8,128)(2,1)}, bf16[256,512]{1,0:T(8,128)(2,1)S(1)}, u32[]{:S(2)}, u32[]{:S(2)}) %collective-permute-start.13) | collective-permute-done | bytes 262176 | tf_op jit(solution)/shard_map/ppermute | solution.py:209
  277.4 5.9 %collective-permute-done.14.rest_15_.refs_21_.refs_19_ = bf16[256,512]{1,0:T(8,128)(2,1)S(1)} collective-permute-done((bf16[256,512]{1,0:T(8,128)(2,1)}, bf16[256,512]{1,0:T(8,128)(2,1)S(1)}, u32[]{:S(2)}, u32[]{:S(2)}) %collective-permute-start.14) | collective-permute-done | bytes 262176 | tf_op jit(solution)/shard_map/ppermute | solution.py:209
  291.2 2.0 collective-permute-start.25
  293.9 5.5 %collective-permute-start.15 = (bf16[64,256]{1,0:T(8,128)(2,1)S(1)}, bf16[64,256]{1,0:T(8,128)(2,1)S(1)}, u32[]{:S(2)}, u32[]{:S(2)}) collective-permute-start(bf16[64,256]{1,0:T(8,128)(2,1)S(1)} %get-tuple-element.38), channel_id=1, source_target_pairs={{0,4},{4,8},{8,12},{12,16},{16,20},{20,24},{24,28},{28,32},{32,36}... | collective-permute-start | bytes 98312 | tf_op jit(solution)/shard_map/ppermute | solution.py:312
  299.4 16.1 %all_gather.15.stats = f32[96,4,128]{2,1,0:T(4,128)S(1)} all-gather(f32[6,4,128]{2,1,0:T(4,128)S(1)} %get-tuple-element.39), channel_id=1, replica_groups=mesh['grp'=4,'seq'=16,'tp'=4] {'seq'}, dimensions={0}, use_global_device_ids=true | all-gather | bytes 208896 | tf_op jit(solution)/shard_map/all_gather | solution.py:336
  315.6 2.4 collective-permute-start.18
  319.6 2.7 collective-permute-start.28
  323.4 2.4 collective-permute-done.16
  325.9 2.1 collective-permute-start.21
  328.4 12.5 %shard_map.82 = bf16[2,6,128,256]{3,2,1,0:T(8,128)(2,1)} custom-call(s32[32]{0:T(128)S(1)} %reshape.134.slots, bf16[6144,512]{1,0:T(8,128)(2,1)} %all-gather.4.cloned.1.call-done.rows, bf16[2,6,128,256]{3,2,1,0:T(8,128)(2,1)S(1)} %copy-done.18, f32[96,4,128]{2,1,0:T(4,128)S(1)} %all_gather.15.stats), custom_call_target="tpu_custom_call" | custom-call | flops 10000000000 | bytes 8388608 | tf_op jit(solution)/shard_map/pallas_call | solution.py:337
  342.6 2.4 collective-permute-start.22
  345.2 3.4 shard_map.80.refs_20_
  348.6 2.2 collective-permute-done.20.refs_0_
  351.9 2.3 shard_map.81
  (118 shorter events, 30.7 us)
Async XLA Ops:
  7.2 53.5 %all-gather.4.cloned.1.call-start = ((), (), s32[]{:S(2)}) async-start(), calls=%async_computation.1 | async-start | bytes 6684672 | tf_op jit(solution)/shard_map/all_gather | solution.py:256
  73.8 210.2 %all-to-all-start = ((bf16[16,144,256]{2,1,0:T(8,128)(2,1)}), bf16[16,144,256]{2,1,0:T(8,128)(2,1)S(1)}, u32[]{:S(2)}, u32[]{:S(2)}) async-start(bf16[16,144,256]{2,1,0:T(8,128)(2,1)} %shard_map.77), calls=%async_computation | async-start | bytes 2359296 | tf_op jit(solution)/shard_map/all_to_all | solution.py:295
  206.7 9.3 %collective-permute-start = (bf16[256,512]{1,0:T(8,128)(2,1)}, bf16[256,512]{1,0:T(8,128)(2,1)S(1)}, u32[]{:S(2)}, u32[]{:S(2)}) collective-permute-start(bf16[256,512]{1,0:T(8,128)(2,1)} %get-tuple-element.22), channel_id=1, source_target_pairs={{0,1},{1,2},{2,3},{3,0},{64,65},{65,66},{66,67},{67,64},{128,129},... | collective-permute-start | bytes 786440 | tf_op jit(solution)/shard_map/ppermute | solution.py:209
  208.0 25.8 %collective-permute-start.1 = (bf16[256,512]{1,0:T(8,128)(2,1)}, bf16[256,512]{1,0:T(8,128)(2,1)S(1)}, u32[]{:S(2)}, u32[]{:S(2)}) collective-permute-start(bf16[256,512]{1,0:T(8,128)(2,1)} %get-tuple-element.23), channel_id=1, source_target_pairs={{0,2},{1,3},{2,0},{3,1},{64,66},{65,67},{66,64},{67,65},{128,130},... | collective-permute-start | bytes 786440 | tf_op jit(solution)/shard_map/ppermute | solution.py:209
  210.4 23.4 %collective-permute-start.2 = (bf16[256,512]{1,0:T(8,128)(2,1)}, bf16[256,512]{1,0:T(8,128)(2,1)S(1)}, u32[]{:S(2)}, u32[]{:S(2)}) collective-permute-start(bf16[256,512]{1,0:T(8,128)(2,1)} %get-tuple-element.24), channel_id=1, source_target_pairs={{0,3},{1,0},{2,1},{3,2},{64,67},{65,64},{66,65},{67,66},{128,131},... | collective-permute-start | bytes 786440 | tf_op jit(solution)/shard_map/ppermute | solution.py:209
  211.6 24.9 %collective-permute-start.3 = (bf16[256,512]{1,0:T(8,128)(2,1)}, bf16[256,512]{1,0:T(8,128)(2,1)S(1)}, u32[]{:S(2)}, u32[]{:S(2)}) collective-permute-start(bf16[256,512]{1,0:T(8,128)(2,1)} %get-tuple-element.25), channel_id=1, source_target_pairs={{0,64},{1,65},{2,66},{3,67},{64,128},{65,129},{66,130},{67,131},{1... | collective-permute-start | bytes 786440 | tf_op jit(solution)/shard_map/ppermute | solution.py:209
  212.8 26.1 %collective-permute-start.4 = (bf16[256,512]{1,0:T(8,128)(2,1)}, bf16[256,512]{1,0:T(8,128)(2,1)S(1)}, u32[]{:S(2)}, u32[]{:S(2)}) collective-permute-start(bf16[256,512]{1,0:T(8,128)(2,1)} %get-tuple-element.26), channel_id=1, source_target_pairs={{0,65},{1,66},{2,67},{3,64},{64,129},{65,130},{66,131},{67,128},{1... | collective-permute-start | bytes 786440 | tf_op jit(solution)/shard_map/ppermute | solution.py:209
  215.9 25.5 %collective-permute-start.5 = (bf16[256,512]{1,0:T(8,128)(2,1)}, bf16[256,512]{1,0:T(8,128)(2,1)S(1)}, u32[]{:S(2)}, u32[]{:S(2)}) collective-permute-start(bf16[256,512]{1,0:T(8,128)(2,1)} %get-tuple-element.27), channel_id=1, source_target_pairs={{0,66},{1,67},{2,64},{3,65},{64,130},{65,131},{66,128},{67,129},{1... | collective-permute-start | bytes 786440 | tf_op jit(solution)/shard_map/ppermute | solution.py:209
  233.8 9.7 %collective-permute-start.6 = (bf16[256,512]{1,0:T(8,128)(2,1)}, bf16[256,512]{1,0:T(8,128)(2,1)S(1)}, u32[]{:S(2)}, u32[]{:S(2)}) collective-permute-start(bf16[256,512]{1,0:T(8,128)(2,1)} %get-tuple-element.28), channel_id=1, source_target_pairs={{0,67},{1,64},{2,65},{3,66},{64,131},{65,128},{66,129},{67,130},{1... | collective-permute-start | bytes 786440 | tf_op jit(solution)/shard_map/ppermute | solution.py:209
  233.8 14.2 %collective-permute-start.7 = (bf16[256,512]{1,0:T(8,128)(2,1)}, bf16[256,512]{1,0:T(8,128)(2,1)S(1)}, u32[]{:S(2)}, u32[]{:S(2)}) collective-permute-start(bf16[256,512]{1,0:T(8,128)(2,1)} %get-tuple-element.29), channel_id=1, source_target_pairs={{0,128},{1,129},{2,130},{3,131},{64,192},{65,193},{66,194},{67,195... | collective-permute-start | bytes 786440 | tf_op jit(solution)/shard_map/ppermute | solution.py:209
  236.5 17.9 %collective-permute-start.8 = (bf16[256,512]{1,0:T(8,128)(2,1)}, bf16[256,512]{1,0:T(8,128)(2,1)S(1)}, u32[]{:S(2)}, u32[]{:S(2)}) collective-permute-start(bf16[256,512]{1,0:T(8,128)(2,1)} %get-tuple-element.30), channel_id=1, source_target_pairs={{0,129},{1,130},{2,131},{3,128},{64,193},{65,194},{66,195},{67,192... | collective-permute-start | bytes 786440 | tf_op jit(solution)/shard_map/ppermute | solution.py:209
  238.8 21.3 %collective-permute-start.9 = (bf16[256,512]{1,0:T(8,128)(2,1)}, bf16[256,512]{1,0:T(8,128)(2,1)}, u32[]{:S(2)}, u32[]{:S(2)}) collective-permute-start(bf16[256,512]{1,0:T(8,128)(2,1)} %get-tuple-element.31), channel_id=1, source_target_pairs={{0,130},{1,131},{2,128},{3,129},{64,194},{65,195},{66,192},{67,193... | collective-permute-start | bytes 786440 | tf_op jit(solution)/shard_map/ppermute | solution.py:209
  241.5 24.8 %collective-permute-start.10 = (bf16[256,512]{1,0:T(8,128)(2,1)}, bf16[256,512]{1,0:T(8,128)(2,1)S(1)}, u32[]{:S(2)}, u32[]{:S(2)}) collective-permute-start(bf16[256,512]{1,0:T(8,128)(2,1)} %get-tuple-element.32), channel_id=1, source_target_pairs={{0,131},{1,128},{2,129},{3,130},{64,195},{65,192},{66,193},{67,194... | collective-permute-start | bytes 786440 | tf_op jit(solution)/shard_map/ppermute | solution.py:209
  243.4 23.6 %collective-permute-start.11 = (bf16[256,512]{1,0:T(8,128)(2,1)}, bf16[256,512]{1,0:T(8,128)(2,1)S(1)}, u32[]{:S(2)}, u32[]{:S(2)}) collective-permute-start(bf16[256,512]{1,0:T(8,128)(2,1)} %get-tuple-element.33), channel_id=1, source_target_pairs={{0,192},{1,193},{2,194},{3,195},{64,0},{65,1},{66,2},{67,3},{128,6... | collective-permute-start | bytes 786440 | tf_op jit(solution)/shard_map/ppermute | solution.py:209
  248.0 23.0 %collective-permute-start.12 = (bf16[256,512]{1,0:T(8,128)(2,1)}, bf16[256,512]{1,0:T(8,128)(2,1)S(1)}, u32[]{:S(2)}, u32[]{:S(2)}) collective-permute-start(bf16[256,512]{1,0:T(8,128)(2,1)} %get-tuple-element.34), channel_id=1, source_target_pairs={{0,193},{1,194},{2,195},{3,192},{64,1},{65,2},{66,3},{67,0},{128,6... | collective-permute-start | bytes 786440 | tf_op jit(solution)/shard_map/ppermute | solution.py:209
  254.4 22.3 %collective-permute-start.13 = (bf16[256,512]{1,0:T(8,128)(2,1)}, bf16[256,512]{1,0:T(8,128)(2,1)S(1)}, u32[]{:S(2)}, u32[]{:S(2)}) collective-permute-start(bf16[256,512]{1,0:T(8,128)(2,1)} %get-tuple-element.35), channel_id=1, source_target_pairs={{0,194},{1,195},{2,192},{3,193},{64,2},{65,3},{66,0},{67,1},{128,6... | collective-permute-start | bytes 786440 | tf_op jit(solution)/shard_map/ppermute | solution.py:209
  260.2 23.1 %collective-permute-start.14 = (bf16[256,512]{1,0:T(8,128)(2,1)}, bf16[256,512]{1,0:T(8,128)(2,1)S(1)}, u32[]{:S(2)}, u32[]{:S(2)}) collective-permute-start(bf16[256,512]{1,0:T(8,128)(2,1)} %get-tuple-element.36), channel_id=1, source_target_pairs={{0,195},{1,192},{2,193},{3,194},{64,3},{65,0},{66,1},{67,2},{128,6... | collective-permute-start | bytes 786440 | tf_op jit(solution)/shard_map/ppermute | solution.py:209
  291.2 28.4 %collective-permute-start.25 = (bf16[192,256]{1,0:T(8,128)(2,1)S(1)}, bf16[192,256]{1,0:T(8,128)(2,1)S(1)}, u32[]{:S(2)}, u32[]{:S(2)}) collective-permute-start(bf16[192,256]{1,0:T(8,128)(2,1)S(1)} %slice.35), channel_id=1, source_target_pairs={{0,3},{1,0},{2,1},{3,2},{4,7},{5,4},{6,5},{7,6},{8,11},{9,8},{10,9... | collective-permute-start | bytes 294920 | tf_op jit(solution)/shard_map/ppermute | solution.py:199
  293.2 26.3 %collective-permute-start.24 = (bf16[192,256]{1,0:T(8,128)(2,1)S(1)}, bf16[192,256]{1,0:T(8,128)(2,1)S(1)}, u32[]{:S(2)}, u32[]{:S(2)}) collective-permute-start(bf16[192,256]{1,0:T(8,128)(2,1)S(1)} %slice.35), channel_id=1, source_target_pairs={{0,2},{1,3},{2,0},{3,1},{4,6},{5,7},{6,4},{7,5},{8,10},{9,11},{10,... | collective-permute-start | bytes 294920 | tf_op jit(solution)/shard_map/ppermute | solution.py:199
  293.4 26.2 %collective-permute-start.23 = (bf16[192,256]{1,0:T(8,128)(2,1)S(1)}, bf16[192,256]{1,0:T(8,128)(2,1)S(1)}, u32[]{:S(2)}, u32[]{:S(2)}) collective-permute-start(bf16[192,256]{1,0:T(8,128)(2,1)S(1)} %slice.35), channel_id=1, source_target_pairs={{0,1},{1,2},{2,3},{3,0},{4,5},{5,6},{6,7},{7,4},{8,9},{9,10},{10,1... | collective-permute-start | bytes 294920 | tf_op jit(solution)/shard_map/ppermute | solution.py:199
  293.9 21.6 %collective-permute-start.15 = (bf16[64,256]{1,0:T(8,128)(2,1)S(1)}, bf16[64,256]{1,0:T(8,128)(2,1)S(1)}, u32[]{:S(2)}, u32[]{:S(2)}) collective-permute-start(bf16[64,256]{1,0:T(8,128)(2,1)S(1)} %get-tuple-element.38), channel_id=1, source_target_pairs={{0,4},{4,8},{8,12},{12,16},{16,20},{20,24},{24,28},{28,32},{32,36}... | collective-permute-start | bytes 98312 | tf_op jit(solution)/shard_map/ppermute | solution.py:312
  315.6 6.8 %collective-permute-start.18 = (bf16[192,256]{1,0:T(8,128)(2,1)S(1)}, bf16[192,256]{1,0:T(8,128)(2,1)S(1)}, u32[]{:S(2)}, u32[]{:S(2)}) collective-permute-start(bf16[192,256]{1,0:T(8,128)(2,1)S(1)} %pad_maximum_fusion.3), channel_id=1, source_target_pairs={{0,192},{64,0},{128,64},{192,128},{1,193},{65,1},{129,65},{193,129... | collective-permute-start | bytes 294920 | tf_op jit(solution)/shard_map/ppermute | solution.py:199
  318.0 5.4 %collective-permute-start.17 = (bf16[192,256]{1,0:T(8,128)(2,1)S(1)}, bf16[192,256]{1,0:T(8,128)(2,1)S(1)}, u32[]{:S(2)}, u32[]{:S(2)}) collective-permute-start(bf16[192,256]{1,0:T(8,128)(2,1)S(1)} %pad_maximum_fusion.3), channel_id=1, source_target_pairs={{0,128},{64,192},{128,0},{192,64},{1,129},{65,193},{129,1},{193,65... | collective-permute-start | bytes 294920 | tf_op jit(solution)/shard_map/ppermute | solution.py:199
  319.6 6.3 %collective-permute-start.16 = (bf16[192,256]{1,0:T(8,128)(2,1)S(1)}, bf16[192,256]{1,0:T(8,128)(2,1)S(1)}, u32[]{:S(2)}, u32[]{:S(2)}) collective-permute-start(bf16[192,256]{1,0:T(8,128)(2,1)S(1)} %pad_maximum_fusion.3), channel_id=1, source_target_pairs={{0,64},{64,128},{128,192},{192,0},{1,65},{65,129},{129,193},{193,1... | collective-permute-start | bytes 294920 | tf_op jit(solution)/shard_map/ppermute | solution.py:199
  319.6 21.2 %collective-permute-start.28 = (bf16[192,1024]{1,0:T(8,128)(2,1)S(1)}, bf16[192,1024]{1,0:T(8,128)(2,1)S(1)}, u32[]{:S(2)}, u32[]{:S(2)}) collective-permute-start(bf16[192,1024]{1,0:T(8,128)(2,1)S(1)} %pad_maximum_fusion.2.refs_3_), channel_id=1, source_target_pairs={{0,192},{64,0},{128,64},{192,128},{1,193},{65,1},{129,65},{193,129... | collective-permute-start | bytes 1179656 | tf_op jit(solution)/shard_map/ppermute | solution.py:199
  322.4 18.6 %collective-permute-start.26 = (bf16[192,1024]{1,0:T(8,128)(2,1)S(1)}, bf16[192,1024]{1,0:T(8,128)(2,1)S(1)}, u32[]{:S(2)}, u32[]{:S(2)}) collective-permute-start(bf16[192,1024]{1,0:T(8,128)(2,1)S(1)} %pad_maximum_fusion.2.refs_3_), channel_id=1, source_target_pairs={{0,64},{64,128},{128,192},{192,0},{1,65},{65,129},{129,193},{193,1... | collective-permute-start | bytes 1179656 | tf_op jit(solution)/shard_map/ppermute | solution.py:199
  325.9 16.6 %collective-permute-start.21 = (bf16[192,1024]{1,0:T(8,128)(2,1)S(1)}, bf16[192,1024]{1,0:T(8,128)(2,1)S(1)}, u32[]{:S(2)}, u32[]{:S(2)}) collective-permute-start(bf16[192,1024]{1,0:T(8,128)(2,1)S(1)} %pad_maximum_fusion.1.refs_0_), channel_id=1, source_target_pairs={{0,3},{1,0},{2,1},{3,2},{4,7},{5,4},{6,5},{7,6},{8,11},{9,8},{10,9... | collective-permute-start | bytes 1179656 | tf_op jit(solution)/shard_map/ppermute | solution.py:199
  328.0 17.0 %collective-permute-start.19 = (bf16[192,1024]{1,0:T(8,128)(2,1)S(1)}, bf16[192,1024]{1,0:T(8,128)(2,1)S(1)}, u32[]{:S(2)}, u32[]{:S(2)}) collective-permute-start(bf16[192,1024]{1,0:T(8,128)(2,1)S(1)} %pad_maximum_fusion.1.refs_0_), channel_id=1, source_target_pairs={{0,1},{1,2},{2,3},{3,0},{4,5},{5,6},{6,7},{7,4},{8,9},{9,10},{10,1... | collective-permute-start | bytes 1179656 | tf_op jit(solution)/shard_map/ppermute | solution.py:199
  340.9 7.7 %collective-permute-start.29 = (bf16[192,512]{1,0:T(8,128)(2,1)S(1)}, bf16[192,512]{1,0:T(8,128)(2,1)S(1)}, u32[]{:S(2)}, u32[]{:S(2)}) collective-permute-start(bf16[192,512]{1,0:T(8,128)(2,1)S(1)} %slice.43), channel_id=1, source_target_pairs={{0,192},{64,0},{128,64},{192,128},{1,193},{65,1},{129,65},{193,129... | collective-permute-start | bytes 589832 | tf_op jit(solution)/shard_map/ppermute | solution.py:199
  341.0 7.5 %collective-permute-start.27 = (bf16[192,512]{1,0:T(8,128)(2,1)S(1)}, bf16[192,512]{1,0:T(8,128)(2,1)S(1)}, u32[]{:S(2)}, u32[]{:S(2)}) collective-permute-start(bf16[192,512]{1,0:T(8,128)(2,1)S(1)} %slice.42), channel_id=1, source_target_pairs={{0,64},{64,128},{128,192},{192,0},{1,65},{65,129},{129,193},{193,1... | collective-permute-start | bytes 589832 | tf_op jit(solution)/shard_map/ppermute | solution.py:199
  342.6 6.0 %collective-permute-start.22 = (bf16[192,512]{1,0:T(8,128)(2,1)S(1)}, bf16[192,512]{1,0:T(8,128)(2,1)S(1)}, u32[]{:S(2)}, u32[]{:S(2)}) collective-permute-start(bf16[192,512]{1,0:T(8,128)(2,1)S(1)} %slice.41), channel_id=1, source_target_pairs={{0,3},{1,0},{2,1},{3,2},{4,7},{5,4},{6,5},{7,6},{8,11},{9,8},{10,9... | collective-permute-start | bytes 589832 | tf_op jit(solution)/shard_map/ppermute | solution.py:199
  345.0 5.8 %collective-permute-start.20 = (bf16[192,512]{1,0:T(8,128)(2,1)S(1)}, bf16[192,512]{1,0:T(8,128)(2,1)S(1)}, u32[]{:S(2)}, u32[]{:S(2)}) collective-permute-start(bf16[192,512]{1,0:T(8,128)(2,1)S(1)} %slice.40), channel_id=1, source_target_pairs={{0,1},{1,2},{2,3},{3,0},{4,5},{5,6},{6,7},{7,4},{8,9},{9,10},{10,1... | collective-permute-start | bytes 589832 | tf_op jit(solution)/shard_map/ppermute | solution.py:199
  (22 other events, 170.3 us)
Sparse Core Ops, SparseCore 0:
  10.4 50.2 all-gather.3

commit v3 on v1

v3 whole, which is shorter than its diff:
```python
import functools

import jax
import jax.numpy as jnp
from jax import lax
from jax.experimental import pallas as pl
from jax.experimental.pallas import tpu as pltpu
from jax.sharding import PartitionSpec as P

HDIM = 128
SPAN = 64
NTOK = 128
KNB = 2
CAP = 2
FEATS = ("grp", "tp")
LOG2E = 1.4426950408889634
NT = (((1,), (1,)), ((), ()))
NN = (((1,), (0,)), ((), ()))
TN = (((0,), (0,)), ((), ()))
VMEM = pl.BlockSpec(memory_space=pltpu.VMEM)
SMEM = pl.BlockSpec(memory_space=pltpu.SMEM)
ANY = pl.BlockSpec(memory_space=pl.ANY)
LIMIT = pltpu.CompilerParams(vmem_limit_bytes=48 * 1024 * 1024)


def cost(gigaflops):
    return pl.CostEstimate(flops=int(gigaflops * 1e9), bytes_accessed=8 * 1024 * 1024, transcendentals=0)


def dot(a, b, dims):
    return lax.dot_general(a, b, dims, preferred_element_type=jnp.float32)


def tied(value, *others):
    return pl.pallas_call(
        lambda *refs: None,
        out_shape=jax.ShapeDtypeStruct(value.shape, value.dtype),
        in_specs=[ANY] * (1 + len(others)),
        out_specs=ANY,
        input_output_aliases={0: 0},
    )(value, *others)


def decode_slot(code):
    return code & 127, (code >> 7) & 7, code >> 10


def span_tokens(rows, span):
    block = jnp.minimum(span + 1, rows.shape[0] // SPAN - 1)
    main = rows[pl.ds(pl.multiple_of(block * SPAN, SPAN), SPAN), :]
    before = rows[pl.ds(pl.multiple_of(span * SPAN + SPAN - 16, 16), 16), :]
    place = lax.broadcasted_iota(jnp.int32, before.shape, 0)
    return jnp.concatenate([main[: SPAN - 16], jnp.where(place == 15, before, main[SPAN - 16 :])], 0)


def diagonal(first, second):
    zero = jnp.zeros_like(first)
    return jnp.concatenate(
        [jnp.concatenate([first, zero], 1), jnp.concatenate([zero, second], 1)], 0
    )


def span_forward(codes, queries, cotangents, store, attention, stats, held, sems):
    blocks, width = queries.shape[0] // SPAN, queries.shape[1]
    windows = blocks + 1
    heads = range(0, width, HDIM)
    scale = HDIM ** (-0.5)
    copies = []
    for i in range(KNB * windows):
        row = codes[i] & 127
        source = store.at[lax.div(row, store.shape[2]), :, lax.rem(row, store.shape[2])]
        copies.append(pltpu.make_async_copy(source, held.at[i], sems.at[i]))
        copies[-1].start()

    lane = lax.broadcasted_iota(jnp.int32, (1, 2 * SPAN), 1)
    early = lane < SPAN
    place = lax.broadcasted_iota(jnp.int32, (16, width), 0)

    def window(ref, i):
        if i == 0 or i == blocks:
            at = min(i, blocks - 1) * SPAN
            return ref[at : at + SPAN, :]
        at = i * SPAN
        tail = jnp.where(place == 15, ref[at - 16 : at, :], ref[at + SPAN - 16 : at + SPAN, :])
        return jnp.concatenate([ref[at : at + SPAN - 16, :], tail], 0)

    attended, lines = {}, {}
    for first in range(0, windows, 2):
        second = min(first + 1, windows - 1)
        for i in range(KNB * first, KNB * (second + 1)):
            copies[i].wait()
        tokens = [window(queries, i) for i in (first, second)]
        others = [window(cotangents, i) for i in (first, second)]
        live = [jnp.where(early, codes[KNB * first + k] >> 7, codes[KNB * second + k] >> 7) > 0 for k in range(KNB)]
        for h, at in enumerate(heads):
            q = diagonal(*[each[:, at : at + HDIM] for each in tokens])
            g = diagonal(*[each[:, at : at + HDIM] for each in others])
            k, v = [
                jnp.concatenate(
                    [
                        jnp.concatenate([held[KNB * i + n, kind, :, at : at + HDIM] for n in range(KNB)], 0)
                        for i in (first, second)
                    ],
                    1,
                )
                for kind in range(2)
            ]
            scores = dot(k, q, NT)
            scores = [jnp.where(live[n], scores[n * NTOK : (n + 1) * NTOK], -1e30) for n in range(KNB)]
            top = jnp.max(jnp.maximum(scores[0], scores[1]), axis=0, keepdims=True)
            weights = [
                jnp.where(live[n], jnp.exp2((scores[n] - top) * (scale * LOG2E)), 0.0) for n in range(KNB)
            ]
            total = jnp.maximum(jnp.sum(weights[0] + weights[1], axis=0, keepdims=True), 1.0)
            weights = jnp.concatenate(weights, 0) * (1.0 / total)
            delta = jnp.sum(weights * dot(v, g, NT), axis=0, keepdims=True)
            mixed = dot(weights.astype(jnp.bfloat16), v, TN)
            attended[first, h], attended[second, h] = mixed[:SPAN, :HDIM], mixed[SPAN:, HDIM:]
            lines[first, h] = jnp.concatenate([top * scale + jnp.log(total), delta], 0)

    final_row = lax.broadcasted_iota(jnp.int32, (SPAN, width), 0) == SPAN - 1
    rolled = {key: pltpu.roll(jnp.concatenate([value] * 4, 0), SPAN, 1)[:2] for key, value in lines.items()}
    for i in range(blocks):
        mixed = [jnp.concatenate([attended[j, h] for h in range(len(heads))], 1) for j in (i, i + 1)]
        attention[pl.ds(i * SPAN, SPAN), :] = jnp.where(final_row, mixed[1], mixed[0]).astype(attention.dtype)
        rows = []
        for h in range(len(heads)):
            both = []
            for j in (i, i + 1):
                pair = (lines[j - j % 2, h], rolled[j - j % 2, h])
                both.append(jnp.where(early, pair[j % 2], pair[1 - j % 2]))
            rows.append(jnp.where(lane % SPAN == SPAN - 1, both[1], both[0]))
        stats[i] = jnp.concatenate([row[kind : kind + 1] for kind in range(2) for row in rows], 0)


def pair_backward(together, slots, rows, states, stats, out, total):
    total[...] = jnp.zeros_like(total)
    width = states.shape[3]
    heads = width // HDIM
    scale = HDIM ** (-0.5)
    lane = lax.broadcasted_iota(jnp.int32, (1, 2 * SPAN), 1)
    early = lane < SPAN
    first_token = lane % SPAN == SPAN - 1
    last_span = stats.shape[0] - 1

    def one_target(target):
        span_0, row_0, live_0 = decode_slot(slots[target * CAP])
        span_1, row_1, live_1 = decode_slot(slots[target * CAP + 1])
        tokens_0, tokens_1 = span_tokens(rows, span_0), span_tokens(rows, span_1)
        span = jnp.where(early, span_0, span_1)
        seen = (jnp.where(early, live_0, live_1) > 0) & (first_token | (span < last_span))
        lines = jnp.where(
            first_token,
            jnp.where(early, stats[span_0], stats[span_1]),
            jnp.where(
                early, stats[jnp.minimum(span_0 + 1, last_span)], stats[jnp.minimum(span_1 + 1, last_span)]
            ),
        )
        parts = []
        for h in range(heads):
            at = h * HDIM
            q = diagonal(tokens_0[:, at : at + HDIM], tokens_1[:, at : at + HDIM])
            g = diagonal(
                tokens_0[:, width + at : width + at + HDIM], tokens_1[:, width + at : width + at + HDIM]
            )
            k = jnp.concatenate([states[0, row_0, :, at : at + HDIM], states[0, row_1, :, at : at + HDIM]], 1)
            v = jnp.concatenate([states[1, row_0, :, at : at + HDIM], states[1, row_1, :, at : at + HDIM]], 1)
            scores = dot(k, q, NT) * scale
            weights = jnp.where(seen, jnp.exp(scores - lines[h : h + 1]), 0.0)
            grads = weights * (dot(v, g, NT) - lines[heads + h : heads + h + 1])
            key_part = dot(grads.astype(jnp.bfloat16), q, NN) * scale
            value_part = dot(weights.astype(jnp.bfloat16), g, NN)
            parts.append((key_part, value_part))
        return row_0, row_1, parts

    def some_targets(step, carry):
        results = [one_target(step * together + i) for i in range(together)]
        for row_0, row_1, parts in results:
            for h, pair in enumerate(parts):
                for kind, part in enumerate(pair):
                    total[kind, row_0, :, h * HDIM : (h + 1) * HDIM] += part[:, :HDIM]
                    total[kind, row_1, :, h * HDIM : (h + 1) * HDIM] += part[:, HDIM:]
        return carry

    lax.fori_loop(0, slots.shape[0] // CAP // together, some_targets, 0)
    out[...] = total[...].astype(out.dtype)


def cut_weight(core, columns, block):
    block[0] = columns[...]


def project(core, blocks, mine, other, out):
    columns = mine.shape[2]
    for weight, at in ((mine, core[0]), (other, 1 - core[0])):
        total = None
        for source in range(blocks.shape[0]):
            term = dot(blocks[source], weight[source], NN)
            total = term if total is None else total + term
        out[:, pl.ds(pl.multiple_of(at * columns, 128), columns)] = total.astype(out.dtype)


def local(queries, neighbour_states, retrieved, valid_blocks, output_weight, attention_cotangent):
    owners = lax.axis_size("seq")
    grps, tps = lax.axis_size("grp"), lax.axis_size("tp")
    me = lax.axis_index("seq")
    tok_rows, width = queries.shape
    span_count = tok_rows // SPAN
    request_count = span_count * KNB
    store_rows = neighbour_states.shape[1]
    out_columns = output_weight.shape[1] // (grps * tps)

    core = (me & 1).reshape(1)
    half = out_columns // 2
    cut = pl.pallas_call(
        cut_weight,
        grid_spec=pltpu.PrefetchScalarGridSpec(
            num_scalar_prefetch=1,
            grid=(grps * tps,),
            in_specs=[pl.BlockSpec((width, half), lambda i, core: (0, 2 * i + core[0]))],
            out_specs=pl.BlockSpec((1, width, half), lambda i, core: (i, 0, 0)),
        ),
        out_shape=jax.ShapeDtypeStruct((grps * tps, width, half), jnp.bfloat16),
    )(core, output_weight)
    weight = lax.all_to_all(cut, FEATS, split_axis=0, concat_axis=0, tiled=True)

    table = lax.all_gather(
        jnp.stack([retrieved.reshape(request_count), valid_blocks.reshape(request_count)]), "seq", axis=0
    )
    owner_of = table[:, 0] // store_rows
    same_owner = owner_of[:, :, None] == owner_of[:, None, :]
    order = jnp.arange(request_count, dtype=jnp.int32)
    earlier = order[None, :] < order[:, None]
    position = jnp.sum((same_owner & earlier[None]).astype(jnp.int32), axis=2)
    span_of = jnp.arange(owners, dtype=jnp.int32)[:, None] * span_count + order[None, :] // KNB
    code = span_of + 128 * (table[:, 0] % store_rows) + 1024 * (table[:, 1] > 0).astype(jnp.int32)
    hit = (owner_of == me)[:, None, :] & (
        position[:, None, :] == jnp.arange(CAP, dtype=jnp.int32)[None, :, None]
    )
    slots = jnp.sum(jnp.where(hit, code[:, None, :], 0), axis=2).reshape(owners * CAP)
    plain = (table[:, 0] + 128 * (table[:, 1] > 0).astype(jnp.int32)).reshape(owners * request_count)
    plain = jnp.concatenate([jnp.zeros((KNB,), jnp.int32), plain])
    codes = lax.dynamic_slice_in_dim(plain, me * request_count, request_count + KNB, 0)

    store = lax.all_gather(neighbour_states, "seq", axis=0)
    store = tied(store, slots, codes, weight)
    both = tied(jnp.concatenate([queries, attention_cotangent], axis=1), store)
    gathered = lax.all_gather(both, "seq", axis=0, tiled=True)
    weight_other = lax.ppermute(weight, "seq", [(source, source ^ 1) for source in range(owners)])

    attention, stats = pl.pallas_call(
        span_forward,
        cost_estimate=cost(5),
        out_shape=(
            jax.ShapeDtypeStruct((tok_rows, width), jnp.bfloat16),
            jax.ShapeDtypeStruct((span_count, 2 * width // HDIM, 2 * SPAN), jnp.float32),
        ),
        in_specs=[SMEM, VMEM, VMEM, ANY],
        out_specs=(VMEM, VMEM),
        scratch_shapes=[
            pltpu.VMEM((request_count + KNB, 2, NTOK, width), jnp.bfloat16),
            pltpu.SemaphoreType.DMA((request_count + KNB,)),
        ],
        compiler_params=LIMIT,
    )(codes, queries, attention_cotangent, store)

    spread = jnp.broadcast_to(attention[None], (grps * tps, tok_rows, width))
    heads = lax.all_to_all(spread, FEATS, split_axis=0, concat_axis=0, tiled=True)
    all_stats = lax.all_gather(stats, "seq", axis=0, tiled=True)
    neighbour_gradient = pl.pallas_call(
        functools.partial(pair_backward, 2),
        cost_estimate=cost(10),
        out_shape=jax.ShapeDtypeStruct(neighbour_states.shape, jnp.bfloat16),
        in_specs=[SMEM, VMEM, VMEM, VMEM],
        out_specs=VMEM,
        scratch_shapes=[pltpu.VMEM(neighbour_states.shape, jnp.float32)],
        compiler_params=LIMIT,
    )(slots, gathered, neighbour_states, all_stats)
    layer_output = pl.pallas_call(
        project,
        cost_estimate=cost(5),
        out_shape=jax.ShapeDtypeStruct((tok_rows, out_columns), jnp.bfloat16),
        in_specs=[SMEM, VMEM, VMEM, VMEM],
        out_specs=VMEM,
        compiler_params=LIMIT,
    )(core, heads, weight, weight_other)
    return (layer_output, neighbour_gradient)


def solution(mesh):
    placed = (
        P("seq", FEATS),
        P(None, "seq", None, FEATS),
        P("seq", None),
        P("seq", None),
        P(FEATS, None),
        P("seq", FEATS),
    )
    return jax.shard_map(
        local,
        mesh=mesh,
        in_specs=placed,
        out_specs=(P("seq", FEATS), P(None, "seq", None, FEATS)),
        check_vma=False,
    )
```

time: 239 us -> 174 us (0.73)
  the two profiles are of different devices: /device:TPU:1 before, /device:TPU:28 now
where the time goes in v3:
time: 174 us; the launch traced here: 173 us
  waiting for transfers between devices  68.8 us (40%)
  blocking collectives  36.6 us (21%)
  Pallas kernels  30.1 us (17%)
  starting transfers between devices  14.8 us (9%)
  between operations  14.1 us (8%)
  local copies, waits for them, and re-layouts  7.71 us (4%)
    all_gather x1, waiting for transfers between devices, local(): store = lax.all_gather(neighbour_states, 'seq', axis=0)  37 us
    all_to_all x1, waiting for transfers between devices, local(): lax.all_to_all(spread, FEATS, split_axis=0, concat_axis=0, tiled=True)  28 us
    all_gather x1, blocking collectives, local(): lax.all_gather(jnp.stack([retrieved.reshape(request_count), valid_blocks....  20 us
    all_gather x1, blocking collectives, local(): all_stats = lax.all_gather(stats, 'seq', axis=0, tiled=True)  16.6 us
    pallas_call x1, Pallas kernels, local(): pl.pallas_call(functools.partial(pair_backward, 2), cost_estimate=cost(10...  12 us
    pallas_call x1, Pallas kernels, local(): pl.pallas_call(cut_weight, grid_spec=pltpu.PrefetchScalarGridSpec(num_sca...  9.5 us
    all_to_all x1, starting transfers between devices, local(): lax.all_to_all(spread, FEATS, split_axis=0, concat_axis=0, tiled=True)  7.34 us
    all_to_all x1, starting transfers between devices, local(): weight = lax.all_to_all(cut, FEATS, split_axis=0, concat_axis=0, tiled=True)  7.26 us
  transfers between devices with their start and end apart: 5, of which 3 were waited for; matrix products, arithmetic and copies ran while one was open for 3% of the time, Pallas kernels for 10%

profile of v3, /device:TPU:28, one launch (start us, length us, event | category | flops | bytes accessed | tf_op | source)
XLA Modules:
  0.0 173.4 jit_solution(13654253722860688448)
XLA Ops:
  7.2 0.7 all-gather.8.cloned.1.call-update
  7.9 9.5 %shard_map.77 = bf16[16,256,256]{2,1,0:T(8,128)(2,1)} custom-call(s32[1]{0:T(128)} %bitcast.core, bf16[256,8192]{1,0:T(8,128)(2,1)} %columns.1), custom_call_target="tpu_custom_call" | custom-call | tf_op jit(solution)/shard_map/pallas_call | solution.py:215
  17.4 7.3 %all-to-all-start = ((bf16[16,256,256]{2,1,0:T(8,128)(2,1)}), bf16[16,256,256]{2,1,0:T(8,128)(2,1)S(1)}, u32[]{:S(2)}, u32[]{:S(2)}) async-start(bf16[16,256,256]{2,1,0:T(8,128)(2,1)} %shard_map.77), calls=%async_computation | async-start | bytes 4194304 | tf_op jit(solution)/shard_map/all_to_all | solution.py:225
  24.7 0.1 copy.50
  24.8 0.1 stack_reshape.6
  24.9 0.1 copy.51
  25.0 0.1 stack_reshape.7
  25.1 20.0 %all-gather.2 = s32[16,2,12]{2,1,0:T(2,128)S(1)} all-gather(s32[1,2,12]{2,1,0:T(2,128)S(1)} %add_bitcast_fusion), channel_id=2, replica_groups=mesh['grp'=4,'seq'=16,'tp'=4] {'seq'}, dimensions={0}, use_global_device_ids=true | all-gather | bytes 1632 | tf_op jit(solution)/shard_map/all_gather | solution.py:227
  45.1 0.1 copy.55
  45.2 0.1 copy.62
  45.3 0.1 copy.59
  45.4 0.1 copy.63
  45.5 0.4 convert_reduce_fusion
  46.0 0.1 copy.60
  46.1 0.6 reshape.143.refs_1_.slots
  46.6 0.1 copy.54
  46.7 0.1 add.61
  46.8 0.6 pad_dynamic-slice_fusion.refs_2_.codes
  47.4 0.8 pad_maximum_fusion.refs_0_
  48.2 3.0 %all-to-all-done.refs_3_.mine = bf16[16,256,256]{2,1,0:T(8,128)(2,1)S(1)} async-done(((bf16[16,256,256]{2,1,0:T(8,128)(2,1)}), bf16[16,256,256]{2,1,0:T(8,128)(2,1)S(1)}, u32[]{:S(2)}, u32[]{:S(2)}) %all-to-all-start) | async-done | bytes 2097184 | tf_op jit(solution)/shard_map/all_to_all | solution.py:225
  51.2 37.0 %all-gather.8.cloned.1.call-done = bf16[32,6,128,256]{3,2,1,0:T(8,128)(2,1)} async-done(((bf16[2,6,128,256]{3,2,1,0:T(8,128)(2,1)}), bf16[32,6,128,256]{3,2,1,0:T(8,128)(2,1)}) %all-gather.8.cloned.1.call-update) | async-done | bytes 12582928 | tf_op jit(solution)/shard_map/all_gather | solution.py:245
  88.3 0.6 copy-done.6
  88.9 4.2 %shard_map.79 = (bf16[384,256]{1,0:T(8,128)(2,1)S(1)}, f32[6,4,128]{2,1,0:T(4,128)S(1)}) custom-call(s32[14]{0:T(128)S(1)} %copy-done.6, bf16[384,256]{1,0:T(8,128)(2,1)S(1)} %copy-done.3, bf16[384,256]{1,0:T(8,128)(2,1)S(1)} %copy-done.4, bf16[16,2,6,128,256]{4,3,2,1,0:T(8,128)(2,1)} %shard_map.78.store.refs_1_), custom_call_target="tpu_custom_call" | custom-call | flops 5000000000 | bytes 8388608 | tf_op jit(solution)/shard_map/pallas_call | solution.py:251
  93.1 2.0 %broadcast_in_dim.19 = bf16[16,384,256]{2,1,0:T(8,128)(2,1)} broadcast(bf16[384,256]{1,0:T(8,128)(2,1)S(1)} %get-tuple-element.4), dimensions={1,2} | broadcast | bytes 3342336 | tf_op jit(solution)/shard_map/broadcast_in_dim | solution.py:267
  95.1 7.3 %all-to-all-start.1 = ((bf16[16,384,256]{2,1,0:T(8,128)(2,1)}), bf16[16,384,256]{2,1,0:T(8,128)(2,1)}, u32[]{:S(2)}, u32[]{:S(2)}) async-start(bf16[16,384,256]{2,1,0:T(8,128)(2,1)} %broadcast_in_dim.19), calls=%async_computation.1 | async-start | bytes 6291456 | tf_op jit(solution)/shard_map/all_to_all | solution.py:268
  102.5 0.1 collective-permute-start
  102.6 16.6 %all_gather.23.stats = f32[96,4,128]{2,1,0:T(4,128)S(1)} all-gather(f32[6,4,128]{2,1,0:T(4,128)S(1)} %get-tuple-element.5), channel_id=1, replica_groups=mesh['grp'=4,'seq'=16,'tp'=4] {'seq'}, dimensions={0}, use_global_device_ids=true | all-gather | bytes 208896 | tf_op jit(solution)/shard_map/all_gather | solution.py:269
  119.2 1.4 copy-done.7
  120.6 28.0 %all-to-all-done.1.blocks = bf16[16,384,256]{2,1,0:T(8,128)(2,1)} async-done(((bf16[16,384,256]{2,1,0:T(8,128)(2,1)}), bf16[16,384,256]{2,1,0:T(8,128)(2,1)}, u32[]{:S(2)}, u32[]{:S(2)}) %all-to-all-start.1) | async-done | bytes 3145760 | tf_op jit(solution)/shard_map/all_to_all | solution.py:268
  148.6 1.6 copy-done.8
  150.1 4.4 %shard_map.80 = bf16[384,512]{1,0:T(8,128)(2,1)} custom-call(s32[1]{0:T(128)} %bitcast.core, bf16[16,384,256]{2,1,0:T(8,128)(2,1)} %all-to-all-done.1.blocks, bf16[16,256,256]{2,1,0:T(8,128)(2,1)S(1)} %copy-done.1, bf16[16,256,256]{2,1,0:T(8,128)(2,1)S(1)} %copy-done.8), custom_call_target="tpu_custom_call" | custom-call | flops 5000000000 | bytes 8388608 | tf_op jit(solution)/shard_map/pallas_call | solution.py:279
  154.6 12.0 %shard_map.82 = bf16[2,6,128,256]{3,2,1,0:T(8,128)(2,1)} custom-call(s32[32]{0:T(128)S(1)} %copy-done.5, bf16[6144,512]{1,0:T(8,128)(2,1)} %all-gather.6.cloned.1.call-done.rows, bf16[2,6,128,256]{3,2,1,0:T(8,128)(2,1)S(1)} %copy-done.2, f32[96,4,128]{2,1,0:T(4,128)S(1)} %all_gather.23.stats), custom_call_target="tpu_custom_call" | custom-call | flops 10000000000 | bytes 8388608 | tf_op jit(solution)/shard_map/pallas_call | solution.py:270
  (38 shorter events, 0.3 us)
Async XLA Ops:
  7.2 81.1 %all-gather.8.cloned.1.call-start = ((), (), s32[]{:S(2)}) async-start(), calls=%async_computation.3 | async-start | bytes 13369344 | tf_op jit(solution)/shard_map/all_gather | solution.py:245
  17.4 7.3 %copy-start.9 = (s32[6,2]{0,1:T(2,128)S(1)}, s32[6,2]{0,1:T(2,128)}, u32[]{:S(2)}) copy-start(s32[6,2]{0,1:T(2,128)} %param.8) | copy-start | bytes 148
  17.4 7.5 %copy-start.10 = (s32[6,2]{0,1:T(2,128)S(1)}, s32[6,2]{0,1:T(2,128)}, u32[]{:S(2)}) copy-start(s32[6,2]{0,1:T(2,128)} %param.9) | copy-start | bytes 148
  17.4 30.0 %copy-start.3 = (bf16[384,256]{1,0:T(8,128)(2,1)S(1)}, bf16[384,256]{1,0:T(8,128)(2,1)}, u32[]{:S(2)}) copy-start(bf16[384,256]{1,0:T(8,128)(2,1)} %queries.1) | copy-start | bytes 589828
  17.4 30.0 %copy-start.4 = (bf16[384,256]{1,0:T(8,128)(2,1)S(1)}, bf16[384,256]{1,0:T(8,128)(2,1)}, u32[]{:S(2)}) copy-start(bf16[384,256]{1,0:T(8,128)(2,1)} %cotangents.1) | copy-start | bytes 589828
  17.4 33.8 %all-to-all-start = ((bf16[16,256,256]{2,1,0:T(8,128)(2,1)}), bf16[16,256,256]{2,1,0:T(8,128)(2,1)S(1)}, u32[]{:S(2)}, u32[]{:S(2)}) async-start(bf16[16,256,256]{2,1,0:T(8,128)(2,1)} %shard_map.77), calls=%async_computation | async-start | bytes 4194304 | tf_op jit(solution)/shard_map/all_to_all | solution.py:225
  24.7 129.9 %all-gather.6.cloned.1.call-start = ((), (), s32[]{:S(2)}) async-start(), calls=%async_computation.2 | async-start | bytes 6684672 | tf_op jit(solution)/shard_map/all_gather | solution.py:248
  51.2 37.0 %copy-start = (bf16[16,256,256]{2,1,0:T(8,128)(2,1)}, bf16[16,256,256]{2,1,0:T(8,128)(2,1)S(1)}, u32[]{:S(2)}) copy-start(bf16[16,256,256]{2,1,0:T(8,128)(2,1)S(1)} %all-to-all-done.refs_3_.mine) | copy-start | bytes 6291460
  88.3 0.7 copy-start.6
  95.1 7.3 %copy-start.1 = (bf16[16,256,256]{2,1,0:T(8,128)(2,1)S(1)}, bf16[16,256,256]{2,1,0:T(8,128)(2,1)}, u32[]{:S(2)}) copy-start(bf16[16,256,256]{2,1,0:T(8,128)(2,1)} %copy-done) | copy-start | bytes 6291460
  95.1 53.4 %all-to-all-start.1 = ((bf16[16,384,256]{2,1,0:T(8,128)(2,1)}), bf16[16,384,256]{2,1,0:T(8,128)(2,1)}, u32[]{:S(2)}, u32[]{:S(2)}) async-start(bf16[16,384,256]{2,1,0:T(8,128)(2,1)} %broadcast_in_dim.19), calls=%async_computation.1 | async-start | bytes 6291456 | tf_op jit(solution)/shard_map/all_to_all | solution.py:268
  102.5 16.7 %collective-permute-start = (bf16[16,256,256]{2,1,0:T(8,128)(2,1)S(1)}, bf16[16,256,256]{2,1,0:T(8,128)(2,1)S(1)}, u32[]{:S(2)}, u32[]{:S(2)}) collective-permute-start(bf16[16,256,256]{2,1,0:T(8,128)(2,1)S(1)} %copy-done.1), channel_id=1, source_target_pairs={{0,4},{4,0},{8,12},{12,8},{16,20},{20,16},{24,28},{28,24},{32,36},... | collective-permute-start | bytes 6291464 | tf_op jit(solution)/shard_map/ppermute | solution.py:249
  119.2 35.4 %copy-start.2 = (bf16[2,6,128,256]{3,2,1,0:T(8,128)(2,1)S(1)}, bf16[2,6,128,256]{3,2,1,0:T(8,128)(2,1)}, u32[]{:S(2)}) copy-start(bf16[2,6,128,256]{3,2,1,0:T(8,128)(2,1)} %states.1) | copy-start | bytes 2359300
  119.2 35.4 %copy-start.5 = (s32[32]{0:T(128)S(1)}, s32[32]{0:T(128)}, u32[]{:S(2)}) copy-start(s32[32]{0:T(128)} %reshape.143.refs_1_.slots) | copy-start | bytes 388
  119.2 1.4 copy-start.7
  148.6 1.6 copy-start.8
Sparse Core Ops, SparseCore 0:
  9.8 78.3 all-gather.7
  90.7 45.6 all-gather.5

commit v4 on v3

--- a/solution.py
+++ b/solution.py
@@ -20,7 +20,9 @@
 VMEM = pl.BlockSpec(memory_space=pltpu.VMEM)
 SMEM = pl.BlockSpec(memory_space=pltpu.SMEM)
 ANY = pl.BlockSpec(memory_space=pl.ANY)
+HBM = pl.BlockSpec(memory_space=pltpu.HBM)
 LIMIT = pltpu.CompilerParams(vmem_limit_bytes=48 * 1024 * 1024)
+WIDE = pltpu.CompilerParams(vmem_limit_bytes=60 * 1024 * 1024)
 
 
 def cost(gigaflops):
@@ -45,12 +47,11 @@
     return code & 127, (code >> 7) & 7, code >> 10
 
 
-def span_tokens(rows, span):
-    block = jnp.minimum(span + 1, rows.shape[0] // SPAN - 1)
-    main = rows[pl.ds(pl.multiple_of(block * SPAN, SPAN), SPAN), :]
-    before = rows[pl.ds(pl.multiple_of(span * SPAN + SPAN - 16, 16), 16), :]
-    place = lax.broadcasted_iota(jnp.int32, before.shape, 0)
-    return jnp.concatenate([main[: SPAN - 16], jnp.where(place == 15, before, main[SPAN - 16 :])], 0)
+def span_tokens(window, span, spans):
+    place = lax.broadcasted_iota(jnp.int32, (16, window.shape[1]), 0)
+    first_token = (place == 15) & (span < spans - 1)
+    tail = jnp.where(first_token, window[:16, :], window[SPAN:, :])
+    return jnp.concatenate([window[16:SPAN, :], tail], 0)
 
 
 def diagonal(first, second):
@@ -60,7 +61,7 @@
     )
 
 
-def span_forward(codes, queries, cotangents, store, attention, stats, held, sems):
+def span_forward(codes, queries, cotangents, store, spread, stats, held, attention, sems, out_sems):
     blocks, width = queries.shape[0] // SPAN, queries.shape[1]
     windows = blocks + 1
     heads = range(0, width, HDIM)
@@ -131,9 +132,24 @@
                 both.append(jnp.where(early, pair[j % 2], pair[1 - j % 2]))
             rows.append(jnp.where(lane % SPAN == SPAN - 1, both[1], both[0]))
         stats[i] = jnp.concatenate([row[kind : kind + 1] for kind in range(2) for row in rows], 0)
-
-
-def pair_backward(together, slots, rows, states, stats, out, total):
+    copies = [pltpu.make_async_copy(attention, spread.at[i], out_sems.at[i]) for i in range(spread.shape[0])]
+    for copy in copies:
+        copy.start()
+    for copy in copies:
+        copy.wait()
+
+
+def pair_backward(together, slots, rows, states, stats, out, finished, total, windows, sems):
+    finished[...] = jnp.zeros_like(finished)
+    spans = stats.shape[0]
+    reach = SPAN + 16
+    copies = []
+    for i in range(slots.shape[0]):
+        span = decode_slot(slots[i])[0]
+        start = jnp.minimum(span * SPAN + SPAN - 16, rows.shape[0] - reach)
+        source = rows.at[pl.ds(pl.multiple_of(start, 16), reach)]
+        copies.append(pltpu.make_async_copy(source, windows.at[i], sems.at[i]))
+        copies[-1].start()
     total[...] = jnp.zeros_like(total)
     width = states.shape[3]
     heads = width // HDIM
@@ -146,7 +162,8 @@
     def one_target(target):
         span_0, row_0, live_0 = decode_slot(slots[target * CAP])
         span_1, row_1, live_1 = decode_slot(slots[target * CAP + 1])
-        tokens_0, tokens_1 = span_tokens(rows, span_0), span_tokens(rows, span_1)
+        tokens_0 = span_tokens(windows.at[target * CAP], span_0, spans)
+        tokens_1 = span_tokens(windows.at[target * CAP + 1], span_1, spans)
         span = jnp.where(early, span_0, span_1)
         seen = (jnp.where(early, live_0, live_1) > 0) & (first_token | (span < last_span))
         lines = jnp.where(
@@ -174,6 +191,9 @@
         return row_0, row_1, parts
 
     def some_targets(step, carry):
+        for i in range(together * CAP):
+            at = step * together * CAP + i
+            pltpu.make_async_copy(rows.at[pl.ds(0, reach)], windows.at[at], sems.at[at]).wait()
         results = [one_target(step * together + i) for i in range(together)]
         for row_0, row_1, parts in results:
             for h, pair in enumerate(parts):
@@ -187,17 +207,29 @@
 
 
 def cut_weight(core, columns, block):
-    block[0] = columns[...]
-
-
-def project(core, blocks, mine, other, out):
+    count, _, half = block.shape
+    for i in range(count):
+        at = pl.multiple_of((2 * i + core[0]) * half, 128)
+        block[i] = columns[:, pl.ds(at, half)]
+
+
+def project(core, blocks, mine, other, earlier, out, total):
     columns = mine.shape[2]
-    for weight, at in ((mine, core[0]), (other, 1 - core[0])):
-        total = None
-        for source in range(blocks.shape[0]):
-            term = dot(blocks[source], weight[source], NN)
-            total = term if total is None else total + term
-        out[:, pl.ds(pl.multiple_of(at * columns, 128), columns)] = total.astype(out.dtype)
+    step = pl.program_id(0)
+
+    @pl.when(step == 0)
+    def _():
+        total[...] = jnp.zeros_like(total)
+
+    for source in range(blocks.shape[0]):
+        total[:, :columns] += dot(blocks[source], mine[source], NN)
+        total[:, columns:] += dot(blocks[source], other[source], NN)
+
+    @pl.when(step == pl.num_programs(0) - 1)
+    def _():
+        for weight, at in ((0, core[0]), (1, 1 - core[0])):
+            part = total[:, weight * columns : (weight + 1) * columns]
+            out[:, pl.ds(pl.multiple_of(at * columns, 128), columns)] = part.astype(out.dtype)
 
 
 def local(queries, neighbour_states, retrieved, valid_blocks, output_weight, attention_cotangent):
@@ -212,13 +244,14 @@
 
     core = (me & 1).reshape(1)
     half = out_columns // 2
+    sources = 4 if grps * tps % 4 == 0 else 1
     cut = pl.pallas_call(
         cut_weight,
         grid_spec=pltpu.PrefetchScalarGridSpec(
             num_scalar_prefetch=1,
-            grid=(grps * tps,),
-            in_specs=[pl.BlockSpec((width, half), lambda i, core: (0, 2 * i + core[0]))],
-            out_specs=pl.BlockSpec((1, width, half), lambda i, core: (i, 0, 0)),
+            grid=(grps * tps // sources,),
+            in_specs=[pl.BlockSpec((width, sources * out_columns), lambda i, core: (0, i))],
+            out_specs=pl.BlockSpec((sources, width, half), lambda i, core: (i, 0, 0)),
         ),
         out_shape=jax.ShapeDtypeStruct((grps * tps, width, half), jnp.bfloat16),
     )(core, output_weight)
@@ -244,46 +277,64 @@
 
     store = lax.all_gather(neighbour_states, "seq", axis=0)
     store = tied(store, slots, codes, weight)
-    both = tied(jnp.concatenate([queries, attention_cotangent], axis=1), store)
+    both = tied(jnp.concatenate([queries, attention_cotangent], axis=1), weight)
     gathered = lax.all_gather(both, "seq", axis=0, tiled=True)
     weight_other = lax.ppermute(weight, "seq", [(source, source ^ 1) for source in range(owners)])
 
-    attention, stats = pl.pallas_call(
+    spread, stats = pl.pallas_call(
         span_forward,
         cost_estimate=cost(5),
         out_shape=(
-            jax.ShapeDtypeStruct((tok_rows, width), jnp.bfloat16),
+            jax.ShapeDtypeStruct((grps * tps, tok_rows, width), jnp.bfloat16),
             jax.ShapeDtypeStruct((span_count, 2 * width // HDIM, 2 * SPAN), jnp.float32),
         ),
         in_specs=[SMEM, VMEM, VMEM, ANY],
+        out_specs=(HBM, VMEM),
+        scratch_shapes=[
+            pltpu.VMEM((request_count + KNB, 2, NTOK, width), jnp.bfloat16),
+            pltpu.VMEM((tok_rows, width), jnp.bfloat16),
+            pltpu.SemaphoreType.DMA((request_count + KNB,)),
+            pltpu.SemaphoreType.DMA((grps * tps,)),
+        ],
+        compiler_params=WIDE,
+    )(codes, queries, attention_cotangent, store)
+
+    heads = lax.all_to_all(spread, FEATS, split_axis=0, concat_axis=0, tiled=True)
+    all_stats = lax.all_gather(stats, "seq", axis=0, tiled=True)
+    neighbour_gradient, finished = pl.pallas_call(
+        functools.partial(pair_backward, 4),
+        cost_estimate=cost(10),
+        out_shape=(
+            jax.ShapeDtypeStruct(neighbour_states.shape, jnp.bfloat16),
+            jax.ShapeDtypeStruct((8, HDIM), jnp.float32),
+        ),
+        in_specs=[SMEM, ANY, VMEM, VMEM],
         out_specs=(VMEM, VMEM),
         scratch_shapes=[
-            pltpu.VMEM((request_count + KNB, 2, NTOK, width), jnp.bfloat16),
-            pltpu.SemaphoreType.DMA((request_count + KNB,)),
+            pltpu.VMEM(neighbour_states.shape, jnp.float32),
+            pltpu.VMEM((owners * CAP, SPAN + 16, 2 * width), jnp.bfloat16),
+            pltpu.SemaphoreType.DMA((owners * CAP,)),
         ],
-        compiler_params=LIMIT,
-    )(codes, queries, attention_cotangent, store)
-
-    spread = jnp.broadcast_to(attention[None], (grps * tps, tok_rows, width))
-    heads = lax.all_to_all(spread, FEATS, split_axis=0, concat_axis=0, tiled=True)
-    all_stats = lax.all_gather(stats, "seq", axis=0, tiled=True)
-    neighbour_gradient = pl.pallas_call(
-        functools.partial(pair_backward, 2),
-        cost_estimate=cost(10),
-        out_shape=jax.ShapeDtypeStruct(neighbour_states.shape, jnp.bfloat16),
-        in_specs=[SMEM, VMEM, VMEM, VMEM],
-        out_specs=VMEM,
-        scratch_shapes=[pltpu.VMEM(neighbour_states.shape, jnp.float32)],
         compiler_params=LIMIT,
     )(slots, gathered, neighbour_states, all_stats)
     layer_output = pl.pallas_call(
         project,
         cost_estimate=cost(5),
+        grid_spec=pltpu.PrefetchScalarGridSpec(
+            num_scalar_prefetch=1,
+            grid=(grps * tps // sources,),
+            in_specs=[
+                pl.BlockSpec((sources, tok_rows, width), lambda i, core: (i, 0, 0)),
+                pl.BlockSpec((sources, width, half), lambda i, core: (i, 0, 0)),
+                pl.BlockSpec((sources, width, half), lambda i, core: (i, 0, 0)),
+                ANY,
+            ],
+            out_specs=pl.BlockSpec((tok_rows, out_columns), lambda i, core: (0, 0)),
+            scratch_shapes=[pltpu.VMEM((tok_rows, out_columns), jnp.float32)],
+        ),
         out_shape=jax.ShapeDtypeStruct((tok_rows, out_columns), jnp.bfloat16),
-        in_specs=[SMEM, VMEM, VMEM, VMEM],
-        out_specs=VMEM,
         compiler_params=LIMIT,
-    )(core, heads, weight, weight_other)
+    )(core, heads, weight, weight_other, finished)
     return (layer_output, neighbour_gradient)
 
 

time: 174 us -> 161 us (0.925)
  the two profiles are of different devices: /device:TPU:28 before, /device:TPU:1 now
where the time goes in v4:
time: 161 us
  waiting for transfers between devices  59.1 us (37%)
  blocking collectives  39.9 us (25%)
  Pallas kernels  27.1 us (17%)
  starting transfers between devices  15.3 us (10%)
  between operations  14.2 us (9%)
  local copies, waits for them, and re-layouts  3.65 us (2%)
    all_to_all x1, waiting for transfers between devices, local(): weight = lax.all_to_all(cut, FEATS, split_axis=0, concat_axis=0, tiled=True)  27 us
    all_gather x1, blocking collectives, local(): lax.all_gather(jnp.stack([retrieved.reshape(request_count), valid_blocks....  23.3 us
    all_gather x1, waiting for transfers between devices, local(): gathered = lax.all_gather(both, 'seq', axis=0, tiled=True)  16.9 us
    all_gather x1, blocking collectives, local(): all_stats = lax.all_gather(stats, 'seq', axis=0, tiled=True)  16.6 us
    all_gather x1, waiting for transfers between devices, local(): store = lax.all_gather(neighbour_states, 'seq', axis=0)  14.5 us
    pallas_call x1, Pallas kernels, local(): pl.pallas_call(functools.partial(pair_backward, 4), cost_estimate=cost(10...  10.5 us
    all_to_all x1, starting transfers between devices, local(): weight = lax.all_to_all(cut, FEATS, split_axis=0, concat_axis=0, tiled=True)  7.73 us
    pallas_call x1, Pallas kernels, local(): pl.pallas_call(span_forward, cost_estimate=cost(5), out_shape=(jax.ShapeD...  7.01 us
  transfers between devices with their start and end apart: 5, of which 3 were waited for; matrix products, arithmetic and copies ran while one was open for 2% of the time, Pallas kernels for 14%

profile of v4, /device:TPU:1, one launch (start us, length us, event | category | flops | bytes accessed | tf_op | source)
XLA Modules:
  0.0 160.5 jit_solution(8736577320236231053)
XLA Ops:
  7.2 0.0 all-gather.8.cloned.1.call-start
  7.2 0.7 all-gather.8.cloned.1.call-update
  7.9 4.3 %shard_map.77 = bf16[16,256,256]{2,1,0:T(8,128)(2,1)} custom-call(s32[1]{0:T(128)} %bitcast.core, bf16[256,8192]{1,0:T(8,128)(2,1)} %columns.1), custom_call_target="tpu_custom_call" | custom-call | tf_op jit(solution)/shard_map/pallas_call | solution.py:248
  12.2 7.7 %all-to-all-start = ((bf16[16,256,256]{2,1,0:T(8,128)(2,1)}), bf16[16,256,256]{2,1,0:T(8,128)(2,1)S(1)}, u32[]{:S(2)}, u32[]{:S(2)}) async-start(bf16[16,256,256]{2,1,0:T(8,128)(2,1)} %shard_map.77), calls=%async_computation | async-start | bytes 4194304 | tf_op jit(solution)/shard_map/all_to_all | solution.py:258
  20.0 0.0 all-gather.6.cloned.1.call-start
  20.0 0.8 pad_maximum_fusion.refs_0_
  20.8 27.0 %all-to-all-done.refs_3_.refs_1_.mine = bf16[16,256,256]{2,1,0:T(8,128)(2,1)S(1)} async-done(((bf16[16,256,256]{2,1,0:T(8,128)(2,1)}), bf16[16,256,256]{2,1,0:T(8,128)(2,1)S(1)}, u32[]{:S(2)}, u32[]{:S(2)}) %all-to-all-start) | async-done | bytes 2097184 | tf_op jit(solution)/shard_map/all_to_all | solution.py:258
  47.8 1.3 copy-done
  49.2 0.1 copy.50
  49.3 0.1 stack_reshape.6
  49.4 0.1 copy.51
  49.5 0.1 stack_reshape.7
  49.6 23.3 %all-gather.2 = s32[16,2,12]{2,1,0:T(2,128)S(1)} all-gather(s32[1,2,12]{2,1,0:T(2,128)S(1)} %add_bitcast_fusion), channel_id=2, replica_groups=mesh['grp'=4,'seq'=16,'tp'=4] {'seq'}, dimensions={0}, use_global_device_ids=true | all-gather | bytes 1632 | tf_op jit(solution)/shard_map/all_gather | solution.py:260
  72.9 0.1 copy.55
  73.0 0.1 copy.62
  73.1 0.1 copy.59
  73.2 0.1 copy.63
  73.3 0.4 convert_reduce_fusion
  73.7 0.1 fusion.4
  73.8 0.1 copy.60
  73.8 0.7 reshape.142.refs_1_.slots
  74.5 0.1 copy.54
  74.6 0.1 add.61
  74.7 0.7 pad_dynamic-slice_fusion.refs_2_.codes
  75.3 14.5 %all-gather.8.cloned.1.call-done = bf16[32,6,128,256]{3,2,1,0:T(8,128)(2,1)} async-done(((bf16[2,6,128,256]{3,2,1,0:T(8,128)(2,1)}), bf16[32,6,128,256]{3,2,1,0:T(8,128)(2,1)}) %all-gather.8.cloned.1.call-update) | async-done | bytes 12582928 | tf_op jit(solution)/shard_map/all_gather | solution.py:278
  89.8 7.0 %shard_map.79 = (bf16[16,384,256]{2,1,0:T(8,128)(2,1)}, f32[6,4,128]{2,1,0:T(4,128)}) custom-call(s32[14]{0:T(128)} %pad_dynamic-slice_fusion.refs_2_.codes, bf16[384,256]{1,0:T(8,128)(2,1)} %queries.1, bf16[384,256]{1,0:T(8,128)(2,1)} %cotangents.1, bf16[16,2,6,128,256]{4,3,2,1,0:T(8,128)(2,1)} %shard_map.78.store), custom_call_target="tpu_custom_call" | custom-call | flops 5000000000 | bytes 8388608 | tf_op jit(solution)/shard_map/pallas_call | solution.py:284
  96.9 6.8 %all-to-all-start.1 = ((bf16[16,384,256]{2,1,0:T(8,128)(2,1)}), bf16[16,384,256]{2,1,0:T(8,128)(2,1)}, u32[]{:S(2)}, u32[]{:S(2)}) async-start(bf16[16,384,256]{2,1,0:T(8,128)(2,1)} %get-tuple-element.6), calls=%async_computation.1 | async-start | bytes 6291456 | tf_op jit(solution)/shard_map/all_to_all | solution.py:302
  103.8 0.6 collective-permute-start
  104.4 16.6 %all_gather.23.stats = f32[96,4,128]{2,1,0:T(4,128)S(1)} all-gather(f32[6,4,128]{2,1,0:T(4,128)S(1)} %copy-done.6), channel_id=1, replica_groups=mesh['grp'=4,'seq'=16,'tp'=4] {'seq'}, dimensions={0}, use_global_device_ids=true | all-gather | bytes 208896 | tf_op jit(solution)/shard_map/all_gather | solution.py:303
  121.0 16.9 %all-gather.6.cloned.1.call-done.rows = bf16[6144,512]{1,0:T(8,128)(2,1)} async-done(((bf16[384,512]{1,0:T(8,128)(2,1)}), bf16[6144,512]{1,0:T(8,128)(2,1)}) %all-gather.6.cloned.1.call-update) | async-done | bytes 6291472 | tf_op jit(solution)/shard_map/all_gather | solution.py:281
  137.9 10.5 %shard_map.81 = (bf16[2,6,128,256]{3,2,1,0:T(8,128)(2,1)}, f32[8,128]{1,0:T(8,128)S(1)}) custom-call(s32[32]{0:T(128)S(1)} %copy-done.3, bf16[6144,512]{1,0:T(8,128)(2,1)} %all-gather.6.cloned.1.call-done.rows, bf16[2,6,128,256]{3,2,1,0:T(8,128)(2,1)S(1)} %copy-done.2, f32[96,4,128]{2,1,0:T(4,128)S(1)} %all_gather.23.stats), custom_call_target="tpu_custom_call" | custom-call | flops 10000000000 | bytes 8388608 | tf_op jit(solution)/shard_map/pallas_call | solution.py:304
  148.4 5.3 %shard_map.82 = bf16[384,512]{1,0:T(8,128)(2,1)} custom-call(s32[1]{0:T(128)} %bitcast.core, bf16[16,384,256]{2,1,0:T(8,128)(2,1)} %all-to-all-done.1.blocks, bf16[16,256,256]{2,1,0:T(8,128)(2,1)S(1)} %copy-done.1, bf16[16,256,256]{2,1,0:T(8,128)(2,1)} %collective-permute-done.other, f32[8,128]{1,0:T(8,128)S(1)} %get-tuple-element.8.earlier), custom_call_target="tpu_custom_call" | custom-call | flops 5000000000 | bytes 8388608 | tf_op jit(solution)/shard_map/pallas_call | solution.py:320
  (33 shorter events, 0.2 us)
Async XLA Ops:
  7.2 82.7 %all-gather.8.cloned.1.call-start = ((), (), s32[]{:S(2)}) async-start(), calls=%async_computation.3 | async-start | bytes 13369344 | tf_op jit(solution)/shard_map/all_gather | solution.py:278
  12.2 7.8 %copy-start.4 = (bf16[384,256]{1,0:T(8,128)(2,1)S(1)}, bf16[384,256]{1,0:T(8,128)(2,1)}, u32[]{:S(2)}) copy-start(bf16[384,256]{1,0:T(8,128)(2,1)} %queries.1) | copy-start | bytes 589828
  12.2 7.8 %copy-start.5 = (bf16[384,256]{1,0:T(8,128)(2,1)S(1)}, bf16[384,256]{1,0:T(8,128)(2,1)}, u32[]{:S(2)}) copy-start(bf16[384,256]{1,0:T(8,128)(2,1)} %cotangents.1) | copy-start | bytes 589828
  12.2 37.0 %copy-start.7 = (s32[6,2]{0,1:T(2,128)S(1)}, s32[6,2]{0,1:T(2,128)}, u32[]{:S(2)}) copy-start(s32[6,2]{0,1:T(2,128)} %param.8) | copy-start | bytes 148
  12.2 37.2 %copy-start.8 = (s32[6,2]{0,1:T(2,128)S(1)}, s32[6,2]{0,1:T(2,128)}, u32[]{:S(2)}) copy-start(s32[6,2]{0,1:T(2,128)} %param.9) | copy-start | bytes 148
  12.2 35.6 %all-to-all-start = ((bf16[16,256,256]{2,1,0:T(8,128)(2,1)}), bf16[16,256,256]{2,1,0:T(8,128)(2,1)S(1)}, u32[]{:S(2)}, u32[]{:S(2)}) async-start(bf16[16,256,256]{2,1,0:T(8,128)(2,1)} %shard_map.77), calls=%async_computation | async-start | bytes 4194304 | tf_op jit(solution)/shard_map/all_to_all | solution.py:258
  20.0 117.9 %all-gather.6.cloned.1.call-start = ((), (), s32[]{:S(2)}) async-start(), calls=%async_computation.2 | async-start | bytes 6684672 | tf_op jit(solution)/shard_map/all_gather | solution.py:281
  47.8 1.3 copy-start
  96.9 6.9 %copy-start.1 = (bf16[16,256,256]{2,1,0:T(8,128)(2,1)S(1)}, bf16[16,256,256]{2,1,0:T(8,128)(2,1)}, u32[]{:S(2)}) copy-start(bf16[16,256,256]{2,1,0:T(8,128)(2,1)} %copy-done) | copy-start | bytes 6291460
  96.9 7.5 %copy-start.6 = (f32[6,4,128]{2,1,0:T(4,128)S(1)}, f32[6,4,128]{2,1,0:T(4,128)}, u32[]{:S(2)}) copy-start(f32[6,4,128]{2,1,0:T(4,128)} %get-tuple-element.7) | copy-start | bytes 36868
  96.9 41.0 %copy-start.2 = (bf16[2,6,128,256]{3,2,1,0:T(8,128)(2,1)S(1)}, bf16[2,6,128,256]{3,2,1,0:T(8,128)(2,1)}, u32[]{:S(2)}) copy-start(bf16[2,6,128,256]{3,2,1,0:T(8,128)(2,1)} %states.1) | copy-start | bytes 2359300
  96.9 41.0 %copy-start.3 = (s32[32]{0:T(128)S(1)}, s32[32]{0:T(128)}, u32[]{:S(2)}) copy-start(s32[32]{0:T(128)} %reshape.142.refs_1_.slots) | copy-start | bytes 388
  96.9 51.5 %all-to-all-start.1 = ((bf16[16,384,256]{2,1,0:T(8,128)(2,1)}), bf16[16,384,256]{2,1,0:T(8,128)(2,1)}, u32[]{:S(2)}, u32[]{:S(2)}) async-start(bf16[16,384,256]{2,1,0:T(8,128)(2,1)} %get-tuple-element.6), calls=%async_computation.1 | async-start | bytes 6291456 | tf_op jit(solution)/shard_map/all_to_all | solution.py:302
  103.8 44.7 %collective-permute-start = (bf16[16,256,256]{2,1,0:T(8,128)(2,1)S(1)}, bf16[16,256,256]{2,1,0:T(8,128)(2,1)}, u32[]{:S(2)}, u32[]{:S(2)}) collective-permute-start(bf16[16,256,256]{2,1,0:T(8,128)(2,1)S(1)} %copy-done.1), channel_id=1, source_target_pairs={{0,4},{4,0},{8,12},{12,8},{16,20},{20,16},{24,28},{28,24},{32,36},... | collective-permute-start | bytes 6291464 | tf_op jit(solution)/shard_map/ppermute | solution.py:282
Sparse Core Ops, SparseCore 0:
  9.8 79.9 all-gather.7
  92.2 45.6 all-gather.5

commit v5 on v2

v5 whole, which is shorter than its diff:
```python
import functools

import jax
import jax.numpy as jnp
from jax import lax
from jax.experimental import pallas as pl
from jax.experimental.pallas import tpu as pltpu
from jax.sharding import PartitionSpec as P

HDIM = 128
SPAN = 64
NTOK = 128
KNB = 2
CAP = 2
FEATS = ("grp", "tp")
LOG2E = 1.4426950408889634
NT = (((1,), (1,)), ((), ()))
NN = (((1,), (0,)), ((), ()))
TN = (((0,), (0,)), ((), ()))
VMEM = pl.BlockSpec(memory_space=pltpu.VMEM)
SMEM = pl.BlockSpec(memory_space=pltpu.SMEM)
ANY = pl.BlockSpec(memory_space=pl.ANY)
LIMIT = pltpu.CompilerParams(vmem_limit_bytes=48 * 1024 * 1024)
WIDE = pltpu.CompilerParams(vmem_limit_bytes=60 * 1024 * 1024)


def cost(gigaflops):
    return pl.CostEstimate(flops=int(gigaflops * 1e9), bytes_accessed=8 * 1024 * 1024, transcendentals=0)


def dot(a, b, dims):
    return lax.dot_general(a, b, dims, preferred_element_type=jnp.float32)


def tied(value, *others):
    return pl.pallas_call(
        lambda *refs: None,
        out_shape=jax.ShapeDtypeStruct(value.shape, value.dtype),
        in_specs=[ANY] * (1 + len(others)),
        out_specs=ANY,
        input_output_aliases={0: 0},
    )(value, *others)


def three_parts(x):
    high = x.astype(jnp.bfloat16).astype(jnp.float32)
    middle = (x - high).astype(jnp.bfloat16).astype(jnp.float32)
    return [high, middle, x - high - middle]


def decode_slot(code):
    return code & 127, (code >> 7) & 7, code >> 10


def span_tokens(window, span, spans):
    place = lax.broadcasted_iota(jnp.int32, (16, window.shape[1]), 0)
    first_token = (place == 15) & (span < spans - 1)
    tail = jnp.where(first_token, window[:16, :], window[SPAN:, :])
    return jnp.concatenate([window[16:SPAN, :], tail], 0)


def diagonal(first, second):
    zero = jnp.zeros_like(first)
    return jnp.concatenate(
        [jnp.concatenate([first, zero], 1), jnp.concatenate([zero, second], 1)], 0
    )


def whole_tokens(rows, span):
    block = jnp.minimum(span + 1, rows.shape[0] // SPAN - 1)
    main = rows[pl.ds(pl.multiple_of(block * SPAN, SPAN), SPAN), :]
    before = rows[pl.ds(pl.multiple_of(span * SPAN + SPAN - 16, 16), 16), :]
    place = lax.broadcasted_iota(jnp.int32, before.shape, 0)
    return jnp.concatenate([main[: SPAN - 16], jnp.where(place == 15, before, main[SPAN - 16 :])], 0)


def pair_forward(together, distances, slots, states, *rest):
    pieces, (out, rows, sems) = rest[:-3], rest[-3:]
    per_core = len(pieces) // 2
    me = lax.axis_index("seq")
    chips = lax.axis_size("seq") // 2
    height = rows.shape[0] // (2 * chips)
    copies = []
    for i, piece in enumerate(pieces):
        distance, start = distances[i % per_core]
        chip = lax.rem(lax.div(me, 2) + (chips - distance) % chips, chips)
        core = lax.rem(lax.rem(me, 2) + i // per_core, 2)
        at = pl.multiple_of((chip * 2 + core) * height + start, 64)
        copies.append(pltpu.make_async_copy(piece, rows.at[pl.ds(at, piece.shape[0])], sems.at[i]))
        copies[-1].start()
    for copy in copies:
        copy.wait()
    width = states.shape[3]
    scale = HDIM ** (-0.5)

    def one_target(target):
        span_0, row_0, _ = decode_slot(slots[target * CAP])
        span_1, row_1, _ = decode_slot(slots[target * CAP + 1])
        tokens_0, tokens_1 = whole_tokens(rows, span_0), whole_tokens(rows, span_1)
        lse_heads, attended_0, attended_1 = [], [], []
        for at in range(0, width, HDIM):
            q = diagonal(tokens_0[:, at : at + HDIM], tokens_1[:, at : at + HDIM])
            k = jnp.concatenate([states[0, row_0, :, at : at + HDIM], states[0, row_1, :, at : at + HDIM]], 1)
            v = jnp.concatenate([states[1, row_0, :, at : at + HDIM], states[1, row_1, :, at : at + HDIM]], 1)
            scores = dot(k, q, NT)
            top = jnp.max(scores, axis=0, keepdims=True)
            weights = jnp.exp2((scores - top) * (scale * LOG2E))
            total = jnp.sum(weights, axis=0, keepdims=True)
            weights = weights * (1.0 / total)
            lse_heads.append(top * scale + jnp.log(total))
            mixed = dot(weights.astype(jnp.bfloat16), v, TN)
            attended_0.append(mixed[:SPAN, :HDIM])
            attended_1.append(mixed[SPAN:, HDIM:])
        lines = three_parts(jnp.concatenate(lse_heads, 1))
        lines.append(jnp.zeros((16 - len(lines), width), jnp.float32))
        return [jnp.concatenate(each, 1) for each in (attended_0, attended_1)] + [jnp.concatenate(lines, 0)]

    def some_targets(step, carry):
        results = [one_target(step * together + i) for i in range(together)]
        for i, parts in enumerate(results):
            target = step * together + i
            out[target, pl.ds(0, SPAN), :] = parts[0].astype(out.dtype)
            out[target, pl.ds(SPAN, SPAN), :] = parts[1].astype(out.dtype)
            out[target, pl.ds(CAP * SPAN, 16), :] = parts[2].astype(out.dtype)
        return carry

    lax.fori_loop(0, out.shape[0] // together, some_targets, 0)


def merge_pairs(requests, arrived, cotangents, next_block, *rest):
    upper, lower, last, stats = rest[-4:]
    width = arrived.shape[2]
    heads = range(0, width, HDIM)
    count = len(heads)
    spans = stats.shape[0]
    early = lax.broadcasted_iota(jnp.int32, (8, HDIM), 1) < SPAN
    lane = lax.broadcasted_iota(jnp.int32, (SPAN, HDIM), 1)
    place = lax.broadcasted_iota(jnp.int32, (16, width), 0)
    final_row = lax.broadcasted_iota(jnp.int32, (SPAN, width), 0) == SPAN - 1
    previous = jnp.zeros((SPAN, width), jnp.float32)
    for span in range(spans):
        lse, live, parts = [], [], []
        for k in range(KNB):
            code = requests[span * KNB + k]
            owner, side, valid = code & 15, (code >> 4) & 1, code >> 5 > 0
            both = arrived[owner, pl.ds(CAP * SPAN, 16), :].astype(jnp.float32)[:8]
            sides = []
            for at in heads:
                part = both[:, at : at + HDIM]
                sides.append(jnp.where(early == (side == 0), part, pltpu.roll(part, SPAN, 1)))
            mine = jnp.concatenate(sides, 1)
            lse.append(jnp.where(valid, mine[0:1] + (mine[1:2] + mine[2:3]), -1e30))
            live.append(valid)
            rows = arrived[owner, pl.ds(pl.multiple_of(side * SPAN, SPAN), SPAN), :]
            parts.append(jnp.where(valid, rows.astype(jnp.float32), 0.0))
        top = jnp.maximum(lse[0], lse[1])
        share = [jnp.where(live[k], jnp.exp(lse[k] - top), 0.0) for k in range(KNB)]
        total = jnp.maximum(share[0] + share[1], 1.0)
        share = [each / total for each in share]
        lse_all = top + jnp.log(total)
        lines = [each[:, at : at + HDIM] for each in share for at in heads]
        columns = jnp.concatenate(lines + [jnp.zeros((HDIM - len(lines), HDIM), jnp.float32)], 0).T[:SPAN]
        mixed = jnp.concatenate(
            [
                parts[0][:, at : at + HDIM] * columns[:, h : h + 1]
                + parts[1][:, at : at + HDIM] * columns[:, count + h : count + h + 1]
                for h, at in enumerate(heads)
            ],
            1,
        )
        block = jnp.where(final_row, mixed, previous)
        half, place_in = (upper, span) if span < spans // 2 else (lower, span - spans // 2)
        half[pl.ds(place_in * SPAN, SPAN), :] = block.astype(half.dtype)
        previous = mixed
        main = cotangents[(span + 1) * SPAN : (span + 2) * SPAN, :] if span < spans - 1 else next_block[...]
        before = cotangents[(span + 1) * SPAN - 16 : (span + 1) * SPAN, :]
        tail = jnp.where(place == 15, before, main[SPAN - 16 :])
        product = mixed * jnp.concatenate([main[: SPAN - 16], tail], 0).astype(jnp.float32)
        square = jnp.zeros((SPAN, HDIM), jnp.float32)
        for h, at in enumerate(heads):
            square = jnp.where(lane == h, jnp.sum(product[:, at : at + HDIM], axis=1, keepdims=True), square)
        delta = jnp.concatenate([square, square], 0).T[:count]
        stats[span] = jnp.concatenate([lse_all[:, at : at + HDIM] for at in heads] + [delta], 0)
    last[...] = previous.astype(last.dtype)


def pair_backward(together, slots, queries, cotangents, states, stats, out, finished, total, windows, sems):
    finished[...] = jnp.zeros_like(finished)
    spans = stats.shape[0]
    reach = SPAN + 16
    for i in range(slots.shape[0]):
        span = decode_slot(slots[i])[0]
        start = jnp.minimum(span * SPAN + SPAN - 16, queries.shape[0] - reach)
        for kind, rows in enumerate((queries, cotangents)):
            source = rows.at[pl.ds(pl.multiple_of(start, 16), reach)]
            pltpu.make_async_copy(source, windows.at[kind, i], sems.at[kind, i]).start()
    total[...] = jnp.zeros_like(total)
    width = states.shape[3]
    heads = width // HDIM
    scale = HDIM ** (-0.5)
    lane = lax.broadcasted_iota(jnp.int32, (1, 2 * SPAN), 1)
    early = lane < SPAN
    first_token = lane % SPAN == SPAN - 1
    last_span = stats.shape[0] - 1

    def one_target(target):
        span_0, row_0, live_0 = decode_slot(slots[target * CAP])
        span_1, row_1, live_1 = decode_slot(slots[target * CAP + 1])
        q_0, g_0 = [span_tokens(windows.at[kind, target * CAP], span_0, spans) for kind in range(2)]
        q_1, g_1 = [span_tokens(windows.at[kind, target * CAP + 1], span_1, spans) for kind in range(2)]
        span = jnp.where(early, span_0, span_1)
        seen = (jnp.where(early, live_0, live_1) > 0) & (first_token | (span < last_span))
        lines = jnp.where(early, stats[span_0], stats[span_1])
        parts = []
        for h in range(heads):
            at = h * HDIM
            q = diagonal(q_0[:, at : at + HDIM], q_1[:, at : at + HDIM])
            g = diagonal(g_0[:, at : at + HDIM], g_1[:, at : at + HDIM])
            k = jnp.concatenate([states[0, row_0, :, at : at + HDIM], states[0, row_1, :, at : at + HDIM]], 1)
            v = jnp.concatenate([states[1, row_0, :, at : at + HDIM], states[1, row_1, :, at : at + HDIM]], 1)
            scores = dot(k, q, NT) * scale
            weights = jnp.where(seen, jnp.exp(scores - lines[h : h + 1]), 0.0)
            grads = weights * (dot(v, g, NT) - lines[heads + h : heads + h + 1])
            key_part = dot(grads.astype(jnp.bfloat16), q, NN) * scale
            value_part = dot(weights.astype(jnp.bfloat16), g, NN)
            parts.append((key_part, value_part))
        return row_0, row_1, parts

    def some_targets(step, carry):
        for i in range(together * CAP):
            at = step * together * CAP + i
            for kind, rows in enumerate((queries, cotangents)):
                pltpu.make_async_copy(
                    rows.at[pl.ds(0, reach)], windows.at[kind, at], sems.at[kind, at]
                ).wait()
        results = [one_target(step * together + i) for i in range(together)]
        for row_0, row_1, parts in results:
            for h, pair in enumerate(parts):
                for kind, part in enumerate(pair):
                    total[kind, row_0, :, h * HDIM : (h + 1) * HDIM] += part[:, :HDIM]
                    total[kind, row_1, :, h * HDIM : (h + 1) * HDIM] += part[:, HDIM:]
        return carry

    lax.fori_loop(0, slots.shape[0] // CAP // together, some_targets, 0)
    out[...] = total[...].astype(out.dtype)


def cut_weight(core, columns, block):
    count, _, half = block.shape
    for i in range(count):
        at = pl.multiple_of((2 * i + core[0]) * half, 128)
        block[i] = columns[:, pl.ds(at, half)]


def shifted(value, axis, steps):
    count = lax.axis_size(axis)
    return lax.ppermute(value, axis, [(source, (source + steps) % count) for source in range(count)])


def halves_round(first, second, axis):
    half = first.shape[1] // 2
    return [shifted(first[:, :half], axis, 1), shifted(second[:, half:], axis, lax.axis_size(axis) - 1)]


def source_of(steps_grp, steps_tp):
    grps, tps = lax.axis_size("grp"), lax.axis_size("tp")
    grp = lax.rem(lax.axis_index("grp") + (grps - steps_grp) % grps, grps)
    return grp * tps + lax.rem(lax.axis_index("tp") + (tps - steps_tp) % tps, tps)


def project_near(*refs):
    blocks, weights, out = refs[:6], refs[6:8], refs[-1]
    side = lax.axis_size("tp")
    rows, width = blocks[0].shape[0], weights[0].shape[1]
    for half in range(2):
        for kind, weight in enumerate(weights):
            total = None
            for block, step in zip(blocks[half * 3 : half * 3 + 3], (0, 1, side - 1)):
                for inner in range(side):
                    source = source_of(inner, step) if half == 0 else source_of(step, inner)
                    term = dot(block[:, inner * width : (inner + 1) * width], weight[source], NN)
                    total = term if total is None else total + term
            out[kind, pl.ds(half * rows, rows), :] = total


def project_far(*refs):
    blocks, weights, partial, out = refs[:4], refs[4:6], refs[6], refs[7]
    side = lax.axis_size("tp")
    rows, width = blocks[0].shape[0], weights[0].shape[1]
    columns = weights[0].shape[2]
    core = lax.rem(lax.axis_index("seq"), 2)
    for half in range(2):
        for kind, weight in enumerate(weights):
            total = partial[kind, pl.ds(half * rows, rows), :]
            for inner in range(side):
                block = blocks[half * 2 + inner // (side // 2)]
                at = inner % (side // 2) * width
                far = side // 2
                source = source_of(inner, far) if half == 0 else source_of(far, inner)
                total = total + dot(block[:, at : at + width], weight[source], NN)
            at = pl.multiple_of((core if kind == 0 else 1 - core) * columns, 128)
            out[pl.ds(half * rows, rows), pl.ds(at, columns)] = total.astype(out.dtype)


def local(queries, neighbour_states, retrieved, valid_blocks, output_weight, attention_cotangent):
    owners = lax.axis_size("seq")
    grps, tps = lax.axis_size("grp"), lax.axis_size("tp")
    me = lax.axis_index("seq")
    tok_rows, width = queries.shape
    span_count = tok_rows // SPAN
    request_count = span_count * KNB
    store_rows = neighbour_states.shape[1]
    out_columns = output_weight.shape[1] // (grps * tps)

    core = (me & 1).reshape(1)
    half = out_columns // 2
    sources = 4 if grps * tps % 4 == 0 else 1
    cut = pl.pallas_call(
        cut_weight,
        grid_spec=pltpu.PrefetchScalarGridSpec(
            num_scalar_prefetch=1,
            grid=(grps * tps // sources,),
            in_specs=[pl.BlockSpec((width, sources * out_columns), lambda i, core: (0, i))],
            out_specs=pl.BlockSpec((sources, width, half), lambda i, core: (i, 0, 0)),
        ),
        out_shape=jax.ShapeDtypeStruct((grps * tps, width, half), jnp.bfloat16),
    )(core, output_weight)
    weight = lax.all_to_all(cut, FEATS, split_axis=0, concat_axis=0, tiled=True)

    table = jnp.stack([retrieved.reshape(request_count), valid_blocks.reshape(request_count)])[None]
    distance = 1
    while distance < owners:
        there = lax.ppermute(table, "seq", [(at, at ^ distance) for at in range(owners)])
        table = jnp.where(
            (me & distance) > 0, jnp.concatenate([there, table]), jnp.concatenate([table, there])
        )
        distance *= 2
    owner_of = table[:, 0] // store_rows
    same_owner = owner_of[:, :, None] == owner_of[:, None, :]
    order = jnp.arange(request_count, dtype=jnp.int32)
    earlier = order[None, :] < order[:, None]
    position = jnp.sum((same_owner & earlier[None]).astype(jnp.int32), axis=2)
    span_of = jnp.arange(owners, dtype=jnp.int32)[:, None] * span_count + order[None, :] // KNB
    code = span_of + 128 * (table[:, 0] % store_rows) + 1024 * (table[:, 1] > 0).astype(jnp.int32)
    hit = (owner_of == me)[:, None, :] & (
        position[:, None, :] == jnp.arange(CAP, dtype=jnp.int32)[None, :, None]
    )
    slots = jnp.sum(jnp.where(hit, code[:, None, :], 0), axis=2).reshape(owners * CAP)
    mine = owner_of + 16 * position + 32 * (table[:, 1] > 0).astype(jnp.int32)
    requests = lax.dynamic_index_in_dim(mine, me, 0, keepdims=False)

    def steps(value, chips):
        return lax.ppermute(value, "seq", [(at, (at + 2 * chips) % owners) for at in range(owners)])

    def swap(value):
        return lax.ppermute(value, "seq", [(at, at ^ 1) for at in range(owners)])

    middle = tok_rows // 2
    up_1, down_1, up_2, down_2 = [steps(queries, i) for i in (1, -1, 2, -2)]
    far = [steps(up_2, 1), steps(down_2, -1), steps(up_2[:middle], 2), steps(down_2[middle:], -2)]
    distances = [(0, 0), (1, 0), (-1, 0), (2, 0), (-2, 0), (3, 0), (-3, 0), (4, 0), (4, middle)]
    pieces = [queries, up_1, down_1, up_2, down_2, *far]
    pieces = pieces + [swap(piece) for piece in pieces]
    next_block = lax.ppermute(attention_cotangent[:SPAN], "seq", [(at + 1, at) for at in range(owners - 1)])
    cotangents = lax.all_gather(attention_cotangent, "seq", axis=0, tiled=True)

    outgoing, all_queries = pl.pallas_call(
        functools.partial(pair_forward, 2, distances),
        cost_estimate=cost(8),
        out_shape=(
            jax.ShapeDtypeStruct((owners, CAP * SPAN + 16, width), jnp.bfloat16),
            jax.ShapeDtypeStruct((owners * tok_rows, width), jnp.bfloat16),
        ),
        in_specs=[SMEM, VMEM] + [ANY] * len(pieces),
        out_specs=(VMEM, VMEM),
        scratch_shapes=[pltpu.SemaphoreType.DMA((len(pieces),))],
        compiler_params=LIMIT,
    )(slots, neighbour_states, *pieces)
    arrived = lax.all_to_all(outgoing, "seq", split_axis=0, concat_axis=0, tiled=True)
    upper, lower, last, stats = pl.pallas_call(
        merge_pairs,
        cost_estimate=cost(2),
        out_shape=(
            jax.ShapeDtypeStruct((middle, width), jnp.bfloat16),
            jax.ShapeDtypeStruct((middle, width), jnp.bfloat16),
            jax.ShapeDtypeStruct((SPAN, width), jnp.bfloat16),
            jax.ShapeDtypeStruct((span_count, 2 * width // HDIM, 2 * SPAN), jnp.float32),
        ),
        in_specs=[SMEM, VMEM, VMEM, VMEM, ANY],
        out_specs=(VMEM, VMEM, VMEM, VMEM),
        compiler_params=LIMIT,
    )(requests, arrived, attention_cotangent, next_block, weight)
    weight_other = swap(weight)

    before = lax.ppermute(last, "seq", [(at, at + 1) for at in range(owners - 1)])
    lower = jnp.concatenate([lower] + [shifted(lower, "tp", i) for i in range(1, tps)], 1)
    final_row = lax.broadcasted_iota(jnp.int32, before.shape, 0) == SPAN - 1
    upper = jnp.concatenate([jnp.where(final_row, upper[:SPAN], before), upper[SPAN:]])
    upper = jnp.concatenate([upper] + [shifted(upper, "grp", i) for i in range(1, grps)], 1)
    upper = [upper, shifted(upper, "tp", 1), shifted(upper, "tp", tps - 1)]
    lower = [lower, shifted(lower, "grp", 1), shifted(lower, "grp", grps - 1)]
    far = halves_round(upper[1], upper[2], "tp") + halves_round(lower[1], lower[2], "grp")
    all_stats = lax.all_to_all(
        jnp.broadcast_to(stats[None], (owners, *stats.shape)), "seq", split_axis=0, concat_axis=0, tiled=True
    ).reshape(owners * span_count, *stats.shape[1:])
    neighbour_gradient, finished = pl.pallas_call(
        functools.partial(pair_backward, 4),
        cost_estimate=cost(10),
        out_shape=(
            jax.ShapeDtypeStruct(neighbour_states.shape, jnp.bfloat16),
            jax.ShapeDtypeStruct((8, HDIM), jnp.float32),
        ),
        in_specs=[SMEM, ANY, ANY, VMEM, VMEM],
        out_specs=(VMEM, VMEM),
        scratch_shapes=[
            pltpu.VMEM(neighbour_states.shape, jnp.float32),
            pltpu.VMEM((2, owners * CAP, SPAN + 16, width), jnp.bfloat16),
            pltpu.SemaphoreType.DMA((2, owners * CAP)),
        ],
        compiler_params=WIDE,
    )(slots, all_queries, cotangents, neighbour_states, all_stats)
    total = pl.pallas_call(
        project_near,
        cost_estimate=cost(3),
        out_shape=jax.ShapeDtypeStruct((2, tok_rows, half), jnp.float32),
        in_specs=[VMEM] * 8 + [ANY],
        out_specs=VMEM,
        compiler_params=LIMIT,
    )(*upper, *lower, weight, weight_other, finished)
    layer_output = pl.pallas_call(
        project_far,
        cost_estimate=cost(2),
        out_shape=jax.ShapeDtypeStruct((tok_rows, out_columns), jnp.bfloat16),
        in_specs=[VMEM] * 7,
        out_specs=VMEM,
        compiler_params=LIMIT,
    )(*far, weight, weight_other, total)
    return (layer_output, neighbour_gradient)


def solution(mesh):
    placed = (
        P("seq", FEATS),
        P(None, "seq", None, FEATS),
        P("seq", None),
        P("seq", None),
        P(FEATS, None),
        P("seq", FEATS),
    )
    return jax.shard_map(
        local,
        mesh=mesh,
        in_specs=placed,
        out_specs=(P("seq", FEATS), P(None, "seq", None, FEATS)),
        check_vma=False,
    )
```

time: 364 us -> 188 us (0.52)
  Pallas kernels: 160 us -> 36.2 us
  waiting for transfers between devices: 85 us -> 45.3 us
  blocking collectives: 37.4 us -> 0 us
  starting transfers between devices: 46.7 us -> 77.4 us
    pallas_call x4, Pallas kernels: 154 us -> 29.6 us  [the longest x1 11.9 us: local(): pl.pallas_call(functools.partial(pair_backward, 4), cost_estimate=cost(10...]
    all_gather x2 -> x0, blocking collectives: 37.4 us -> none  [the longest x1 21.3 us: local(): lax.all_gather(jnp.stack([retrieved.reshape(request_count), valid_blocks....]
    all_gather x1, waiting for transfers between devices: 27.1 us -> 0.01 us  [local(): cotangents = lax.all_gather(attention_cotangent, 'seq', axis=0, tiled=True)]
    all_to_all x0 -> x2, starting transfers between devices: none -> 14 us  [the longest x1 7.09 us: local(): lax.all_to_all(jnp.broadcast_to(stats[None], (owners, *stats.shape)), 'se...]
    ppermute x16 -> x24, waiting for transfers between devices: 52.2 us -> 42 us  [the longest x1 25.6 us: local(): lax.ppermute(attention_cotangent[:SPAN], 'seq', [(at + 1, at) for at in r...]
    ppermute x16 -> x24, starting transfers between devices: 26.1 us -> 35 us  [the longest x8 16.1 us: steps(): lax.ppermute(value, 'seq', [(at, (at + 2 * chips) % owners) for at in ran...]
    unnamed x48 -> x19, local copies, waits for them, and re-layouts: 13.9 us -> 5.8 us
    ppermute x14, waiting for transfers between devices: 5.74 us -> 0.04 us  [shifted(): lax.ppermute(value, axis, [(source, (source + steps) % count) for source...]
  transfers between devices with their start and end apart: 32 -> 42, of which waited for: 13 -> 13; matrix products, arithmetic and copies ran while one was open for 1% -> 6% of each run, Pallas kernels for 40% -> 18%
where the time goes in v5:
time: 188 us; the launch traced here: 187 us
  starting transfers between devices  77.4 us (41%)
  waiting for transfers between devices  45.3 us (24%)
  Pallas kernels  36.2 us (19%)
  between operations  14.4 us (8%)
  local copies, waits for them, and re-layouts  13 us (7%)
    ppermute x1, waiting for transfers between devices, local(): lax.ppermute(attention_cotangent[:SPAN], 'seq', [(at + 1, at) for at in r...  25.6 us
    ppermute x14, starting transfers between devices, shifted(): lax.ppermute(value, axis, [(source, (source + steps) % count) for source...  21.2 us
    ppermute x8, starting transfers between devices, steps(): lax.ppermute(value, 'seq', [(at, (at + 2 * chips) % owners) for at in ran...  16.1 us
    pallas_call x1, Pallas kernels, local(): pl.pallas_call(functools.partial(pair_backward, 4), cost_estimate=cost(10...  11.9 us
    pallas_call x1, Pallas kernels, local(): pl.pallas_call(functools.partial(pair_forward, 2, distances), cost_estima...  11.3 us
    ppermute x10, starting transfers between devices, swap(): return lax.ppermute(value, 'seq', [(at, at ^ 1) for at in range(owners)])  7.8 us
    ppermute x4, waiting for transfers between devices, local(): lax.ppermute(table, 'seq', [(at, at ^ distance) for at in range(owners)])  7.68 us
    ppermute x8, waiting for transfers between devices, steps(): lax.ppermute(value, 'seq', [(at, (at + 2 * chips) % owners) for at in ran...  7.63 us
  transfers between devices with their start and end apart: 42, of which 13 were waited for; matrix products, arithmetic and copies ran while one was open for 6% of the time, Pallas kernels for 18%

profile of v5, /device:TPU:1, one launch (start us, length us, event | category | flops | bytes accessed | tf_op | source)
XLA Modules:
  0.0 187.4 jit_solution(2831492174639201468)
XLA Ops:
  7.2 3.9 %collective-permute-start.6 = (bf16[384,256]{1,0:T(8,128)(2,1)}, bf16[384,256]{1,0:T(8,128)(2,1)S(1)}, u32[]{:S(2)}, u32[]{:S(2)}) collective-permute-start(bf16[384,256]{1,0:T(8,128)(2,1)} %rest_0_.1), channel_id=1, source_target_pairs={{0,16},{4,20},{8,24},{12,28},{16,32},{20,36},{24,40},{28,44},{32,4... | collective-permute-start | bytes 589832 | tf_op jit(solution)/shard_map/ppermute | solution.py:353
  11.1 3.1 %collective-permute-start.7 = (bf16[384,256]{1,0:T(8,128)(2,1)}, bf16[384,256]{1,0:T(8,128)(2,1)S(1)}, u32[]{:S(2)}, u32[]{:S(2)}) collective-permute-start(bf16[384,256]{1,0:T(8,128)(2,1)} %rest_0_.1), channel_id=1, source_target_pairs={{0,48},{4,52},{8,56},{12,60},{16,0},{20,4},{24,8},{28,12},{32,16},... | collective-permute-start | bytes 589832 | tf_op jit(solution)/shard_map/ppermute | solution.py:353
  14.9 1.9 %collective-permute-start.5 = (bf16[384,256]{1,0:T(8,128)(2,1)}, bf16[384,256]{1,0:T(8,128)(2,1)}, u32[]{:S(2)}, u32[]{:S(2)}) collective-permute-start(bf16[384,256]{1,0:T(8,128)(2,1)} %rest_0_.1), channel_id=1, source_target_pairs={{0,56},{4,60},{8,0},{12,4},{16,8},{20,12},{24,16},{28,20},{32,24},... | collective-permute-start | bytes 589832 | tf_op jit(solution)/shard_map/ppermute | solution.py:353
  20.2 4.3 %shard_map.78 = bf16[16,256,256]{2,1,0:T(8,128)(2,1)} custom-call(s32[1]{0:T(128)} %bitcast.7.core, bf16[256,8192]{1,0:T(8,128)(2,1)} %columns.1), custom_call_target="tpu_custom_call" | custom-call | tf_op jit(solution)/shard_map/pallas_call | solution.py:318
  24.5 6.9 %all-to-all-start.1 = ((bf16[16,256,256]{2,1,0:T(8,128)(2,1)}), bf16[16,256,256]{2,1,0:T(8,128)(2,1)S(1)}, u32[]{:S(2)}, u32[]{:S(2)}) async-start(bf16[16,256,256]{2,1,0:T(8,128)(2,1)} %shard_map.78), calls=%async_computation.1 | async-start | bytes 4194304 | tf_op jit(solution)/shard_map/all_to_all | solution.py:328
  32.4 2.9 %collective-permute-done.1 = s32[2,2,12]{0,2,1:T(8,128)S(1)} collective-permute-done((s32[2,2,12]{0,2,1:T(8,128)S(1)}, s32[2,2,12]{0,2,1:T(8,128)S(1)}, u32[]{:S(2)}, u32[]{:S(2)}) %collective-permute-start.1) | collective-permute-done | bytes 224 | tf_op jit(solution)/shard_map/ppermute | solution.py:333
  36.2 3.0 %collective-permute-done.2 = s32[4,2,12]{0,2,1:T(8,128)S(1)} collective-permute-done((s32[4,2,12]{0,2,1:T(8,128)S(1)}, s32[4,2,12]{0,2,1:T(8,128)S(1)}, u32[]{:S(2)}, u32[]{:S(2)}) %collective-permute-start.2) | collective-permute-done | bytes 416 | tf_op jit(solution)/shard_map/ppermute | solution.py:333
  39.3 4.7 %collective-permute-start.3 = (s32[8,2,12]{0,2,1:T(8,128)S(1)}, s32[8,2,12]{0,2,1:T(8,128)S(1)}, u32[]{:S(2)}, u32[]{:S(2)}) collective-permute-start(s32[8,2,12]{0,2,1:T(8,128)S(1)} %add_select_fusion.1), channel_id=1, source_target_pairs={{0,32},{4,36},{8,40},{12,44},{16,48},{20,52},{24,56},{28,60},{32,0... | collective-permute-start | bytes 2312 | tf_op jit(solution)/shard_map/ppermute | solution.py:333
  44.0 1.8 collective-permute-done.3
  45.8 3.2 %collective-permute-start.12 = (bf16[384,256]{1,0:T(8,128)(2,1)S(1)}, bf16[384,256]{1,0:T(8,128)(2,1)S(1)}, u32[]{:S(2)}, u32[]{:S(2)}) collective-permute-start(bf16[384,256]{1,0:T(8,128)(2,1)S(1)} %copy-done.3), channel_id=1, source_target_pairs={{0,4},{4,0},{8,12},{12,8},{16,20},{20,16},{24,28},{28,24},{32,36},... | collective-permute-start | bytes 589832 | tf_op jit(solution)/shard_map/ppermute | solution.py:356
  49.8 3.0 %collective-permute-start.11 = (bf16[192,256]{1,0:T(8,128)(2,1)S(1)}, bf16[192,256]{1,0:T(8,128)(2,1)}, u32[]{:S(2)}, u32[]{:S(2)}) collective-permute-start(bf16[192,256]{1,0:T(8,128)(2,1)S(1)} %slice.49), channel_id=1, source_target_pairs={{0,48},{4,52},{8,56},{12,60},{16,0},{20,4},{24,8},{28,12},{32,16},... | collective-permute-start | bytes 294920 | tf_op jit(solution)/shard_map/ppermute | solution.py:353
  53.0 2.7 %collective-permute-start.9 = (bf16[384,256]{1,0:T(8,128)(2,1)S(1)}, bf16[384,256]{1,0:T(8,128)(2,1)}, u32[]{:S(2)}, u32[]{:S(2)}) collective-permute-start(bf16[384,256]{1,0:T(8,128)(2,1)S(1)} %collective-permute-done.7.rest_4_), channel_id=1, source_target_pairs={{0,56},{4,60},{8,0},{12,4},{16,8},{20,12},{24,16},{28,20},{32,24},... | collective-permute-start | bytes 589832 | tf_op jit(solution)/shard_map/ppermute | solution.py:353
  57.4 2.7 %collective-permute-done.10.rest_7_ = bf16[192,256]{1,0:T(8,128)(2,1)} collective-permute-done((bf16[192,256]{1,0:T(8,128)(2,1)S(1)}, bf16[192,256]{1,0:T(8,128)(2,1)}, u32[]{:S(2)}, u32[]{:S(2)}) %collective-permute-start.10) | collective-permute-done | bytes 98336 | tf_op jit(solution)/shard_map/ppermute | solution.py:353
  61.9 4.7 %collective-permute-done.8.rest_5_ = bf16[384,256]{1,0:T(8,128)(2,1)} collective-permute-done((bf16[384,256]{1,0:T(8,128)(2,1)S(1)}, bf16[384,256]{1,0:T(8,128)(2,1)}, u32[]{:S(2)}, u32[]{:S(2)}) %collective-permute-start.8) | collective-permute-done | bytes 196640 | tf_op jit(solution)/shard_map/ppermute | solution.py:353
  71.3 11.3 %shard_map.77 = (bf16[16,144,256]{2,1,0:T(8,128)(2,1)}, bf16[6144,256]{1,0:T(8,128)(2,1)}) custom-call(s32[32]{0:T(128)S(1)} %reshape.141.slots, bf16[2,6,128,256]{3,2,1,0:T(8,128)(2,1)S(1)} %copy-done.2, bf16[384,256]{1,0:T(8,128)(2,1)S(1)} %copy-done.3, bf16[384,256]{1,0:T(8,128)(2,1)} %collective-permute-done.4.rest_1_, ...), custom_call_target="tpu_custom_call" | custom-call | flops 8000000000 | bytes 8388608 | tf_op jit(solution)/shard_map/pallas_call | solution.py:367
  82.6 7.1 %all-to-all-start = ((bf16[16,144,256]{2,1,0:T(8,128)(2,1)}), bf16[16,144,256]{2,1,0:T(8,128)(2,1)S(1)}, u32[]{:S(2)}, u32[]{:S(2)}) async-start(bf16[16,144,256]{2,1,0:T(8,128)(2,1)} %get-tuple-element.10), calls=%async_computation | async-start | bytes 2359296 | tf_op jit(solution)/shard_map/all_to_all | solution.py:379
  90.4 2.0 %collective-permute-start.21 = (bf16[64,256]{1,0:T(8,128)(2,1)}, bf16[64,256]{1,0:T(8,128)(2,1)S(1)}, u32[]{:S(2)}, u32[]{:S(2)}) collective-permute-start(bf16[64,256]{1,0:T(8,128)(2,1)} %slice.39), channel_id=1, source_target_pairs={{4,0},{8,4},{12,8},{16,12},{20,16},{24,20},{28,24},{32,28},{36,32}... | collective-permute-start | bytes 98312 | tf_op jit(solution)/shard_map/ppermute | solution.py:364
  92.7 25.6 %collective-permute-done.21.next_block = bf16[64,256]{1,0:T(8,128)(2,1)S(1)} collective-permute-done((bf16[64,256]{1,0:T(8,128)(2,1)}, bf16[64,256]{1,0:T(8,128)(2,1)S(1)}, u32[]{:S(2)}, u32[]{:S(2)}) %collective-permute-start.21) | collective-permute-done | bytes 32800 | tf_op jit(solution)/shard_map/ppermute | solution.py:364
  118.3 2.1 %all-to-all-done.arrived = bf16[16,144,256]{2,1,0:T(8,128)(2,1)S(1)} async-done(((bf16[16,144,256]{2,1,0:T(8,128)(2,1)}), bf16[16,144,256]{2,1,0:T(8,128)(2,1)S(1)}, u32[]{:S(2)}, u32[]{:S(2)}) %all-to-all-start) | async-done | bytes 1179680 | tf_op jit(solution)/shard_map/all_to_all | solution.py:379
  120.3 2.2 %shard_map.79 = (bf16[192,256]{1,0:T(8,128)(2,1)S(1)}, bf16[192,256]{1,0:T(8,128)(2,1)S(1)}, bf16[64,256]{1,0:T(8,128)(2,1)S(1)}, f32[6,4,128]{2,1,0:T(4,128)S(1)}) custom-call(s32[12]{0:T(128)S(1)} %fusion.5.requests, bf16[16,144,256]{2,1,0:T(8,128)(2,1)S(1)} %all-to-all-done.arrived, bf16[384,256]{1,0:T(8,128)(2,1)S(1)} %copy-done, ...), custom_call_target="tpu_custom_call" | custom-call | flops 2000000000 | bytes 8388608 | tf_op jit(solution)/shard_map/pallas_call | solution.py:380
  122.5 1.9 %collective-permute-start.22 = (bf16[64,256]{1,0:T(8,128)(2,1)S(1)}, bf16[64,256]{1,0:T(8,128)(2,1)S(1)}, u32[]{:S(2)}, u32[]{:S(2)}) collective-permute-start(bf16[64,256]{1,0:T(8,128)(2,1)S(1)} %get-tuple-element.12), channel_id=1, source_target_pairs={{0,4},{4,8},{8,12},{12,16},{16,20},{20,24},{24,28},{28,32},{32,36}... | collective-permute-start | bytes 98312 | tf_op jit(solution)/shard_map/ppermute | solution.py:395
  125.1 1.9 %collective-permute-start.30 = (bf16[192,256]{1,0:T(8,128)(2,1)S(1)}, bf16[192,256]{1,0:T(8,128)(2,1)S(1)}, u32[]{:S(2)}, u32[]{:S(2)}) collective-permute-start(bf16[192,256]{1,0:T(8,128)(2,1)S(1)} %get-tuple-element.13), channel_id=1, source_target_pairs={{0,1},{1,2},{2,3},{3,0},{4,5},{5,6},{6,7},{7,4},{8,9},{9,10},{10,1... | collective-permute-start | bytes 294920 | tf_op jit(solution)/shard_map/ppermute | solution.py:257
  127.0 2.4 %collective-permute-start.31 = (bf16[192,256]{1,0:T(8,128)(2,1)S(1)}, bf16[192,256]{1,0:T(8,128)(2,1)S(1)}, u32[]{:S(2)}, u32[]{:S(2)}) collective-permute-start(bf16[192,256]{1,0:T(8,128)(2,1)S(1)} %get-tuple-element.13), channel_id=1, source_target_pairs={{0,2},{1,3},{2,0},{3,1},{4,6},{5,7},{6,4},{7,5},{8,10},{9,11},{10,... | collective-permute-start | bytes 294920 | tf_op jit(solution)/shard_map/ppermute | solution.py:257
  131.8 2.5 %collective-permute-start.24 = (bf16[192,256]{1,0:T(8,128)(2,1)S(1)}, bf16[192,256]{1,0:T(8,128)(2,1)S(1)}, u32[]{:S(2)}, u32[]{:S(2)}) collective-permute-start(bf16[192,256]{1,0:T(8,128)(2,1)S(1)} %pad_maximum_fusion.1), channel_id=1, source_target_pairs={{0,128},{64,192},{128,0},{192,64},{1,129},{65,193},{129,1},{193,65... | collective-permute-start | bytes 294920 | tf_op jit(solution)/shard_map/ppermute | solution.py:257
  137.8 2.5 %collective-permute-start.35 = (bf16[192,1024]{1,0:T(8,128)(2,1)}, bf16[192,1024]{1,0:T(8,128)(2,1)S(1)}, u32[]{:S(2)}, u32[]{:S(2)}) collective-permute-start(bf16[192,1024]{1,0:T(8,128)(2,1)} %constant_dynamic-update-slice_fusion.refs_3_), channel_id=1, source_target_pairs={{0,192},{64,0},{128,64},{192,128},{1,193},{65,1},{129,65},{193,129... | collective-permute-start | bytes 1179656 | tf_op jit(solution)/shard_map/ppermute | solution.py:257
  140.6 2.5 %collective-permute-start.28 = (bf16[192,1024]{1,0:T(8,128)(2,1)S(1)}, bf16[192,1024]{1,0:T(8,128)(2,1)}, u32[]{:S(2)}, u32[]{:S(2)}) collective-permute-start(bf16[192,1024]{1,0:T(8,128)(2,1)S(1)} %pad_maximum_fusion.refs_0_), channel_id=1, source_target_pairs={{0,3},{1,0},{2,1},{3,2},{4,7},{5,4},{6,5},{7,6},{8,11},{9,8},{10,9... | collective-permute-start | bytes 1179656 | tf_op jit(solution)/shard_map/ppermute | solution.py:257
  143.8 7.1 %all-to-all-start.2 = ((f32[16,6,4,128]{3,2,1,0:T(4,128)}), f32[16,6,4,128]{3,2,1,0:T(4,128)}, u32[]{:S(2)}, u32[]{:S(2)}) async-start(f32[16,6,4,128]{3,2,1,0:T(4,128)} %broadcast_in_dim.22), calls=%async_computation.2 | async-start | bytes 393216 | tf_op jit(solution)/shard_map/all_to_all | solution.py:403
  152.3 2.7 %collective-permute-start.36 = (bf16[192,512]{1,0:T(8,128)(2,1)}, bf16[192,512]{1,0:T(8,128)(2,1)}, u32[]{:S(2)}, u32[]{:S(2)}) collective-permute-start(bf16[192,512]{1,0:T(8,128)(2,1)} %slice.53), channel_id=1, source_target_pairs={{0,192},{64,0},{128,64},{192,128},{1,193},{65,1},{129,65},{193,129... | collective-permute-start | bytes 589832 | tf_op jit(solution)/shard_map/ppermute | solution.py:257
  158.2 2.7 %collective-permute-start.29 = (bf16[192,512]{1,0:T(8,128)(2,1)}, bf16[192,512]{1,0:T(8,128)(2,1)}, u32[]{:S(2)}, u32[]{:S(2)}) collective-permute-start(bf16[192,512]{1,0:T(8,128)(2,1)} %slice.51), channel_id=1, source_target_pairs={{0,3},{1,0},{2,1},{3,2},{4,7},{5,4},{6,5},{7,6},{8,11},{9,8},{10,9... | collective-permute-start | bytes 589832 | tf_op jit(solution)/shard_map/ppermute | solution.py:257
  161.3 11.9 %shard_map.80 = (bf16[2,6,128,256]{3,2,1,0:T(8,128)(2,1)}, f32[8,128]{1,0:T(8,128)}) custom-call(s32[32]{0:T(128)} %copy-done.1, bf16[6144,256]{1,0:T(8,128)(2,1)} %get-tuple-element.14.queries, bf16[6144,256]{1,0:T(8,128)(2,1)} %all-gather.2.cloned.1.call-done.cotangents, bf16[2,6,128,256]{3,2,1,0:T(8,128)(2,1)} %states.3, f32[96,4,128]{2,1,0:T(4,128)} %bitcast.8.stats), custom_call_target="tpu_custom_call" | custom-call | flops 10000000000 | bytes 8388608 | tf_op jit(solution)/shard_map/pallas_call | solution.py:406
  173.9 3.4 %shard_map.81.refs_6_ = f32[2,384,256]{2,1,0:T(8,128)S(1)} custom-call(bf16[192,1024]{1,0:T(8,128)(2,1)S(1)} %pad_maximum_fusion.refs_0_, bf16[192,1024]{1,0:T(8,128)(2,1)} %collective-permute-done.26.refs_1_, bf16[192,1024]{1,0:T(8,128)(2,1)} %collective-permute-done.28.refs_2_, bf16[192,1024]{1,0:T(8,128)(2,1)} %constant_dynamic-update-slice_fusion.refs_3_, ...), custom_call_target="tpu_custom_call" | custom-call | flops 3000000000 | bytes 8388608 | tf_op jit(solution)/shard_map/pallas_call | solution.py:422
  177.3 3.2 %shard_map.82 = bf16[384,512]{1,0:T(8,128)(2,1)} custom-call(bf16[192,512]{1,0:T(8,128)(2,1)} %collective-permute-done.27.refs_0_, bf16[192,512]{1,0:T(8,128)(2,1)} %collective-permute-done.29.refs_1_, bf16[192,512]{1,0:T(8,128)(2,1)S(1)} %collective-permute-done.34.refs_2_, bf16[192,512]{1,0:T(8,128)(2,1)} %collective-permute-done.36.refs_3_, ...), custom_call_target="tpu_custom_call" | custom-call | flops 2000000000 | bytes 8388608 | tf_op jit(solution)/shard_map/pallas_call | solution.py:430
  (115 shorter events, 29.4 us)
Async XLA Ops:
  7.2 41.9 %collective-permute-start.6 = (bf16[384,256]{1,0:T(8,128)(2,1)}, bf16[384,256]{1,0:T(8,128)(2,1)S(1)}, u32[]{:S(2)}, u32[]{:S(2)}) collective-permute-start(bf16[384,256]{1,0:T(8,128)(2,1)} %rest_0_.1), channel_id=1, source_target_pairs={{0,16},{4,20},{8,24},{12,28},{16,32},{20,36},{24,40},{28,44},{32,4... | collective-permute-start | bytes 589832 | tf_op jit(solution)/shard_map/ppermute | solution.py:353
  11.1 38.7 %collective-permute-start.7 = (bf16[384,256]{1,0:T(8,128)(2,1)}, bf16[384,256]{1,0:T(8,128)(2,1)S(1)}, u32[]{:S(2)}, u32[]{:S(2)}) collective-permute-start(bf16[384,256]{1,0:T(8,128)(2,1)} %rest_0_.1), channel_id=1, source_target_pairs={{0,48},{4,52},{8,56},{12,60},{16,0},{20,4},{24,8},{28,12},{32,16},... | collective-permute-start | bytes 589832 | tf_op jit(solution)/shard_map/ppermute | solution.py:353
  14.2 38.7 %collective-permute-start.4 = (bf16[384,256]{1,0:T(8,128)(2,1)}, bf16[384,256]{1,0:T(8,128)(2,1)}, u32[]{:S(2)}, u32[]{:S(2)}) collective-permute-start(bf16[384,256]{1,0:T(8,128)(2,1)} %rest_0_.1), channel_id=1, source_target_pairs={{0,8},{4,12},{8,16},{12,20},{16,24},{20,28},{24,32},{28,36},{32,40... | collective-permute-start | bytes 589832 | tf_op jit(solution)/shard_map/ppermute | solution.py:353
  14.9 38.0 %collective-permute-start.5 = (bf16[384,256]{1,0:T(8,128)(2,1)}, bf16[384,256]{1,0:T(8,128)(2,1)}, u32[]{:S(2)}, u32[]{:S(2)}) collective-permute-start(bf16[384,256]{1,0:T(8,128)(2,1)} %rest_0_.1), channel_id=1, source_target_pairs={{0,56},{4,60},{8,0},{12,4},{16,8},{20,12},{24,16},{28,20},{32,24},... | collective-permute-start | bytes 589832 | tf_op jit(solution)/shard_map/ppermute | solution.py:353
  18.6 13.6 %collective-permute-start = (s32[1,2,12]{2,1,0:T(2,128)S(1)}, s32[1,2,12]{2,1,0:T(2,128)S(1)}, u32[]{:S(2)}, u32[]{:S(2)}) collective-permute-start(s32[1,2,12]{2,1,0:T(2,128)S(1)} %add_bitcast_fusion), channel_id=1, source_target_pairs={{0,4},{4,0},{8,12},{12,8},{16,20},{20,16},{24,28},{28,24},{32,36},... | collective-permute-start | bytes 296 | tf_op jit(solution)/shard_map/ppermute | solution.py:333
  24.5 58.1 %all-to-all-start.1 = ((bf16[16,256,256]{2,1,0:T(8,128)(2,1)}), bf16[16,256,256]{2,1,0:T(8,128)(2,1)S(1)}, u32[]{:S(2)}, u32[]{:S(2)}) async-start(bf16[16,256,256]{2,1,0:T(8,128)(2,1)} %shard_map.78), calls=%async_computation.1 | async-start | bytes 4194304 | tf_op jit(solution)/shard_map/all_to_all | solution.py:328
  31.4 130.0 %all-gather.2.cloned.1.call-start = ((), (), s32[]{:S(2)}) async-start(), calls=%async_computation.3 | async-start | bytes 3342336 | tf_op jit(solution)/shard_map/all_gather | solution.py:365
  45.8 9.8 %collective-permute-start.12 = (bf16[384,256]{1,0:T(8,128)(2,1)S(1)}, bf16[384,256]{1,0:T(8,128)(2,1)S(1)}, u32[]{:S(2)}, u32[]{:S(2)}) collective-permute-start(bf16[384,256]{1,0:T(8,128)(2,1)S(1)} %copy-done.3), channel_id=1, source_target_pairs={{0,4},{4,0},{8,12},{12,8},{16,20},{20,16},{24,28},{28,24},{32,36},... | collective-permute-start | bytes 589832 | tf_op jit(solution)/shard_map/ppermute | solution.py:356
  49.1 11.1 %collective-permute-start.10 = (bf16[192,256]{1,0:T(8,128)(2,1)S(1)}, bf16[192,256]{1,0:T(8,128)(2,1)}, u32[]{:S(2)}, u32[]{:S(2)}) collective-permute-start(bf16[192,256]{1,0:T(8,128)(2,1)S(1)} %slice.48), channel_id=1, source_target_pairs={{0,16},{4,20},{8,24},{12,28},{16,32},{20,36},{24,40},{28,44},{32,4... | collective-permute-start | bytes 294920 | tf_op jit(solution)/shard_map/ppermute | solution.py:353
  49.8 10.9 %collective-permute-start.11 = (bf16[192,256]{1,0:T(8,128)(2,1)S(1)}, bf16[192,256]{1,0:T(8,128)(2,1)}, u32[]{:S(2)}, u32[]{:S(2)}) collective-permute-start(bf16[192,256]{1,0:T(8,128)(2,1)S(1)} %slice.49), channel_id=1, source_target_pairs={{0,48},{4,52},{8,56},{12,60},{16,0},{20,4},{24,8},{28,12},{32,16},... | collective-permute-start | bytes 294920 | tf_op jit(solution)/shard_map/ppermute | solution.py:353
  52.9 13.7 %collective-permute-start.8 = (bf16[384,256]{1,0:T(8,128)(2,1)S(1)}, bf16[384,256]{1,0:T(8,128)(2,1)}, u32[]{:S(2)}, u32[]{:S(2)}) collective-permute-start(bf16[384,256]{1,0:T(8,128)(2,1)S(1)} %collective-permute-done.6.rest_3_), channel_id=1, source_target_pairs={{0,8},{4,12},{8,16},{12,20},{16,24},{20,28},{24,32},{28,36},{32,40... | collective-permute-start | bytes 589832 | tf_op jit(solution)/shard_map/ppermute | solution.py:353
  53.0 14.6 %collective-permute-start.9 = (bf16[384,256]{1,0:T(8,128)(2,1)S(1)}, bf16[384,256]{1,0:T(8,128)(2,1)}, u32[]{:S(2)}, u32[]{:S(2)}) collective-permute-start(bf16[384,256]{1,0:T(8,128)(2,1)S(1)} %collective-permute-done.7.rest_4_), channel_id=1, source_target_pairs={{0,56},{4,60},{8,0},{12,4},{16,8},{20,12},{24,16},{28,20},{32,24},... | collective-permute-start | bytes 589832 | tf_op jit(solution)/shard_map/ppermute | solution.py:353
  56.3 11.8 %collective-permute-start.15 = (bf16[384,256]{1,0:T(8,128)(2,1)S(1)}, bf16[384,256]{1,0:T(8,128)(2,1)}, u32[]{:S(2)}, u32[]{:S(2)}) collective-permute-start(bf16[384,256]{1,0:T(8,128)(2,1)S(1)} %collective-permute-done.6.rest_3_), channel_id=1, source_target_pairs={{0,4},{4,0},{8,12},{12,8},{16,20},{20,16},{24,28},{28,24},{32,36},... | collective-permute-start | bytes 589832 | tf_op jit(solution)/shard_map/ppermute | solution.py:356
  60.2 7.4 %collective-permute-start.19 = (bf16[192,256]{1,0:T(8,128)(2,1)}, bf16[192,256]{1,0:T(8,128)(2,1)}, u32[]{:S(2)}, u32[]{:S(2)}) collective-permute-start(bf16[192,256]{1,0:T(8,128)(2,1)} %collective-permute-done.10.rest_7_), channel_id=1, source_target_pairs={{0,4},{4,0},{8,12},{12,8},{16,20},{20,16},{24,28},{28,24},{32,36},... | collective-permute-start | bytes 294920 | tf_op jit(solution)/shard_map/ppermute | solution.py:356
  60.8 7.3 %collective-permute-start.20 = (bf16[192,256]{1,0:T(8,128)(2,1)}, bf16[192,256]{1,0:T(8,128)(2,1)}, u32[]{:S(2)}, u32[]{:S(2)}) collective-permute-start(bf16[192,256]{1,0:T(8,128)(2,1)} %collective-permute-done.11.rest_8_), channel_id=1, source_target_pairs={{0,4},{4,0},{8,12},{12,8},{16,20},{20,16},{24,28},{28,24},{32,36},... | collective-permute-start | bytes 294920 | tf_op jit(solution)/shard_map/ppermute | solution.py:356
  82.6 37.7 %all-to-all-start = ((bf16[16,144,256]{2,1,0:T(8,128)(2,1)}), bf16[16,144,256]{2,1,0:T(8,128)(2,1)S(1)}, u32[]{:S(2)}, u32[]{:S(2)}) async-start(bf16[16,144,256]{2,1,0:T(8,128)(2,1)} %get-tuple-element.10), calls=%async_computation | async-start | bytes 2359296 | tf_op jit(solution)/shard_map/all_to_all | solution.py:379
  90.4 27.9 %collective-permute-start.21 = (bf16[64,256]{1,0:T(8,128)(2,1)}, bf16[64,256]{1,0:T(8,128)(2,1)S(1)}, u32[]{:S(2)}, u32[]{:S(2)}) collective-permute-start(bf16[64,256]{1,0:T(8,128)(2,1)} %slice.39), channel_id=1, source_target_pairs={{4,0},{8,4},{12,8},{16,12},{20,16},{24,20},{28,24},{32,28},{36,32}... | collective-permute-start | bytes 98312 | tf_op jit(solution)/shard_map/ppermute | solution.py:364
  92.6 80.6 %collective-permute-start.37 = (bf16[16,256,256]{2,1,0:T(8,128)(2,1)S(1)}, bf16[16,256,256]{2,1,0:T(8,128)(2,1)}, u32[]{:S(2)}, u32[]{:S(2)}) collective-permute-start(bf16[16,256,256]{2,1,0:T(8,128)(2,1)S(1)} %all-to-all-done.1.rest_0_.refs_6_.refs_4_), channel_id=1, source_target_pairs={{0,4},{4,0},{8,12},{12,8},{16,20},{20,16},{24,28},{28,24},{32,36},... | collective-permute-start | bytes 6291464 | tf_op jit(solution)/shard_map/ppermute | solution.py:356
  122.5 8.1 %collective-permute-start.22 = (bf16[64,256]{1,0:T(8,128)(2,1)S(1)}, bf16[64,256]{1,0:T(8,128)(2,1)S(1)}, u32[]{:S(2)}, u32[]{:S(2)}) collective-permute-start(bf16[64,256]{1,0:T(8,128)(2,1)S(1)} %get-tuple-element.12), channel_id=1, source_target_pairs={{0,4},{4,8},{8,12},{12,16},{16,20},{20,24},{24,28},{28,32},{32,36}... | collective-permute-start | bytes 98312 | tf_op jit(solution)/shard_map/ppermute | solution.py:395
  127.0 8.0 %collective-permute-start.31 = (bf16[192,256]{1,0:T(8,128)(2,1)S(1)}, bf16[192,256]{1,0:T(8,128)(2,1)S(1)}, u32[]{:S(2)}, u32[]{:S(2)}) collective-permute-start(bf16[192,256]{1,0:T(8,128)(2,1)S(1)} %get-tuple-element.13), channel_id=1, source_target_pairs={{0,2},{1,3},{2,0},{3,1},{4,6},{5,7},{6,4},{7,5},{8,10},{9,11},{10,... | collective-permute-start | bytes 294920 | tf_op jit(solution)/shard_map/ppermute | solution.py:257
  129.4 7.6 %collective-permute-start.32 = (bf16[192,256]{1,0:T(8,128)(2,1)S(1)}, bf16[192,256]{1,0:T(8,128)(2,1)S(1)}, u32[]{:S(2)}, u32[]{:S(2)}) collective-permute-start(bf16[192,256]{1,0:T(8,128)(2,1)S(1)} %get-tuple-element.13), channel_id=1, source_target_pairs={{0,3},{1,0},{2,1},{3,2},{4,7},{5,4},{6,5},{7,6},{8,11},{9,8},{10,9... | collective-permute-start | bytes 294920 | tf_op jit(solution)/shard_map/ppermute | solution.py:257
  130.7 7.1 %collective-permute-start.23 = (bf16[192,256]{1,0:T(8,128)(2,1)S(1)}, bf16[192,256]{1,0:T(8,128)(2,1)S(1)}, u32[]{:S(2)}, u32[]{:S(2)}) collective-permute-start(bf16[192,256]{1,0:T(8,128)(2,1)S(1)} %pad_maximum_fusion.1), channel_id=1, source_target_pairs={{0,64},{64,128},{128,192},{192,0},{1,65},{65,129},{129,193},{193,1... | collective-permute-start | bytes 294920 | tf_op jit(solution)/shard_map/ppermute | solution.py:257
  131.8 8.4 %collective-permute-start.24 = (bf16[192,256]{1,0:T(8,128)(2,1)S(1)}, bf16[192,256]{1,0:T(8,128)(2,1)S(1)}, u32[]{:S(2)}, u32[]{:S(2)}) collective-permute-start(bf16[192,256]{1,0:T(8,128)(2,1)S(1)} %pad_maximum_fusion.1), channel_id=1, source_target_pairs={{0,128},{64,192},{128,0},{192,64},{1,129},{65,193},{129,1},{193,65... | collective-permute-start | bytes 294920 | tf_op jit(solution)/shard_map/ppermute | solution.py:257
  137.6 13.3 %collective-permute-start.33 = (bf16[192,1024]{1,0:T(8,128)(2,1)}, bf16[192,1024]{1,0:T(8,128)(2,1)S(1)}, u32[]{:S(2)}, u32[]{:S(2)}) collective-permute-start(bf16[192,1024]{1,0:T(8,128)(2,1)} %constant_dynamic-update-slice_fusion.refs_3_), channel_id=1, source_target_pairs={{0,64},{64,128},{128,192},{192,0},{1,65},{65,129},{129,193},{193,1... | collective-permute-start | bytes 1179656 | tf_op jit(solution)/shard_map/ppermute | solution.py:257
  137.8 13.8 %collective-permute-start.35 = (bf16[192,1024]{1,0:T(8,128)(2,1)}, bf16[192,1024]{1,0:T(8,128)(2,1)S(1)}, u32[]{:S(2)}, u32[]{:S(2)}) collective-permute-start(bf16[192,1024]{1,0:T(8,128)(2,1)} %constant_dynamic-update-slice_fusion.refs_3_), channel_id=1, source_target_pairs={{0,192},{64,0},{128,64},{192,128},{1,193},{65,1},{129,65},{193,129... | collective-permute-start | bytes 1179656 | tf_op jit(solution)/shard_map/ppermute | solution.py:257
  140.3 14.6 %collective-permute-start.26 = (bf16[192,1024]{1,0:T(8,128)(2,1)S(1)}, bf16[192,1024]{1,0:T(8,128)(2,1)}, u32[]{:S(2)}, u32[]{:S(2)}) collective-permute-start(bf16[192,1024]{1,0:T(8,128)(2,1)S(1)} %pad_maximum_fusion.refs_0_), channel_id=1, source_target_pairs={{0,1},{1,2},{2,3},{3,0},{4,5},{5,6},{6,7},{7,4},{8,9},{9,10},{10,1... | collective-permute-start | bytes 1179656 | tf_op jit(solution)/shard_map/ppermute | solution.py:257
  140.6 16.0 %collective-permute-start.28 = (bf16[192,1024]{1,0:T(8,128)(2,1)S(1)}, bf16[192,1024]{1,0:T(8,128)(2,1)}, u32[]{:S(2)}, u32[]{:S(2)}) collective-permute-start(bf16[192,1024]{1,0:T(8,128)(2,1)S(1)} %pad_maximum_fusion.refs_0_), channel_id=1, source_target_pairs={{0,3},{1,0},{2,1},{3,2},{4,7},{5,4},{6,5},{7,6},{8,11},{9,8},{10,9... | collective-permute-start | bytes 1179656 | tf_op jit(solution)/shard_map/ppermute | solution.py:257
  143.8 17.6 %all-to-all-start.2 = ((f32[16,6,4,128]{3,2,1,0:T(4,128)}), f32[16,6,4,128]{3,2,1,0:T(4,128)}, u32[]{:S(2)}, u32[]{:S(2)}) async-start(f32[16,6,4,128]{3,2,1,0:T(4,128)} %broadcast_in_dim.22), calls=%async_computation.2 | async-start | bytes 393216 | tf_op jit(solution)/shard_map/all_to_all | solution.py:403
  151.6 25.7 %collective-permute-start.34 = (bf16[192,512]{1,0:T(8,128)(2,1)}, bf16[192,512]{1,0:T(8,128)(2,1)S(1)}, u32[]{:S(2)}, u32[]{:S(2)}) collective-permute-start(bf16[192,512]{1,0:T(8,128)(2,1)} %slice.52), channel_id=1, source_target_pairs={{0,64},{64,128},{128,192},{192,0},{1,65},{65,129},{129,193},{193,1... | collective-permute-start | bytes 589832 | tf_op jit(solution)/shard_map/ppermute | solution.py:257
  152.3 25.0 %collective-permute-start.36 = (bf16[192,512]{1,0:T(8,128)(2,1)}, bf16[192,512]{1,0:T(8,128)(2,1)}, u32[]{:S(2)}, u32[]{:S(2)}) collective-permute-start(bf16[192,512]{1,0:T(8,128)(2,1)} %slice.53), channel_id=1, source_target_pairs={{0,192},{64,0},{128,64},{192,128},{1,193},{65,1},{129,65},{193,129... | collective-permute-start | bytes 589832 | tf_op jit(solution)/shard_map/ppermute | solution.py:257
  156.6 20.7 %collective-permute-start.27 = (bf16[192,512]{1,0:T(8,128)(2,1)}, bf16[192,512]{1,0:T(8,128)(2,1)}, u32[]{:S(2)}, u32[]{:S(2)}) collective-permute-start(bf16[192,512]{1,0:T(8,128)(2,1)} %slice.50), channel_id=1, source_target_pairs={{0,1},{1,2},{2,3},{3,0},{4,5},{5,6},{6,7},{7,4},{8,9},{9,10},{10,1... | collective-permute-start | bytes 589832 | tf_op jit(solution)/shard_map/ppermute | solution.py:257
  158.2 19.1 %collective-permute-start.29 = (bf16[192,512]{1,0:T(8,128)(2,1)}, bf16[192,512]{1,0:T(8,128)(2,1)}, u32[]{:S(2)}, u32[]{:S(2)}) collective-permute-start(bf16[192,512]{1,0:T(8,128)(2,1)} %slice.51), channel_id=1, source_target_pairs={{0,3},{1,0},{2,1},{3,2},{4,7},{5,4},{6,5},{7,6},{8,11},{9,8},{10,9... | collective-permute-start | bytes 589832 | tf_op jit(solution)/shard_map/ppermute | solution.py:257
  (17 other events, 125.9 us)
Sparse Core Ops, SparseCore 0:
  34.0 46.3 all-gather.1

commit v6 on v4

--- a/solution.py
+++ b/solution.py
@@ -20,9 +20,7 @@
 VMEM = pl.BlockSpec(memory_space=pltpu.VMEM)
 SMEM = pl.BlockSpec(memory_space=pltpu.SMEM)
 ANY = pl.BlockSpec(memory_space=pl.ANY)
-HBM = pl.BlockSpec(memory_space=pltpu.HBM)
 LIMIT = pltpu.CompilerParams(vmem_limit_bytes=48 * 1024 * 1024)
-WIDE = pltpu.CompilerParams(vmem_limit_bytes=60 * 1024 * 1024)
 
 
 def cost(gigaflops):
@@ -61,7 +59,7 @@
     )
 
 
-def span_forward(codes, queries, cotangents, store, spread, stats, held, attention, sems, out_sems):
+def span_forward(codes, queries, cotangents, store, upper, lower, stats, held, sems):
     blocks, width = queries.shape[0] // SPAN, queries.shape[1]
     windows = blocks + 1
     heads = range(0, width, HDIM)
@@ -123,7 +121,8 @@
     rolled = {key: pltpu.roll(jnp.concatenate([value] * 4, 0), SPAN, 1)[:2] for key, value in lines.items()}
     for i in range(blocks):
         mixed = [jnp.concatenate([attended[j, h] for h in range(len(heads))], 1) for j in (i, i + 1)]
-        attention[pl.ds(i * SPAN, SPAN), :] = jnp.where(final_row, mixed[1], mixed[0]).astype(attention.dtype)
+        half, at = (upper, i) if i < blocks // 2 else (lower, i - blocks // 2)
+        half[pl.ds(at * SPAN, SPAN), :] = jnp.where(final_row, mixed[1], mixed[0]).astype(half.dtype)
         rows = []
         for h in range(len(heads)):
             both = []
@@ -132,15 +131,10 @@
                 both.append(jnp.where(early, pair[j % 2], pair[1 - j % 2]))
             rows.append(jnp.where(lane % SPAN == SPAN - 1, both[1], both[0]))
         stats[i] = jnp.concatenate([row[kind : kind + 1] for kind in range(2) for row in rows], 0)
-    copies = [pltpu.make_async_copy(attention, spread.at[i], out_sems.at[i]) for i in range(spread.shape[0])]
-    for copy in copies:
-        copy.start()
-    for copy in copies:
-        copy.wait()
-
-
-def pair_backward(together, slots, rows, states, stats, out, finished, total, windows, sems):
-    finished[...] = jnp.zeros_like(finished)
+
+
+def pair_backward(together, slots, rows, states, stats, *rest):
+    out, total, windows, sems = rest[-4:]
     spans = stats.shape[0]
     reach = SPAN + 16
     copies = []
@@ -213,23 +207,54 @@
         block[i] = columns[:, pl.ds(at, half)]
 
 
-def project(core, blocks, mine, other, earlier, out, total):
-    columns = mine.shape[2]
-    step = pl.program_id(0)
-
-    @pl.when(step == 0)
-    def _():
-        total[...] = jnp.zeros_like(total)
-
-    for source in range(blocks.shape[0]):
-        total[:, :columns] += dot(blocks[source], mine[source], NN)
-        total[:, columns:] += dot(blocks[source], other[source], NN)
-
-    @pl.when(step == pl.num_programs(0) - 1)
-    def _():
-        for weight, at in ((0, core[0]), (1, 1 - core[0])):
-            part = total[:, weight * columns : (weight + 1) * columns]
-            out[:, pl.ds(pl.multiple_of(at * columns, 128), columns)] = part.astype(out.dtype)
+def shifted(value, axis, steps):
+    count = lax.axis_size(axis)
+    return lax.ppermute(value, axis, [(source, (source + steps) % count) for source in range(count)])
+
+
+def halves_round(first, second, axis):
+    half = first.shape[1] // 2
+    return [shifted(first[:, :half], axis, 1), shifted(second[:, half:], axis, lax.axis_size(axis) - 1)]
+
+
+def source_of(steps_grp, steps_tp):
+    grps, tps = lax.axis_size("grp"), lax.axis_size("tp")
+    grp = lax.rem(lax.axis_index("grp") + (grps - steps_grp) % grps, grps)
+    return grp * tps + lax.rem(lax.axis_index("tp") + (tps - steps_tp) % tps, tps)
+
+
+def project_near(*refs):
+    blocks, weights, out = refs[:6], refs[6:8], refs[-1]
+    side = lax.axis_size("tp")
+    rows, width = blocks[0].shape[0], weights[0].shape[1]
+    for half in range(2):
+        for kind, weight in enumerate(weights):
+            total = None
+            for block, step in zip(blocks[half * 3 : half * 3 + 3], (0, 1, side - 1)):
+                for inner in range(side):
+                    source = source_of(inner, step) if half == 0 else source_of(step, inner)
+                    term = dot(block[:, inner * width : (inner + 1) * width], weight[source], NN)
+                    total = term if total is None else total + term
+            out[kind, pl.ds(half * rows, rows), :] = total
+
+
+def project_far(*refs):
+    blocks, weights, partial, out = refs[:4], refs[4:6], refs[6], refs[7]
+    side = lax.axis_size("tp")
+    rows, width = blocks[0].shape[0], weights[0].shape[1]
+    columns = weights[0].shape[2]
+    core = lax.rem(lax.axis_index("seq"), 2)
+    for half in range(2):
+        for kind, weight in enumerate(weights):
+            total = partial[kind, pl.ds(half * rows, rows), :]
+            for inner in range(side):
+                block = blocks[half * 2 + inner // (side // 2)]
+                at = inner % (side // 2) * width
+                far = side // 2
+                source = source_of(inner, far) if half == 0 else source_of(far, inner)
+                total = total + dot(block[:, at : at + width], weight[source], NN)
+            at = pl.multiple_of((core if kind == 0 else 1 - core) * columns, 128)
+            out[pl.ds(half * rows, rows), pl.ds(at, columns)] = total.astype(out.dtype)
 
 
 def local(queries, neighbour_states, retrieved, valid_blocks, output_weight, attention_cotangent):
@@ -281,60 +306,62 @@
     gathered = lax.all_gather(both, "seq", axis=0, tiled=True)
     weight_other = lax.ppermute(weight, "seq", [(source, source ^ 1) for source in range(owners)])
 
-    spread, stats = pl.pallas_call(
+    middle = tok_rows // 2
+    upper, lower, stats = pl.pallas_call(
         span_forward,
         cost_estimate=cost(5),
         out_shape=(
-            jax.ShapeDtypeStruct((grps * tps, tok_rows, width), jnp.bfloat16),
+            jax.ShapeDtypeStruct((middle, width), jnp.bfloat16),
+            jax.ShapeDtypeStruct((middle, width), jnp.bfloat16),
             jax.ShapeDtypeStruct((span_count, 2 * width // HDIM, 2 * SPAN), jnp.float32),
         ),
         in_specs=[SMEM, VMEM, VMEM, ANY],
-        out_specs=(HBM, VMEM),
+        out_specs=(VMEM, VMEM, VMEM),
         scratch_shapes=[
             pltpu.VMEM((request_count + KNB, 2, NTOK, width), jnp.bfloat16),
-            pltpu.VMEM((tok_rows, width), jnp.bfloat16),
             pltpu.SemaphoreType.DMA((request_count + KNB,)),
-            pltpu.SemaphoreType.DMA((grps * tps,)),
         ],
-        compiler_params=WIDE,
+        compiler_params=LIMIT,
     )(codes, queries, attention_cotangent, store)
 
-    heads = lax.all_to_all(spread, FEATS, split_axis=0, concat_axis=0, tiled=True)
-    all_stats = lax.all_gather(stats, "seq", axis=0, tiled=True)
-    neighbour_gradient, finished = pl.pallas_call(
+    lower = jnp.concatenate([lower] + [shifted(lower, "tp", i) for i in range(1, tps)], 1)
+    upper = jnp.concatenate([upper] + [shifted(upper, "grp", i) for i in range(1, grps)], 1)
+    upper = [upper, shifted(upper, "tp", 1), shifted(upper, "tp", tps - 1)]
+    lower = [lower, shifted(lower, "grp", 1), shifted(lower, "grp", grps - 1)]
+    far = halves_round(upper[1], upper[2], "tp") + halves_round(lower[1], lower[2], "grp")
+    total = pl.pallas_call(
+        project_near,
+        cost_estimate=cost(3),
+        out_shape=jax.ShapeDtypeStruct((2, tok_rows, half), jnp.float32),
+        in_specs=[VMEM] * 8,
+        out_specs=VMEM,
+        compiler_params=LIMIT,
+    )(*upper, *lower, weight, weight_other)
+    layer_output = pl.pallas_call(
+        project_far,
+        cost_estimate=cost(2),
+        out_shape=jax.ShapeDtypeStruct((tok_rows, out_columns), jnp.bfloat16),
+        in_specs=[VMEM] * 7,
+        out_specs=VMEM,
+        compiler_params=LIMIT,
+    )(*far, weight, weight_other, total)
+
+    all_stats = lax.all_to_all(
+        jnp.broadcast_to(stats[None], (owners, *stats.shape)), "seq", split_axis=0, concat_axis=0, tiled=True
+    ).reshape(owners * span_count, *stats.shape[1:])
+    neighbour_gradient = pl.pallas_call(
         functools.partial(pair_backward, 4),
         cost_estimate=cost(10),
-        out_shape=(
-            jax.ShapeDtypeStruct(neighbour_states.shape, jnp.bfloat16),
-            jax.ShapeDtypeStruct((8, HDIM), jnp.float32),
-        ),
-        in_specs=[SMEM, ANY, VMEM, VMEM],
-        out_specs=(VMEM, VMEM),
+        out_shape=jax.ShapeDtypeStruct(neighbour_states.shape, jnp.bfloat16),
+        in_specs=[SMEM, ANY, VMEM, VMEM, ANY],
+        out_specs=VMEM,
         scratch_shapes=[
             pltpu.VMEM(neighbour_states.shape, jnp.float32),
             pltpu.VMEM((owners * CAP, SPAN + 16, 2 * width), jnp.bfloat16),
             pltpu.SemaphoreType.DMA((owners * CAP,)),
         ],
         compiler_params=LIMIT,
-    )(slots, gathered, neighbour_states, all_stats)
-    layer_output = pl.pallas_call(
-        project,
-        cost_estimate=cost(5),
-        grid_spec=pltpu.PrefetchScalarGridSpec(
-            num_scalar_prefetch=1,
-            grid=(grps * tps // sources,),
-            in_specs=[
-                pl.BlockSpec((sources, tok_rows, width), lambda i, core: (i, 0, 0)),
-                pl.BlockSpec((sources, width, half), lambda i, core: (i, 0, 0)),
-                pl.BlockSpec((sources, width, half), lambda i, core: (i, 0, 0)),
-                ANY,
-            ],
-            out_specs=pl.BlockSpec((tok_rows, out_columns), lambda i, core: (0, 0)),
-            scratch_shapes=[pltpu.VMEM((tok_rows, out_columns), jnp.float32)],
-        ),
-        out_shape=jax.ShapeDtypeStruct((tok_rows, out_columns), jnp.bfloat16),
-        compiler_params=LIMIT,
-    )(core, heads, weight, weight_other, finished)
+    )(slots, gathered, neighbour_states, all_stats, layer_output)
     return (layer_output, neighbour_gradient)
 
 

time: 161 us -> 159 us (0.988)
  starting transfers between devices: 15.3 us -> 36.1 us
  blocking collectives: 39.9 us -> 23.3 us
  waiting for transfers between devices: 59.1 us -> 46.3 us
  local copies, waits for them, and re-layouts: 3.65 us -> 12 us
  Pallas kernels: 27.1 us -> 25.4 us
    ppermute x0 -> x14, starting transfers between devices: none -> 20.8 us  [shifted(): lax.ppermute(value, axis, [(source, (source + steps) % count) for source...]
    all_gather x1 -> x0, blocking collectives: 16.6 us -> none  [local(): all_stats = lax.all_gather(stats, 'seq', axis=0, tiled=True)]
    all_gather x1, waiting for transfers between devices: 16.9 us -> 4.17 us  [local(): gathered = lax.all_gather(both, 'seq', axis=0, tiled=True)]
    unnamed x22 -> x30, local copies, waits for them, and re-layouts: 1.73 us -> 7.22 us
    pallas_call x1, Pallas kernels: 7.01 us -> 4.27 us  [local(): pl.pallas_call(span_forward, cost_estimate=cost(5), out_shape=(jax.ShapeD...]
    pallas_call x1 -> x2, Pallas kernels: 5.26 us -> 6.34 us  [the longest x1 3.35 us: local(): pl.pallas_call(project_near, cost_estimate=cost(3), out_shape=jax.ShapeDt...]
  transfers between devices with their start and end apart: 5 -> 19, of which waited for: 3 -> 3; matrix products, arithmetic and copies ran while one was open for 2% -> 7% of each run, Pallas kernels for 14% -> 9%
where the time goes in v6:
time: 159 us
  waiting for transfers between devices  46.3 us (29%)
  starting transfers between devices  36.1 us (23%)
  Pallas kernels  25.4 us (16%)
  blocking collectives  23.3 us (15%)
  between operations  14.3 us (9%)
  local copies, waits for them, and re-layouts  12 us (8%)
    all_to_all x1, waiting for transfers between devices, local(): weight = lax.all_to_all(cut, FEATS, split_axis=0, concat_axis=0, tiled=True)  27 us
    all_gather x1, blocking collectives, local(): lax.all_gather(jnp.stack([retrieved.reshape(request_count), valid_blocks....  23.3 us
    ppermute x14, starting transfers between devices, shifted(): lax.ppermute(value, axis, [(source, (source + steps) % count) for source...  20.8 us
    all_gather x1, waiting for transfers between devices, local(): store = lax.all_gather(neighbour_states, 'seq', axis=0)  14.4 us
    pallas_call x1, Pallas kernels, local(): pl.pallas_call(functools.partial(pair_backward, 4), cost_estimate=cost(10...  10.4 us
    all_to_all x1, starting transfers between devices, local(): weight = lax.all_to_all(cut, FEATS, split_axis=0, concat_axis=0, tiled=True)  7.72 us
    all_to_all x1, starting transfers between devices, local(): lax.all_to_all(jnp.broadcast_to(stats[None], (owners, *stats.shape)), 'se...  7.32 us
    unnamed x30, local copies, waits for them, and re-layouts  7.22 us
  transfers between devices with their start and end apart: 19, of which 3 were waited for; matrix products, arithmetic and copies ran while one was open for 7% of the time, Pallas kernels for 9%

profile of v6, /device:TPU:1, one launch (start us, length us, event | category | flops | bytes accessed | tf_op | source)
XLA Modules:
  0.0 158.7 jit_solution(12417357842582060231)
XLA Ops:
  7.2 0.7 all-gather.8.cloned.1.call-update
  7.9 4.4 %shard_map.77 = bf16[16,256,256]{2,1,0:T(8,128)(2,1)} custom-call(s32[1]{0:T(128)} %bitcast.6.core, bf16[256,8192]{1,0:T(8,128)(2,1)} %columns.1), custom_call_target="tpu_custom_call" | custom-call | tf_op jit(solution)/shard_map/pallas_call | solution.py:273
  12.3 7.7 %all-to-all-start = ((bf16[16,256,256]{2,1,0:T(8,128)(2,1)}), bf16[16,256,256]{2,1,0:T(8,128)(2,1)S(1)}, u32[]{:S(2)}, u32[]{:S(2)}) async-start(bf16[16,256,256]{2,1,0:T(8,128)(2,1)} %shard_map.77), calls=%async_computation | async-start | bytes 4194304 | tf_op jit(solution)/shard_map/all_to_all | solution.py:283
  20.1 0.8 pad_maximum_fusion.refs_0_
  20.9 27.0 %all-to-all-done.refs_3_.refs_6_.refs_4_.refs_1_ = bf16[16,256,256]{2,1,0:T(8,128)(2,1)S(1)} async-done(((bf16[16,256,256]{2,1,0:T(8,128)(2,1)}), bf16[16,256,256]{2,1,0:T(8,128)(2,1)S(1)}, u32[]{:S(2)}, u32[]{:S(2)}) %all-to-all-start) | async-done | bytes 2097184 | tf_op jit(solution)/shard_map/all_to_all | solution.py:283
  47.9 1.3 copy-done
  49.6 23.3 %all-gather.2 = s32[16,2,12]{2,1,0:T(2,128)S(1)} all-gather(s32[1,2,12]{2,1,0:T(2,128)S(1)} %add_bitcast_fusion), channel_id=2, replica_groups=mesh['grp'=4,'seq'=16,'tp'=4] {'seq'}, dimensions={0}, use_global_device_ids=true | all-gather | bytes 1632 | tf_op jit(solution)/shard_map/all_gather | solution.py:285
  75.4 14.4 %all-gather.8.cloned.1.call-done = bf16[32,6,128,256]{3,2,1,0:T(8,128)(2,1)} async-done(((bf16[2,6,128,256]{3,2,1,0:T(8,128)(2,1)}), bf16[32,6,128,256]{3,2,1,0:T(8,128)(2,1)}) %all-gather.8.cloned.1.call-update) | async-done | bytes 12582928 | tf_op jit(solution)/shard_map/all_gather | solution.py:303
  89.8 0.7 copy-done.6
  90.5 4.3 %shard_map.79 = (bf16[192,256]{1,0:T(8,128)(2,1)S(1)}, bf16[192,256]{1,0:T(8,128)(2,1)S(1)}, f32[6,4,128]{2,1,0:T(4,128)S(1)}) custom-call(s32[14]{0:T(128)S(1)} %copy-done.6, bf16[384,256]{1,0:T(8,128)(2,1)S(1)} %copy-done.3, bf16[384,256]{1,0:T(8,128)(2,1)S(1)} %copy-done.4, bf16[16,2,6,128,256]{4,3,2,1,0:T(8,128)(2,1)} %shard_map.78.store), custom_call_target="tpu_custom_call" | custom-call | flops 5000000000 | bytes 8388608 | tf_op jit(solution)/shard_map/pallas_call | solution.py:310
  94.8 1.3 collective-permute-start.7
  96.1 2.4 %collective-permute-start.8 = (bf16[192,256]{1,0:T(8,128)(2,1)S(1)}, bf16[192,256]{1,0:T(8,128)(2,1)S(1)}, u32[]{:S(2)}, u32[]{:S(2)}) collective-permute-start(bf16[192,256]{1,0:T(8,128)(2,1)S(1)} %get-tuple-element.6), channel_id=1, source_target_pairs={{0,2},{1,3},{2,0},{3,1},{4,6},{5,7},{6,4},{7,5},{8,10},{9,11},{10,... | collective-permute-start | bytes 294920 | tf_op jit(solution)/shard_map/ppermute | solution.py:212
  98.5 1.2 collective-permute-start.9
  99.6 1.2 collective-permute-start
  100.8 0.6 constant_dynamic-update-slice_fusion.7
  102.1 2.4 %collective-permute-start.1 = (bf16[192,256]{1,0:T(8,128)(2,1)S(1)}, bf16[192,256]{1,0:T(8,128)(2,1)S(1)}, u32[]{:S(2)}, u32[]{:S(2)}) collective-permute-start(bf16[192,256]{1,0:T(8,128)(2,1)S(1)} %get-tuple-element.5), channel_id=1, source_target_pairs={{0,128},{64,192},{128,0},{192,64},{1,129},{65,193},{129,1},{193,65... | collective-permute-start | bytes 294920 | tf_op jit(solution)/shard_map/ppermute | solution.py:212
  105.2 1.2 collective-permute-start.2
  107.0 0.6 constant_dynamic-update-slice_fusion.4.refs_3_
  108.0 2.4 %collective-permute-start.12 = (bf16[192,1024]{1,0:T(8,128)(2,1)}, bf16[192,1024]{1,0:T(8,128)(2,1)S(1)}, u32[]{:S(2)}, u32[]{:S(2)}) collective-permute-start(bf16[192,1024]{1,0:T(8,128)(2,1)} %constant_dynamic-update-slice_fusion.4.refs_3_), channel_id=1, source_target_pairs={{0,192},{64,0},{128,64},{192,128},{1,193},{65,1},{129,65},{193,129... | collective-permute-start | bytes 1179656 | tf_op jit(solution)/shard_map/ppermute | solution.py:212
  111.0 0.6 constant_dynamic-update-slice_fusion.1
  111.7 0.6 constant_dynamic-update-slice_fusion.refs_0_
  112.6 2.4 %collective-permute-start.5 = (bf16[192,1024]{1,0:T(8,128)(2,1)}, bf16[192,1024]{1,0:T(8,128)(2,1)}, u32[]{:S(2)}, u32[]{:S(2)}) collective-permute-start(bf16[192,1024]{1,0:T(8,128)(2,1)} %constant_dynamic-update-slice_fusion.refs_0_), channel_id=1, source_target_pairs={{0,3},{1,0},{2,1},{3,2},{4,7},{5,4},{6,5},{7,6},{8,11},{9,8},{10,9... | collective-permute-start | bytes 1179656 | tf_op jit(solution)/shard_map/ppermute | solution.py:212
  115.0 0.7 broadcast_in_dim.19
  115.7 7.3 %all-to-all-start.1 = ((f32[16,6,4,128]{3,2,1,0:T(4,128)}), f32[16,6,4,128]{3,2,1,0:T(4,128)S(1)}, u32[]{:S(2)}, u32[]{:S(2)}) async-start(f32[16,6,4,128]{3,2,1,0:T(4,128)} %broadcast_in_dim.19), calls=%async_computation.1 | async-start | bytes 393216 | tf_op jit(solution)/shard_map/all_to_all | solution.py:349
  123.2 2.9 %collective-permute-start.13 = (bf16[192,512]{1,0:T(8,128)(2,1)S(1)}, bf16[192,512]{1,0:T(8,128)(2,1)S(1)}, u32[]{:S(2)}, u32[]{:S(2)}) collective-permute-start(bf16[192,512]{1,0:T(8,128)(2,1)S(1)} %slice.32), channel_id=1, source_target_pairs={{0,192},{64,0},{128,64},{192,128},{1,193},{65,1},{129,65},{193,129... | collective-permute-start | bytes 589832 | tf_op jit(solution)/shard_map/ppermute | solution.py:212
  126.2 0.9 slice.30
  127.2 2.7 %collective-permute-start.6 = (bf16[192,512]{1,0:T(8,128)(2,1)S(1)}, bf16[192,512]{1,0:T(8,128)(2,1)S(1)}, u32[]{:S(2)}, u32[]{:S(2)}) collective-permute-start(bf16[192,512]{1,0:T(8,128)(2,1)S(1)} %slice.30), channel_id=1, source_target_pairs={{0,3},{1,0},{2,1},{3,2},{4,7},{5,4},{6,5},{7,6},{8,11},{9,8},{10,9... | collective-permute-start | bytes 589832 | tf_op jit(solution)/shard_map/ppermute | solution.py:212
  129.9 3.4 %shard_map.80.refs_6_ = f32[2,384,256]{2,1,0:T(8,128)S(1)} custom-call(bf16[192,1024]{1,0:T(8,128)(2,1)} %constant_dynamic-update-slice_fusion.refs_0_, bf16[192,1024]{1,0:T(8,128)(2,1)S(1)} %collective-permute-done.3.refs_1_, bf16[192,1024]{1,0:T(8,128)(2,1)} %collective-permute-done.5.refs_2_, ...), custom_call_target="tpu_custom_call" | custom-call | flops 3000000000 | bytes 8388608 | tf_op jit(solution)/shard_map/pallas_call | solution.py:332
  133.3 3.0 %shard_map.81.rest_0_ = bf16[384,512]{1,0:T(8,128)(2,1)} custom-call(bf16[192,512]{1,0:T(8,128)(2,1)S(1)} %collective-permute-done.4.refs_0_, bf16[192,512]{1,0:T(8,128)(2,1)S(1)} %collective-permute-done.6.refs_1_, bf16[192,512]{1,0:T(8,128)(2,1)S(1)} %collective-permute-done.11.refs_2_, bf16[192,512]{1,0:T(8,128)(2,1)S(1)} %collective-permute-done.13.refs_3_, ...), custom_call_target="tpu_custom_call" | custom-call | flops 2000000000 | bytes 8388608 | tf_op jit(solution)/shard_map/pallas_call | solution.py:340
  136.3 4.2 %all-gather.6.cloned.1.call-done.rows = bf16[6144,512]{1,0:T(8,128)(2,1)} async-done(((bf16[384,512]{1,0:T(8,128)(2,1)}), bf16[6144,512]{1,0:T(8,128)(2,1)}) %all-gather.6.cloned.1.call-update) | async-done | bytes 6291472 | tf_op jit(solution)/shard_map/all_gather | solution.py:306
  140.5 1.0 copy-done.7
  141.5 10.4 %shard_map.83 = bf16[2,6,128,256]{3,2,1,0:T(8,128)(2,1)} custom-call(s32[32]{0:T(128)S(1)} %copy-done.5, bf16[6144,512]{1,0:T(8,128)(2,1)} %all-gather.6.cloned.1.call-done.rows, bf16[2,6,128,256]{3,2,1,0:T(8,128)(2,1)S(1)} %copy-done.2, f32[96,4,128]{2,1,0:T(4,128)S(1)} %bitcast.19, bf16[384,512]{1,0:T(8,128)(2,1)S(1)} %copy-done.7), custom_call_target="tpu_custom_call" | custom-call | flops 10000000000 | bytes 8388608 | tf_op jit(solution)/shard_map/pallas_call | solution.py:352
  (76 shorter events, 6.4 us)
Async XLA Ops:
  7.2 82.7 %all-gather.8.cloned.1.call-start = ((), (), s32[]{:S(2)}) async-start(), calls=%async_computation.3 | async-start | bytes 13369344 | tf_op jit(solution)/shard_map/all_gather | solution.py:303
  7.9 12.2 %copy-start.3 = (bf16[384,256]{1,0:T(8,128)(2,1)S(1)}, bf16[384,256]{1,0:T(8,128)(2,1)}, u32[]{:S(2)}) copy-start(bf16[384,256]{1,0:T(8,128)(2,1)} %queries.1) | copy-start | bytes 589828
  7.9 12.2 %copy-start.4 = (bf16[384,256]{1,0:T(8,128)(2,1)S(1)}, bf16[384,256]{1,0:T(8,128)(2,1)}, u32[]{:S(2)}) copy-start(bf16[384,256]{1,0:T(8,128)(2,1)} %cotangents.1) | copy-start | bytes 589828
  12.3 36.9 %copy-start.8 = (s32[6,2]{0,1:T(2,128)S(1)}, s32[6,2]{0,1:T(2,128)}, u32[]{:S(2)}) copy-start(s32[6,2]{0,1:T(2,128)} %param.8) | copy-start | bytes 148
  12.3 37.1 %copy-start.9 = (s32[6,2]{0,1:T(2,128)S(1)}, s32[6,2]{0,1:T(2,128)}, u32[]{:S(2)}) copy-start(s32[6,2]{0,1:T(2,128)} %param.9) | copy-start | bytes 148
  12.3 35.6 %all-to-all-start = ((bf16[16,256,256]{2,1,0:T(8,128)(2,1)}), bf16[16,256,256]{2,1,0:T(8,128)(2,1)S(1)}, u32[]{:S(2)}, u32[]{:S(2)}) async-start(bf16[16,256,256]{2,1,0:T(8,128)(2,1)} %shard_map.77), calls=%async_computation | async-start | bytes 4194304 | tf_op jit(solution)/shard_map/all_to_all | solution.py:283
  20.0 120.5 %all-gather.6.cloned.1.call-start = ((), (), s32[]{:S(2)}) async-start(), calls=%async_computation.2 | async-start | bytes 6684672 | tf_op jit(solution)/shard_map/all_gather | solution.py:306
  47.9 1.3 copy-start
  74.5 55.4 %collective-permute-start.14 = (bf16[16,256,256]{2,1,0:T(8,128)(2,1)}, bf16[16,256,256]{2,1,0:T(8,128)(2,1)}, u32[]{:S(2)}, u32[]{:S(2)}) collective-permute-start(bf16[16,256,256]{2,1,0:T(8,128)(2,1)} %copy-done), channel_id=1, source_target_pairs={{0,4},{4,0},{8,12},{12,8},{16,20},{20,16},{24,28},{28,24},{32,36},... | collective-permute-start | bytes 6291464 | tf_op jit(solution)/shard_map/ppermute | solution.py:307
  89.8 0.7 copy-start.6
  90.5 39.4 %copy-start.1 = (bf16[16,256,256]{2,1,0:T(8,128)(2,1)S(1)}, bf16[16,256,256]{2,1,0:T(8,128)(2,1)}, u32[]{:S(2)}) copy-start(bf16[16,256,256]{2,1,0:T(8,128)(2,1)} %copy-done) | copy-start | bytes 6291460
  94.8 7.4 %collective-permute-start.7 = (bf16[192,256]{1,0:T(8,128)(2,1)S(1)}, bf16[192,256]{1,0:T(8,128)(2,1)S(1)}, u32[]{:S(2)}, u32[]{:S(2)}) collective-permute-start(bf16[192,256]{1,0:T(8,128)(2,1)S(1)} %get-tuple-element.6), channel_id=1, source_target_pairs={{0,1},{1,2},{2,3},{3,0},{4,5},{5,6},{6,7},{7,4},{8,9},{9,10},{10,1... | collective-permute-start | bytes 294920 | tf_op jit(solution)/shard_map/ppermute | solution.py:212
  96.1 9.1 %collective-permute-start.8 = (bf16[192,256]{1,0:T(8,128)(2,1)S(1)}, bf16[192,256]{1,0:T(8,128)(2,1)S(1)}, u32[]{:S(2)}, u32[]{:S(2)}) collective-permute-start(bf16[192,256]{1,0:T(8,128)(2,1)S(1)} %get-tuple-element.6), channel_id=1, source_target_pairs={{0,2},{1,3},{2,0},{3,1},{4,6},{5,7},{6,4},{7,5},{8,10},{9,11},{10,... | collective-permute-start | bytes 294920 | tf_op jit(solution)/shard_map/ppermute | solution.py:212
  98.5 8.5 %collective-permute-start.9 = (bf16[192,256]{1,0:T(8,128)(2,1)S(1)}, bf16[192,256]{1,0:T(8,128)(2,1)S(1)}, u32[]{:S(2)}, u32[]{:S(2)}) collective-permute-start(bf16[192,256]{1,0:T(8,128)(2,1)S(1)} %get-tuple-element.6), channel_id=1, source_target_pairs={{0,3},{1,0},{2,1},{3,2},{4,7},{5,4},{6,5},{7,6},{8,11},{9,8},{10,9... | collective-permute-start | bytes 294920 | tf_op jit(solution)/shard_map/ppermute | solution.py:212
  99.6 8.3 %collective-permute-start = (bf16[192,256]{1,0:T(8,128)(2,1)S(1)}, bf16[192,256]{1,0:T(8,128)(2,1)S(1)}, u32[]{:S(2)}, u32[]{:S(2)}) collective-permute-start(bf16[192,256]{1,0:T(8,128)(2,1)S(1)} %get-tuple-element.5), channel_id=1, source_target_pairs={{0,64},{64,128},{128,192},{192,0},{1,65},{65,129},{129,193},{193,1... | collective-permute-start | bytes 294920 | tf_op jit(solution)/shard_map/ppermute | solution.py:212
  102.1 8.9 %collective-permute-start.1 = (bf16[192,256]{1,0:T(8,128)(2,1)S(1)}, bf16[192,256]{1,0:T(8,128)(2,1)S(1)}, u32[]{:S(2)}, u32[]{:S(2)}) collective-permute-start(bf16[192,256]{1,0:T(8,128)(2,1)S(1)} %get-tuple-element.5), channel_id=1, source_target_pairs={{0,128},{64,192},{128,0},{192,64},{1,129},{65,193},{129,1},{193,65... | collective-permute-start | bytes 294920 | tf_op jit(solution)/shard_map/ppermute | solution.py:212
  105.2 6.5 %collective-permute-start.2 = (bf16[192,256]{1,0:T(8,128)(2,1)S(1)}, bf16[192,256]{1,0:T(8,128)(2,1)S(1)}, u32[]{:S(2)}, u32[]{:S(2)}) collective-permute-start(bf16[192,256]{1,0:T(8,128)(2,1)S(1)} %get-tuple-element.5), channel_id=1, source_target_pairs={{0,192},{64,0},{128,64},{192,128},{1,193},{65,1},{129,65},{193,129... | collective-permute-start | bytes 294920 | tf_op jit(solution)/shard_map/ppermute | solution.py:212
  107.7 15.3 %collective-permute-start.10 = (bf16[192,1024]{1,0:T(8,128)(2,1)}, bf16[192,1024]{1,0:T(8,128)(2,1)S(1)}, u32[]{:S(2)}, u32[]{:S(2)}) collective-permute-start(bf16[192,1024]{1,0:T(8,128)(2,1)} %constant_dynamic-update-slice_fusion.4.refs_3_), channel_id=1, source_target_pairs={{0,64},{64,128},{128,192},{192,0},{1,65},{65,129},{129,193},{193,1... | collective-permute-start | bytes 1179656 | tf_op jit(solution)/shard_map/ppermute | solution.py:212
  108.0 15.2 %collective-permute-start.12 = (bf16[192,1024]{1,0:T(8,128)(2,1)}, bf16[192,1024]{1,0:T(8,128)(2,1)S(1)}, u32[]{:S(2)}, u32[]{:S(2)}) collective-permute-start(bf16[192,1024]{1,0:T(8,128)(2,1)} %constant_dynamic-update-slice_fusion.4.refs_3_), channel_id=1, source_target_pairs={{0,192},{64,0},{128,64},{192,128},{1,193},{65,1},{129,65},{193,129... | collective-permute-start | bytes 1179656 | tf_op jit(solution)/shard_map/ppermute | solution.py:212
  112.3 13.8 %collective-permute-start.3 = (bf16[192,1024]{1,0:T(8,128)(2,1)}, bf16[192,1024]{1,0:T(8,128)(2,1)S(1)}, u32[]{:S(2)}, u32[]{:S(2)}) collective-permute-start(bf16[192,1024]{1,0:T(8,128)(2,1)} %constant_dynamic-update-slice_fusion.refs_0_), channel_id=1, source_target_pairs={{0,1},{1,2},{2,3},{3,0},{4,5},{5,6},{6,7},{7,4},{8,9},{9,10},{10,1... | collective-permute-start | bytes 1179656 | tf_op jit(solution)/shard_map/ppermute | solution.py:212
  112.6 13.6 %collective-permute-start.5 = (bf16[192,1024]{1,0:T(8,128)(2,1)}, bf16[192,1024]{1,0:T(8,128)(2,1)}, u32[]{:S(2)}, u32[]{:S(2)}) collective-permute-start(bf16[192,1024]{1,0:T(8,128)(2,1)} %constant_dynamic-update-slice_fusion.refs_0_), channel_id=1, source_target_pairs={{0,3},{1,0},{2,1},{3,2},{4,7},{5,4},{6,5},{7,6},{8,11},{9,8},{10,9... | collective-permute-start | bytes 1179656 | tf_op jit(solution)/shard_map/ppermute | solution.py:212
  115.7 24.8 %all-to-all-start.1 = ((f32[16,6,4,128]{3,2,1,0:T(4,128)}), f32[16,6,4,128]{3,2,1,0:T(4,128)S(1)}, u32[]{:S(2)}, u32[]{:S(2)}) async-start(f32[16,6,4,128]{3,2,1,0:T(4,128)} %broadcast_in_dim.19), calls=%async_computation.1 | async-start | bytes 393216 | tf_op jit(solution)/shard_map/all_to_all | solution.py:349
  123.0 10.2 %collective-permute-start.11 = (bf16[192,512]{1,0:T(8,128)(2,1)S(1)}, bf16[192,512]{1,0:T(8,128)(2,1)S(1)}, u32[]{:S(2)}, u32[]{:S(2)}) collective-permute-start(bf16[192,512]{1,0:T(8,128)(2,1)S(1)} %slice.31), channel_id=1, source_target_pairs={{0,64},{64,128},{128,192},{192,0},{1,65},{65,129},{129,193},{193,1... | collective-permute-start | bytes 589832 | tf_op jit(solution)/shard_map/ppermute | solution.py:212
  123.2 10.1 %collective-permute-start.13 = (bf16[192,512]{1,0:T(8,128)(2,1)S(1)}, bf16[192,512]{1,0:T(8,128)(2,1)S(1)}, u32[]{:S(2)}, u32[]{:S(2)}) collective-permute-start(bf16[192,512]{1,0:T(8,128)(2,1)S(1)} %slice.32), channel_id=1, source_target_pairs={{0,192},{64,0},{128,64},{192,128},{1,193},{65,1},{129,65},{193,129... | collective-permute-start | bytes 589832 | tf_op jit(solution)/shard_map/ppermute | solution.py:212
  126.1 7.2 %collective-permute-start.4 = (bf16[192,512]{1,0:T(8,128)(2,1)S(1)}, bf16[192,512]{1,0:T(8,128)(2,1)S(1)}, u32[]{:S(2)}, u32[]{:S(2)}) collective-permute-start(bf16[192,512]{1,0:T(8,128)(2,1)S(1)} %slice.29), channel_id=1, source_target_pairs={{0,1},{1,2},{2,3},{3,0},{4,5},{5,6},{6,7},{7,4},{8,9},{9,10},{10,1... | collective-permute-start | bytes 589832 | tf_op jit(solution)/shard_map/ppermute | solution.py:212
  127.2 6.2 %collective-permute-start.6 = (bf16[192,512]{1,0:T(8,128)(2,1)S(1)}, bf16[192,512]{1,0:T(8,128)(2,1)S(1)}, u32[]{:S(2)}, u32[]{:S(2)}) collective-permute-start(bf16[192,512]{1,0:T(8,128)(2,1)S(1)} %slice.30), channel_id=1, source_target_pairs={{0,3},{1,0},{2,1},{3,2},{4,7},{5,4},{6,5},{7,6},{8,11},{9,8},{10,9... | collective-permute-start | bytes 589832 | tf_op jit(solution)/shard_map/ppermute | solution.py:212
  133.3 7.2 %copy-start.2 = (bf16[2,6,128,256]{3,2,1,0:T(8,128)(2,1)S(1)}, bf16[2,6,128,256]{3,2,1,0:T(8,128)(2,1)}, u32[]{:S(2)}) copy-start(bf16[2,6,128,256]{3,2,1,0:T(8,128)(2,1)} %states.1) | copy-start | bytes 2359300
  133.3 7.2 %copy-start.5 = (s32[32]{0:T(128)S(1)}, s32[32]{0:T(128)}, u32[]{:S(2)}) copy-start(s32[32]{0:T(128)} %reshape.145.refs_1_.slots) | copy-start | bytes 388
  140.5 1.0 copy-start.7
Sparse Core Ops, SparseCore 0:
  9.8 79.9 all-gather.7
  91.7 48.7 all-gather.5

commit v7 on v6

--- a/solution.py
+++ b/solution.py
@@ -130,12 +130,15 @@
                 pair = (lines[j - j % 2, h], rolled[j - j % 2, h])
                 both.append(jnp.where(early, pair[j % 2], pair[1 - j % 2]))
             rows.append(jnp.where(lane % SPAN == SPAN - 1, both[1], both[0]))
-        stats[i] = jnp.concatenate([row[kind : kind + 1] for kind in range(2) for row in rows], 0)
+        both = jnp.concatenate([row[kind : kind + 1] for kind in range(2) for row in rows], 0)
+        if i % 2:
+            stats[i // 2] = jnp.where(early, previous, both)
+        previous = both
 
 
 def pair_backward(together, slots, rows, states, stats, *rest):
     out, total, windows, sems = rest[-4:]
-    spans = stats.shape[0]
+    spans = 2 * stats.shape[0]
     reach = SPAN + 16
     copies = []
     for i in range(slots.shape[0]):
@@ -151,7 +154,12 @@
     lane = lax.broadcasted_iota(jnp.int32, (1, 2 * SPAN), 1)
     early = lane < SPAN
     first_token = lane % SPAN == SPAN - 1
-    last_span = stats.shape[0] - 1
+    last_span = spans - 1
+
+    def block_lines(block):
+        held = stats[block >> 1]
+        turned = pltpu.roll(jnp.concatenate([held, held], 0), SPAN, 1)[: held.shape[0]]
+        return jnp.where(early == ((block & 1) == 0), held, turned)
 
     def one_target(target):
         span_0, row_0, live_0 = decode_slot(slots[target * CAP])
@@ -162,9 +170,11 @@
         seen = (jnp.where(early, live_0, live_1) > 0) & (first_token | (span < last_span))
         lines = jnp.where(
             first_token,
-            jnp.where(early, stats[span_0], stats[span_1]),
+            jnp.where(early, block_lines(span_0), block_lines(span_1)),
             jnp.where(
-                early, stats[jnp.minimum(span_0 + 1, last_span)], stats[jnp.minimum(span_1 + 1, last_span)]
+                early,
+                block_lines(jnp.minimum(span_0 + 1, last_span)),
+                block_lines(jnp.minimum(span_1 + 1, last_span)),
             ),
         )
         parts = []
@@ -176,9 +186,10 @@
             )
             k = jnp.concatenate([states[0, row_0, :, at : at + HDIM], states[0, row_1, :, at : at + HDIM]], 1)
             v = jnp.concatenate([states[1, row_0, :, at : at + HDIM], states[1, row_1, :, at : at + HDIM]], 1)
-            scores = dot(k, q, NT) * scale
+            both = dot(jnp.concatenate([k, v], 0), jnp.concatenate([q, g], 0), NT)
+            scores = both[:NTOK, : 2 * SPAN] * scale
             weights = jnp.where(seen, jnp.exp(scores - lines[h : h + 1]), 0.0)
-            grads = weights * (dot(v, g, NT) - lines[heads + h : heads + h + 1])
+            grads = weights * (both[NTOK:, 2 * SPAN :] - lines[heads + h : heads + h + 1])
             key_part = dot(grads.astype(jnp.bfloat16), q, NN) * scale
             value_part = dot(weights.astype(jnp.bfloat16), g, NN)
             parts.append((key_part, value_part))
@@ -239,7 +250,8 @@
 
 
 def project_far(*refs):
-    blocks, weights, partial, out = refs[:4], refs[4:6], refs[6], refs[7]
+    blocks, weights, partial, out, finished = refs[:4], refs[4:6], refs[6], refs[7], refs[8]
+    finished[...] = jnp.zeros_like(finished)
     side = lax.axis_size("tp")
     rows, width = blocks[0].shape[0], weights[0].shape[1]
     columns = weights[0].shape[2]
@@ -313,7 +325,7 @@
         out_shape=(
             jax.ShapeDtypeStruct((middle, width), jnp.bfloat16),
             jax.ShapeDtypeStruct((middle, width), jnp.bfloat16),
-            jax.ShapeDtypeStruct((span_count, 2 * width // HDIM, 2 * SPAN), jnp.float32),
+            jax.ShapeDtypeStruct((span_count // 2, 2 * width // HDIM, 2 * SPAN), jnp.float32),
         ),
         in_specs=[SMEM, VMEM, VMEM, ANY],
         out_specs=(VMEM, VMEM, VMEM),
@@ -337,23 +349,26 @@
         out_specs=VMEM,
         compiler_params=LIMIT,
     )(*upper, *lower, weight, weight_other)
-    layer_output = pl.pallas_call(
+    layer_output, finished = pl.pallas_call(
         project_far,
         cost_estimate=cost(2),
-        out_shape=jax.ShapeDtypeStruct((tok_rows, out_columns), jnp.bfloat16),
+        out_shape=(
+            jax.ShapeDtypeStruct((tok_rows, out_columns), jnp.bfloat16),
+            jax.ShapeDtypeStruct((8, HDIM), jnp.float32),
+        ),
         in_specs=[VMEM] * 7,
-        out_specs=VMEM,
+        out_specs=(VMEM, VMEM),
         compiler_params=LIMIT,
     )(*far, weight, weight_other, total)
 
     all_stats = lax.all_to_all(
         jnp.broadcast_to(stats[None], (owners, *stats.shape)), "seq", split_axis=0, concat_axis=0, tiled=True
-    ).reshape(owners * span_count, *stats.shape[1:])
+    ).reshape(owners * span_count // 2, *stats.shape[1:])
     neighbour_gradient = pl.pallas_call(
         functools.partial(pair_backward, 4),
         cost_estimate=cost(10),
         out_shape=jax.ShapeDtypeStruct(neighbour_states.shape, jnp.bfloat16),
-        in_specs=[SMEM, ANY, VMEM, VMEM, ANY],
+        in_specs=[SMEM, ANY, VMEM, VMEM, VMEM],
         out_specs=VMEM,
         scratch_shapes=[
             pltpu.VMEM(neighbour_states.shape, jnp.float32),
@@ -361,7 +376,7 @@
             pltpu.SemaphoreType.DMA((owners * CAP,)),
         ],
         compiler_params=LIMIT,
-    )(slots, gathered, neighbour_states, all_stats, layer_output)
+    )(slots, gathered, neighbour_states, all_stats, finished)
     return (layer_output, neighbour_gradient)
 
 

time: 159 us -> 155 us (0.975)
  waiting for transfers between devices: 46.3 us -> 44.2 us
    all_gather x1, waiting for transfers between devices: 4.17 us -> 2.08 us  [local(): gathered = lax.all_gather(both, 'seq', axis=0, tiled=True)]
    unnamed x30 -> x28, local copies, waits for them, and re-layouts: 7.22 us -> 6.23 us
  transfers between devices with their start and end apart: 19 -> 19, of which waited for: 3 -> 3; matrix products, arithmetic and copies ran while one was open for 7% -> 7% of each run, Pallas kernels for 9% -> 10%
where the time goes in v7:
time: 155 us
  waiting for transfers between devices  44.2 us (29%)
  starting transfers between devices  36.1 us (23%)
  Pallas kernels  24.3 us (16%)
  blocking collectives  23.3 us (15%)
  between operations  14.3 us (9%)
  local copies, waits for them, and re-layouts  11 us (7%)
    all_to_all x1, waiting for transfers between devices, local(): weight = lax.all_to_all(cut, FEATS, split_axis=0, concat_axis=0, tiled=True)  27 us
    all_gather x1, blocking collectives, local(): lax.all_gather(jnp.stack([retrieved.reshape(request_count), valid_blocks....  23.3 us
    ppermute x14, starting transfers between devices, shifted(): lax.ppermute(value, axis, [(source, (source + steps) % count) for source...  20.8 us
    all_gather x1, waiting for transfers between devices, local(): store = lax.all_gather(neighbour_states, 'seq', axis=0)  14.4 us
    pallas_call x1, Pallas kernels, local(): pl.pallas_call(functools.partial(pair_backward, 4), cost_estimate=cost(10...  9.33 us
    all_to_all x1, starting transfers between devices, local(): weight = lax.all_to_all(cut, FEATS, split_axis=0, concat_axis=0, tiled=True)  7.72 us
    all_to_all x1, starting transfers between devices, local(): lax.all_to_all(jnp.broadcast_to(stats[None], (owners, *stats.shape)), 'se...  7.32 us
    unnamed x28, local copies, waits for them, and re-layouts  6.23 us
  transfers between devices with their start and end apart: 19, of which 3 were waited for; matrix products, arithmetic and copies ran while one was open for 7% of the time, Pallas kernels for 10%

profile of v7, /device:TPU:1, one launch (start us, length us, event | category | flops | bytes accessed | tf_op | source)
XLA Modules:
  0.0 154.6 jit_solution(12989594319502398116)
XLA Ops:
  7.2 0.7 all-gather.8.cloned.1.call-update
  7.9 4.4 %shard_map.77 = bf16[16,256,256]{2,1,0:T(8,128)(2,1)} custom-call(s32[1]{0:T(128)} %bitcast.6.core, bf16[256,8192]{1,0:T(8,128)(2,1)} %columns.1), custom_call_target="tpu_custom_call" | custom-call | tf_op jit(solution)/shard_map/pallas_call | solution.py:285
  12.3 7.7 %all-to-all-start = ((bf16[16,256,256]{2,1,0:T(8,128)(2,1)}), bf16[16,256,256]{2,1,0:T(8,128)(2,1)S(1)}, u32[]{:S(2)}, u32[]{:S(2)}) async-start(bf16[16,256,256]{2,1,0:T(8,128)(2,1)} %shard_map.77), calls=%async_computation | async-start | bytes 4194304 | tf_op jit(solution)/shard_map/all_to_all | solution.py:295
  20.1 0.8 pad_maximum_fusion.refs_0_
  20.9 27.0 %all-to-all-done.refs_3_.refs_6_.refs_4_.refs_1_ = bf16[16,256,256]{2,1,0:T(8,128)(2,1)S(1)} async-done(((bf16[16,256,256]{2,1,0:T(8,128)(2,1)}), bf16[16,256,256]{2,1,0:T(8,128)(2,1)S(1)}, u32[]{:S(2)}, u32[]{:S(2)}) %all-to-all-start) | async-done | bytes 2097184 | tf_op jit(solution)/shard_map/all_to_all | solution.py:295
  47.9 1.3 copy-done
  49.6 23.3 %all-gather.2 = s32[16,2,12]{2,1,0:T(2,128)S(1)} all-gather(s32[1,2,12]{2,1,0:T(2,128)S(1)} %add_bitcast_fusion), channel_id=2, replica_groups=mesh['grp'=4,'seq'=16,'tp'=4] {'seq'}, dimensions={0}, use_global_device_ids=true | all-gather | bytes 1632 | tf_op jit(solution)/shard_map/all_gather | solution.py:297
  75.4 14.4 %all-gather.8.cloned.1.call-done = bf16[32,6,128,256]{3,2,1,0:T(8,128)(2,1)} async-done(((bf16[2,6,128,256]{3,2,1,0:T(8,128)(2,1)}), bf16[32,6,128,256]{3,2,1,0:T(8,128)(2,1)}) %all-gather.8.cloned.1.call-update) | async-done | bytes 12582928 | tf_op jit(solution)/shard_map/all_gather | solution.py:315
  89.8 0.7 copy-done.6
  90.5 4.3 %shard_map.79 = (bf16[192,256]{1,0:T(8,128)(2,1)S(1)}, bf16[192,256]{1,0:T(8,128)(2,1)S(1)}, f32[3,4,128]{2,1,0:T(4,128)S(1)}) custom-call(s32[14]{0:T(128)S(1)} %copy-done.6, bf16[384,256]{1,0:T(8,128)(2,1)S(1)} %copy-done.3, bf16[384,256]{1,0:T(8,128)(2,1)S(1)} %copy-done.4, bf16[16,2,6,128,256]{4,3,2,1,0:T(8,128)(2,1)} %shard_map.78.store), custom_call_target="tpu_custom_call" | custom-call | flops 5000000000 | bytes 8388608 | tf_op jit(solution)/shard_map/pallas_call | solution.py:322
  94.8 1.3 collective-permute-start.7
  96.1 2.4 %collective-permute-start.8 = (bf16[192,256]{1,0:T(8,128)(2,1)S(1)}, bf16[192,256]{1,0:T(8,128)(2,1)S(1)}, u32[]{:S(2)}, u32[]{:S(2)}) collective-permute-start(bf16[192,256]{1,0:T(8,128)(2,1)S(1)} %get-tuple-element.8), channel_id=1, source_target_pairs={{0,2},{1,3},{2,0},{3,1},{4,6},{5,7},{6,4},{7,5},{8,10},{9,11},{10,... | collective-permute-start | bytes 294920 | tf_op jit(solution)/shard_map/ppermute | solution.py:223
  98.5 1.2 collective-permute-start.9
  99.7 1.2 collective-permute-start
  100.8 0.6 constant_dynamic-update-slice_fusion.7
  101.5 0.6 constant_dynamic-update-slice_fusion.3
  102.1 2.4 %collective-permute-start.1 = (bf16[192,256]{1,0:T(8,128)(2,1)S(1)}, bf16[192,256]{1,0:T(8,128)(2,1)S(1)}, u32[]{:S(2)}, u32[]{:S(2)}) collective-permute-start(bf16[192,256]{1,0:T(8,128)(2,1)S(1)} %get-tuple-element.7), channel_id=1, source_target_pairs={{0,128},{64,192},{128,0},{192,64},{1,129},{65,193},{129,1},{193,65... | collective-permute-start | bytes 294920 | tf_op jit(solution)/shard_map/ppermute | solution.py:223
  105.2 1.2 collective-permute-start.2
  107.0 0.6 constant_dynamic-update-slice_fusion.4.refs_3_
  108.0 2.4 %collective-permute-start.12 = (bf16[192,1024]{1,0:T(8,128)(2,1)}, bf16[192,1024]{1,0:T(8,128)(2,1)S(1)}, u32[]{:S(2)}, u32[]{:S(2)}) collective-permute-start(bf16[192,1024]{1,0:T(8,128)(2,1)} %constant_dynamic-update-slice_fusion.4.refs_3_), channel_id=1, source_target_pairs={{0,192},{64,0},{128,64},{192,128},{1,193},{65,1},{129,65},{193,129... | collective-permute-start | bytes 1179656 | tf_op jit(solution)/shard_map/ppermute | solution.py:223
  111.0 0.6 constant_dynamic-update-slice_fusion.1
  111.7 0.6 constant_dynamic-update-slice_fusion.refs_0_
  112.6 2.4 %collective-permute-start.5 = (bf16[192,1024]{1,0:T(8,128)(2,1)}, bf16[192,1024]{1,0:T(8,128)(2,1)}, u32[]{:S(2)}, u32[]{:S(2)}) collective-permute-start(bf16[192,1024]{1,0:T(8,128)(2,1)} %constant_dynamic-update-slice_fusion.refs_0_), channel_id=1, source_target_pairs={{0,3},{1,0},{2,1},{3,2},{4,7},{5,4},{6,5},{7,6},{8,11},{9,8},{10,9... | collective-permute-start | bytes 1179656 | tf_op jit(solution)/shard_map/ppermute | solution.py:223
  115.0 0.7 broadcast_in_dim.19
  115.6 7.3 %all-to-all-start.1 = ((f32[16,3,4,128]{3,2,1,0:T(4,128)}), f32[16,3,4,128]{3,2,1,0:T(4,128)S(1)}, u32[]{:S(2)}, u32[]{:S(2)}) async-start(f32[16,3,4,128]{3,2,1,0:T(4,128)} %broadcast_in_dim.19), calls=%async_computation.1 | async-start | bytes 196608 | tf_op jit(solution)/shard_map/all_to_all | solution.py:364
  123.1 2.9 %collective-permute-start.13 = (bf16[192,512]{1,0:T(8,128)(2,1)S(1)}, bf16[192,512]{1,0:T(8,128)(2,1)S(1)}, u32[]{:S(2)}, u32[]{:S(2)}) collective-permute-start(bf16[192,512]{1,0:T(8,128)(2,1)S(1)} %slice.32), channel_id=1, source_target_pairs={{0,192},{64,0},{128,64},{192,128},{1,193},{65,1},{129,65},{193,129... | collective-permute-start | bytes 589832 | tf_op jit(solution)/shard_map/ppermute | solution.py:223
  126.2 0.9 slice.30
  127.1 2.7 %collective-permute-start.6 = (bf16[192,512]{1,0:T(8,128)(2,1)S(1)}, bf16[192,512]{1,0:T(8,128)(2,1)S(1)}, u32[]{:S(2)}, u32[]{:S(2)}) collective-permute-start(bf16[192,512]{1,0:T(8,128)(2,1)S(1)} %slice.30), channel_id=1, source_target_pairs={{0,3},{1,0},{2,1},{3,2},{4,7},{5,4},{6,5},{7,6},{8,11},{9,8},{10,9... | collective-permute-start | bytes 589832 | tf_op jit(solution)/shard_map/ppermute | solution.py:223
  129.9 3.4 %shard_map.80.refs_6_ = f32[2,384,256]{2,1,0:T(8,128)S(1)} custom-call(bf16[192,1024]{1,0:T(8,128)(2,1)} %constant_dynamic-update-slice_fusion.refs_0_, bf16[192,1024]{1,0:T(8,128)(2,1)S(1)} %collective-permute-done.3.refs_1_, bf16[192,1024]{1,0:T(8,128)(2,1)} %collective-permute-done.5.refs_2_, ...), custom_call_target="tpu_custom_call" | custom-call | flops 3000000000 | bytes 8388608 | tf_op jit(solution)/shard_map/pallas_call | solution.py:344
  133.3 3.0 %shard_map.81 = (bf16[384,512]{1,0:T(8,128)(2,1)}, f32[8,128]{1,0:T(8,128)S(1)}) custom-call(bf16[192,512]{1,0:T(8,128)(2,1)S(1)} %collective-permute-done.4.refs_0_, bf16[192,512]{1,0:T(8,128)(2,1)S(1)} %collective-permute-done.6.refs_1_, bf16[192,512]{1,0:T(8,128)(2,1)S(1)} %collective-permute-done.11.refs_2_, ...), custom_call_target="tpu_custom_call" | custom-call | flops 2000000000 | bytes 8388608 | tf_op jit(solution)/shard_map/pallas_call | solution.py:352
  136.3 2.1 %all-gather.6.cloned.1.call-done.rows = bf16[6144,512]{1,0:T(8,128)(2,1)} async-done(((bf16[384,512]{1,0:T(8,128)(2,1)}), bf16[6144,512]{1,0:T(8,128)(2,1)}) %all-gather.6.cloned.1.call-update) | async-done | bytes 6291472 | tf_op jit(solution)/shard_map/all_gather | solution.py:318
  138.4 9.3 %shard_map.83 = bf16[2,6,128,256]{3,2,1,0:T(8,128)(2,1)} custom-call(s32[32]{0:T(128)S(1)} %copy-done.5, bf16[6144,512]{1,0:T(8,128)(2,1)} %all-gather.6.cloned.1.call-done.rows, bf16[2,6,128,256]{3,2,1,0:T(8,128)(2,1)S(1)} %copy-done.2, f32[48,4,128]{2,1,0:T(4,128)S(1)} %bitcast.19, f32[8,128]{1,0:T(8,128)S(1)} %get-tuple-element.11.rest_0_), custom_call_target="tpu_custom_call" | custom-call | flops 10000000000 | bytes 8388608 | tf_op jit(solution)/shard_map/pallas_call | solution.py:367
  (74 shorter events, 5.8 us)
Async XLA Ops:
  7.2 82.7 %all-gather.8.cloned.1.call-start = ((), (), s32[]{:S(2)}) async-start(), calls=%async_computation.3 | async-start | bytes 13369344 | tf_op jit(solution)/shard_map/all_gather | solution.py:315
  7.9 12.2 %copy-start.3 = (bf16[384,256]{1,0:T(8,128)(2,1)S(1)}, bf16[384,256]{1,0:T(8,128)(2,1)}, u32[]{:S(2)}) copy-start(bf16[384,256]{1,0:T(8,128)(2,1)} %queries.1) | copy-start | bytes 589828
  7.9 12.2 %copy-start.4 = (bf16[384,256]{1,0:T(8,128)(2,1)S(1)}, bf16[384,256]{1,0:T(8,128)(2,1)}, u32[]{:S(2)}) copy-start(bf16[384,256]{1,0:T(8,128)(2,1)} %cotangents.1) | copy-start | bytes 589828
  12.3 36.9 %copy-start.7 = (s32[6,2]{0,1:T(2,128)S(1)}, s32[6,2]{0,1:T(2,128)}, u32[]{:S(2)}) copy-start(s32[6,2]{0,1:T(2,128)} %param.8) | copy-start | bytes 148
  12.3 37.1 %copy-start.8 = (s32[6,2]{0,1:T(2,128)S(1)}, s32[6,2]{0,1:T(2,128)}, u32[]{:S(2)}) copy-start(s32[6,2]{0,1:T(2,128)} %param.9) | copy-start | bytes 148
  12.3 35.6 %all-to-all-start = ((bf16[16,256,256]{2,1,0:T(8,128)(2,1)}), bf16[16,256,256]{2,1,0:T(8,128)(2,1)S(1)}, u32[]{:S(2)}, u32[]{:S(2)}) async-start(bf16[16,256,256]{2,1,0:T(8,128)(2,1)} %shard_map.77), calls=%async_computation | async-start | bytes 4194304 | tf_op jit(solution)/shard_map/all_to_all | solution.py:295
  20.0 118.4 %all-gather.6.cloned.1.call-start = ((), (), s32[]{:S(2)}) async-start(), calls=%async_computation.2 | async-start | bytes 6684672 | tf_op jit(solution)/shard_map/all_gather | solution.py:318
  47.9 1.3 copy-start
  74.5 55.4 %collective-permute-start.14 = (bf16[16,256,256]{2,1,0:T(8,128)(2,1)}, bf16[16,256,256]{2,1,0:T(8,128)(2,1)}, u32[]{:S(2)}, u32[]{:S(2)}) collective-permute-start(bf16[16,256,256]{2,1,0:T(8,128)(2,1)} %copy-done), channel_id=1, source_target_pairs={{0,4},{4,0},{8,12},{12,8},{16,20},{20,16},{24,28},{28,24},{32,36},... | collective-permute-start | bytes 6291464 | tf_op jit(solution)/shard_map/ppermute | solution.py:319
  89.8 0.7 copy-start.6
  90.5 39.4 %copy-start.1 = (bf16[16,256,256]{2,1,0:T(8,128)(2,1)S(1)}, bf16[16,256,256]{2,1,0:T(8,128)(2,1)}, u32[]{:S(2)}) copy-start(bf16[16,256,256]{2,1,0:T(8,128)(2,1)} %copy-done) | copy-start | bytes 6291460
  94.8 7.4 %collective-permute-start.7 = (bf16[192,256]{1,0:T(8,128)(2,1)S(1)}, bf16[192,256]{1,0:T(8,128)(2,1)S(1)}, u32[]{:S(2)}, u32[]{:S(2)}) collective-permute-start(bf16[192,256]{1,0:T(8,128)(2,1)S(1)} %get-tuple-element.8), channel_id=1, source_target_pairs={{0,1},{1,2},{2,3},{3,0},{4,5},{5,6},{6,7},{7,4},{8,9},{9,10},{10,1... | collective-permute-start | bytes 294920 | tf_op jit(solution)/shard_map/ppermute | solution.py:223
  96.1 9.1 %collective-permute-start.8 = (bf16[192,256]{1,0:T(8,128)(2,1)S(1)}, bf16[192,256]{1,0:T(8,128)(2,1)S(1)}, u32[]{:S(2)}, u32[]{:S(2)}) collective-permute-start(bf16[192,256]{1,0:T(8,128)(2,1)S(1)} %get-tuple-element.8), channel_id=1, source_target_pairs={{0,2},{1,3},{2,0},{3,1},{4,6},{5,7},{6,4},{7,5},{8,10},{9,11},{10,... | collective-permute-start | bytes 294920 | tf_op jit(solution)/shard_map/ppermute | solution.py:223
  98.5 8.5 %collective-permute-start.9 = (bf16[192,256]{1,0:T(8,128)(2,1)S(1)}, bf16[192,256]{1,0:T(8,128)(2,1)S(1)}, u32[]{:S(2)}, u32[]{:S(2)}) collective-permute-start(bf16[192,256]{1,0:T(8,128)(2,1)S(1)} %get-tuple-element.8), channel_id=1, source_target_pairs={{0,3},{1,0},{2,1},{3,2},{4,7},{5,4},{6,5},{7,6},{8,11},{9,8},{10,9... | collective-permute-start | bytes 294920 | tf_op jit(solution)/shard_map/ppermute | solution.py:223
  99.7 8.3 %collective-permute-start = (bf16[192,256]{1,0:T(8,128)(2,1)S(1)}, bf16[192,256]{1,0:T(8,128)(2,1)S(1)}, u32[]{:S(2)}, u32[]{:S(2)}) collective-permute-start(bf16[192,256]{1,0:T(8,128)(2,1)S(1)} %get-tuple-element.7), channel_id=1, source_target_pairs={{0,64},{64,128},{128,192},{192,0},{1,65},{65,129},{129,193},{193,1... | collective-permute-start | bytes 294920 | tf_op jit(solution)/shard_map/ppermute | solution.py:223
  102.1 8.9 %collective-permute-start.1 = (bf16[192,256]{1,0:T(8,128)(2,1)S(1)}, bf16[192,256]{1,0:T(8,128)(2,1)S(1)}, u32[]{:S(2)}, u32[]{:S(2)}) collective-permute-start(bf16[192,256]{1,0:T(8,128)(2,1)S(1)} %get-tuple-element.7), channel_id=1, source_target_pairs={{0,128},{64,192},{128,0},{192,64},{1,129},{65,193},{129,1},{193,65... | collective-permute-start | bytes 294920 | tf_op jit(solution)/shard_map/ppermute | solution.py:223
  105.2 6.5 %collective-permute-start.2 = (bf16[192,256]{1,0:T(8,128)(2,1)S(1)}, bf16[192,256]{1,0:T(8,128)(2,1)S(1)}, u32[]{:S(2)}, u32[]{:S(2)}) collective-permute-start(bf16[192,256]{1,0:T(8,128)(2,1)S(1)} %get-tuple-element.7), channel_id=1, source_target_pairs={{0,192},{64,0},{128,64},{192,128},{1,193},{65,1},{129,65},{193,129... | collective-permute-start | bytes 294920 | tf_op jit(solution)/shard_map/ppermute | solution.py:223
  107.7 15.3 %collective-permute-start.10 = (bf16[192,1024]{1,0:T(8,128)(2,1)}, bf16[192,1024]{1,0:T(8,128)(2,1)S(1)}, u32[]{:S(2)}, u32[]{:S(2)}) collective-permute-start(bf16[192,1024]{1,0:T(8,128)(2,1)} %constant_dynamic-update-slice_fusion.4.refs_3_), channel_id=1, source_target_pairs={{0,64},{64,128},{128,192},{192,0},{1,65},{65,129},{129,193},{193,1... | collective-permute-start | bytes 1179656 | tf_op jit(solution)/shard_map/ppermute | solution.py:223
  108.0 15.1 %collective-permute-start.12 = (bf16[192,1024]{1,0:T(8,128)(2,1)}, bf16[192,1024]{1,0:T(8,128)(2,1)S(1)}, u32[]{:S(2)}, u32[]{:S(2)}) collective-permute-start(bf16[192,1024]{1,0:T(8,128)(2,1)} %constant_dynamic-update-slice_fusion.4.refs_3_), channel_id=1, source_target_pairs={{0,192},{64,0},{128,64},{192,128},{1,193},{65,1},{129,65},{193,129... | collective-permute-start | bytes 1179656 | tf_op jit(solution)/shard_map/ppermute | solution.py:223
  112.3 13.8 %collective-permute-start.3 = (bf16[192,1024]{1,0:T(8,128)(2,1)}, bf16[192,1024]{1,0:T(8,128)(2,1)S(1)}, u32[]{:S(2)}, u32[]{:S(2)}) collective-permute-start(bf16[192,1024]{1,0:T(8,128)(2,1)} %constant_dynamic-update-slice_fusion.refs_0_), channel_id=1, source_target_pairs={{0,1},{1,2},{2,3},{3,0},{4,5},{5,6},{6,7},{7,4},{8,9},{9,10},{10,1... | collective-permute-start | bytes 1179656 | tf_op jit(solution)/shard_map/ppermute | solution.py:223
  112.6 13.6 %collective-permute-start.5 = (bf16[192,1024]{1,0:T(8,128)(2,1)}, bf16[192,1024]{1,0:T(8,128)(2,1)}, u32[]{:S(2)}, u32[]{:S(2)}) collective-permute-start(bf16[192,1024]{1,0:T(8,128)(2,1)} %constant_dynamic-update-slice_fusion.refs_0_), channel_id=1, source_target_pairs={{0,3},{1,0},{2,1},{3,2},{4,7},{5,4},{6,5},{7,6},{8,11},{9,8},{10,9... | collective-permute-start | bytes 1179656 | tf_op jit(solution)/shard_map/ppermute | solution.py:223
  115.6 22.7 %all-to-all-start.1 = ((f32[16,3,4,128]{3,2,1,0:T(4,128)}), f32[16,3,4,128]{3,2,1,0:T(4,128)S(1)}, u32[]{:S(2)}, u32[]{:S(2)}) async-start(f32[16,3,4,128]{3,2,1,0:T(4,128)} %broadcast_in_dim.19), calls=%async_computation.1 | async-start | bytes 196608 | tf_op jit(solution)/shard_map/all_to_all | solution.py:364
  123.0 10.2 %collective-permute-start.11 = (bf16[192,512]{1,0:T(8,128)(2,1)S(1)}, bf16[192,512]{1,0:T(8,128)(2,1)S(1)}, u32[]{:S(2)}, u32[]{:S(2)}) collective-permute-start(bf16[192,512]{1,0:T(8,128)(2,1)S(1)} %slice.31), channel_id=1, source_target_pairs={{0,64},{64,128},{128,192},{192,0},{1,65},{65,129},{129,193},{193,1... | collective-permute-start | bytes 589832 | tf_op jit(solution)/shard_map/ppermute | solution.py:223
  123.1 10.1 %collective-permute-start.13 = (bf16[192,512]{1,0:T(8,128)(2,1)S(1)}, bf16[192,512]{1,0:T(8,128)(2,1)S(1)}, u32[]{:S(2)}, u32[]{:S(2)}) collective-permute-start(bf16[192,512]{1,0:T(8,128)(2,1)S(1)} %slice.32), channel_id=1, source_target_pairs={{0,192},{64,0},{128,64},{192,128},{1,193},{65,1},{129,65},{193,129... | collective-permute-start | bytes 589832 | tf_op jit(solution)/shard_map/ppermute | solution.py:223
  126.1 7.2 %collective-permute-start.4 = (bf16[192,512]{1,0:T(8,128)(2,1)S(1)}, bf16[192,512]{1,0:T(8,128)(2,1)S(1)}, u32[]{:S(2)}, u32[]{:S(2)}) collective-permute-start(bf16[192,512]{1,0:T(8,128)(2,1)S(1)} %slice.29), channel_id=1, source_target_pairs={{0,1},{1,2},{2,3},{3,0},{4,5},{5,6},{6,7},{7,4},{8,9},{9,10},{10,1... | collective-permute-start | bytes 589832 | tf_op jit(solution)/shard_map/ppermute | solution.py:223
  127.1 6.2 %collective-permute-start.6 = (bf16[192,512]{1,0:T(8,128)(2,1)S(1)}, bf16[192,512]{1,0:T(8,128)(2,1)S(1)}, u32[]{:S(2)}, u32[]{:S(2)}) collective-permute-start(bf16[192,512]{1,0:T(8,128)(2,1)S(1)} %slice.30), channel_id=1, source_target_pairs={{0,3},{1,0},{2,1},{3,2},{4,7},{5,4},{6,5},{7,6},{8,11},{9,8},{10,9... | collective-permute-start | bytes 589832 | tf_op jit(solution)/shard_map/ppermute | solution.py:223
  133.2 5.2 %copy-start.2 = (bf16[2,6,128,256]{3,2,1,0:T(8,128)(2,1)S(1)}, bf16[2,6,128,256]{3,2,1,0:T(8,128)(2,1)}, u32[]{:S(2)}) copy-start(bf16[2,6,128,256]{3,2,1,0:T(8,128)(2,1)} %states.1) | copy-start | bytes 2359300
  133.2 5.2 %copy-start.5 = (s32[32]{0:T(128)S(1)}, s32[32]{0:T(128)}, u32[]{:S(2)}) copy-start(s32[32]{0:T(128)} %reshape.145.refs_1_.slots) | copy-start | bytes 388
Sparse Core Ops, SparseCore 0:
  9.8 79.9 all-gather.7
  91.7 46.6 all-gather.5

commit v8 on v7

--- a/solution.py
+++ b/solution.py
@@ -59,17 +59,47 @@
     )
 
 
-def span_forward(codes, queries, cotangents, store, upper, lower, stats, held, sems):
+def span_forward(distances, codes, queries, cotangents, store, *rest):
+    pieces, (upper, lower, stats, held, extra, sems, extra_sems) = rest[:-7], rest[-7:]
+    per_core = len(pieces) // 2
+    me = lax.axis_index("seq")
+    chips = lax.axis_size("seq") // 2
+    piece_copies = []
+    for i, piece in enumerate(pieces):
+        distance, start = distances[i % per_core]
+        chip = lax.rem(lax.div(me, 2) + (chips - distance) % chips, chips)
+        core = lax.rem(lax.rem(me, 2) + i // per_core, 2)
+        target = extra.at[chip * 2 + core, pl.ds(start, piece.shape[0])]
+        piece_copies.append(pltpu.make_async_copy(piece, target, extra_sems.at[i]))
+        piece_copies[-1].start()
+    store_rows = (store.shape[1] + extra.shape[1] // NTOK) // 2
+    value_rows = store.shape[1] - store_rows
     blocks, width = queries.shape[0] // SPAN, queries.shape[1]
     windows = blocks + 1
     heads = range(0, width, HDIM)
     scale = HDIM ** (-0.5)
     copies = []
+    owners, rows = [], []
     for i in range(KNB * windows):
         row = codes[i] & 127
-        source = store.at[lax.div(row, store.shape[2]), :, lax.rem(row, store.shape[2])]
-        copies.append(pltpu.make_async_copy(source, held.at[i], sems.at[i]))
+        owners.append(lax.div(row, store_rows))
+        rows.append(lax.rem(row, store_rows))
+        copies.append(pltpu.make_async_copy(store.at[owners[i], rows[i]], held.at[i, 0], sems.at[i, 0]))
         copies[-1].start()
+    for copy in piece_copies:
+        copy.wait()
+    for i in range(KNB * windows):
+        early_row = jnp.minimum(rows[i], value_rows - 1)
+        late_row = pl.multiple_of(jnp.maximum(rows[i] - value_rows, 0) * NTOK, NTOK)
+        stored = pltpu.make_async_copy(
+            store.at[owners[i], store_rows + early_row], held.at[i, 1], sems.at[i, 1]
+        )
+        moved = pltpu.make_async_copy(
+            extra.at[owners[i], pl.ds(late_row, NTOK)], held.at[i, 1], sems.at[i, 1]
+        )
+        pl.when(rows[i] < value_rows)(stored.start)
+        pl.when(rows[i] >= value_rows)(moved.start)
+        copies.append(stored)
 
     lane = lax.broadcasted_iota(jnp.int32, (1, 2 * SPAN), 1)
     early = lane < SPAN
@@ -88,6 +118,7 @@
         second = min(first + 1, windows - 1)
         for i in range(KNB * first, KNB * (second + 1)):
             copies[i].wait()
+            copies[KNB * windows + i].wait()
         tokens = [window(queries, i) for i in (first, second)]
         others = [window(cotangents, i) for i in (first, second)]
         live = [jnp.where(early, codes[KNB * first + k] >> 7, codes[KNB * second + k] >> 7) > 0 for k in range(KNB)]
@@ -294,9 +325,24 @@
     )(core, output_weight)
     weight = lax.all_to_all(cut, FEATS, split_axis=0, concat_axis=0, tiled=True)
 
-    table = lax.all_gather(
-        jnp.stack([retrieved.reshape(request_count), valid_blocks.reshape(request_count)]), "seq", axis=0
-    )
+    def steps(value, chips):
+        return lax.ppermute(value, "seq", [(at, (at + 2 * chips) % owners) for at in range(owners)])
+
+    def swap(value):
+        return lax.ppermute(value, "seq", [(at, at ^ 1) for at in range(owners)])
+
+    stacked = neighbour_states.reshape(2 * store_rows, NTOK, width)
+    late_rows = store_rows // 2
+    store = lax.all_gather(stacked[: 2 * store_rows - late_rows], "seq", axis=0)
+    late = tied(stacked[2 * store_rows - late_rows :].reshape(late_rows * NTOK, width), cut)
+    cut_at = late_rows * NTOK // 2
+    up_1, down_1, up_2, down_2 = [steps(late, i) for i in (1, -1, 2, -2)]
+    further = [steps(up_2, 1), steps(down_2, -1), steps(up_2[:cut_at], 2), steps(down_2[cut_at:], -2)]
+    distances = [(0, 0), (1, 0), (-1, 0), (2, 0), (-2, 0), (3, 0), (-3, 0), (4, 0), (4, cut_at)]
+    late = [late, up_1, down_1, up_2, down_2, *further]
+    late = late + [swap(piece) for piece in late]
+    table = jnp.stack([retrieved.reshape(request_count), valid_blocks.reshape(request_count)])
+    table = lax.all_gather(tied(table, up_2, down_2), "seq", axis=0)
     owner_of = table[:, 0] // store_rows
     same_owner = owner_of[:, :, None] == owner_of[:, None, :]
     order = jnp.arange(request_count, dtype=jnp.int32)
@@ -308,34 +354,36 @@
         position[:, None, :] == jnp.arange(CAP, dtype=jnp.int32)[None, :, None]
     )
     slots = jnp.sum(jnp.where(hit, code[:, None, :], 0), axis=2).reshape(owners * CAP)
-    plain = (table[:, 0] + 128 * (table[:, 1] > 0).astype(jnp.int32)).reshape(owners * request_count)
-    plain = jnp.concatenate([jnp.zeros((KNB,), jnp.int32), plain])
-    codes = lax.dynamic_slice_in_dim(plain, me * request_count, request_count + KNB, 0)
-
-    store = lax.all_gather(neighbour_states, "seq", axis=0)
-    store = tied(store, slots, codes, weight)
-    both = tied(jnp.concatenate([queries, attention_cotangent], axis=1), weight)
+    codes = (retrieved + 128 * (valid_blocks > 0).astype(jnp.int32)).reshape(request_count)
+    before = lax.ppermute(codes[-KNB:], "seq", [(at, at + 1) for at in range(owners - 1)])
+    codes = jnp.concatenate([before, codes])
+
+    store = tied(store, codes, slots)
+    both = tied(jnp.concatenate([queries, attention_cotangent], axis=1), slots)
     gathered = lax.all_gather(both, "seq", axis=0, tiled=True)
-    weight_other = lax.ppermute(weight, "seq", [(source, source ^ 1) for source in range(owners)])
 
     middle = tok_rows // 2
     upper, lower, stats = pl.pallas_call(
-        span_forward,
+        functools.partial(span_forward, distances),
         cost_estimate=cost(5),
         out_shape=(
             jax.ShapeDtypeStruct((middle, width), jnp.bfloat16),
             jax.ShapeDtypeStruct((middle, width), jnp.bfloat16),
             jax.ShapeDtypeStruct((span_count // 2, 2 * width // HDIM, 2 * SPAN), jnp.float32),
         ),
-        in_specs=[SMEM, VMEM, VMEM, ANY],
+        in_specs=[SMEM, VMEM, VMEM, ANY] + [ANY] * len(late),
         out_specs=(VMEM, VMEM, VMEM),
         scratch_shapes=[
             pltpu.VMEM((request_count + KNB, 2, NTOK, width), jnp.bfloat16),
-            pltpu.SemaphoreType.DMA((request_count + KNB,)),
+            pltpu.VMEM((owners, late_rows * NTOK, width), jnp.bfloat16),
+            pltpu.SemaphoreType.DMA((request_count + KNB, 2)),
+            pltpu.SemaphoreType.DMA((len(late),)),
         ],
         compiler_params=LIMIT,
-    )(codes, queries, attention_cotangent, store)
-
+    )(codes, queries, attention_cotangent, store, *late)
+
+    weight = tied(weight, stats)
+    weight_other = swap(weight)
     lower = jnp.concatenate([lower] + [shifted(lower, "tp", i) for i in range(1, tps)], 1)
     upper = jnp.concatenate([upper] + [shifted(upper, "grp", i) for i in range(1, grps)], 1)
     upper = [upper, shifted(upper, "tp", 1), shifted(upper, "tp", tps - 1)]
@@ -365,7 +413,7 @@
         jnp.broadcast_to(stats[None], (owners, *stats.shape)), "seq", split_axis=0, concat_axis=0, tiled=True
     ).reshape(owners * span_count // 2, *stats.shape[1:])
     neighbour_gradient = pl.pallas_call(
-        functools.partial(pair_backward, 4),
+        functools.partial(pair_backward, 8),
         cost_estimate=cost(10),
         out_shape=jax.ShapeDtypeStruct(neighbour_states.shape, jnp.bfloat16),
         in_specs=[SMEM, ANY, VMEM, VMEM, VMEM],

time: 155 us -> 168 us (1.084)
  starting transfers between devices: 36.1 us -> 59 us
  waiting for transfers between devices: 44.2 us -> 25.9 us
  local copies, waits for them, and re-layouts: 11 us -> 20.6 us
  blocking collectives: 23.3 us -> 17.6 us
  Pallas kernels: 24.3 us -> 27.4 us
    all_to_all x1, waiting for transfers between devices: 27 us -> 0.01 us  [local(): weight = lax.all_to_all(cut, FEATS, split_axis=0, concat_axis=0, tiled=True)]
    ppermute x1 -> x19, waiting for transfers between devices: 0.01 us -> 25.8 us  [the longest x8 21.3 us: steps(): lax.ppermute(value, 'seq', [(at, (at + 2 * chips) % owners) for at in ran...]
    ppermute x1 -> x19, starting transfers between devices: 0.19 us -> 22.1 us  [the longest x8 13.4 us: steps(): lax.ppermute(value, 'seq', [(at, (at + 2 * chips) % owners) for at in ran...]
    all_gather x1, waiting for transfers between devices: 14.4 us -> 0.01 us  [local(): store = lax.all_gather(stacked[:2 * store_rows - late_rows], 'seq', axis=0)]
    unnamed x28 -> x72, local copies, waits for them, and re-layouts: 6.23 us -> 14.9 us
    all_gather x1, blocking collectives: 23.3 us -> 17.6 us  [local(): table = lax.all_gather(tied(table, up_2, down_2), 'seq', axis=0)]
    slice x1 -> x6, local copies, waits for them, and re-layouts: 0.08 us -> 3.82 us  [the longest x1 1.92 us: local(): store = lax.all_gather(stacked[:2 * store_rows - late_rows], 'seq', axis=0)]
    pallas_call x2, Pallas kernels: 13.6 us -> 17 us  [the longest x1 9.07 us: local(): pl.pallas_call(functools.partial(pair_backward, 8), cost_estimate=cost(10...]
  transfers between devices with their start and end apart: 19 -> 37, of which waited for: 3 -> 7; matrix products, arithmetic and copies ran while one was open for 7% -> 4% of each run, Pallas kernels for 10% -> 11%
where the time goes in v8:
time: 168 us; the launch traced here: 167 us
  starting transfers between devices  59 us (35%)
  Pallas kernels  27.4 us (16%)
  waiting for transfers between devices  25.9 us (15%)
  local copies, waits for them, and re-layouts  20.6 us (12%)
  blocking collectives  17.6 us (10%)
  between operations  14.5 us (9%)
  other arithmetic  2.47 us (1%)
    ppermute x14, starting transfers between devices, shifted(): lax.ppermute(value, axis, [(source, (source + steps) % count) for source...  22.2 us
    ppermute x8, waiting for transfers between devices, steps(): lax.ppermute(value, 'seq', [(at, (at + 2 * chips) % owners) for at in ran...  21.3 us
    all_gather x1, blocking collectives, local(): table = lax.all_gather(tied(table, up_2, down_2), 'seq', axis=0)  17.6 us
    unnamed x72, local copies, waits for them, and re-layouts  14.9 us
    ppermute x8, starting transfers between devices, steps(): lax.ppermute(value, 'seq', [(at, (at + 2 * chips) % owners) for at in ran...  13.4 us
    pallas_call x1, Pallas kernels, local(): pl.pallas_call(functools.partial(pair_backward, 8), cost_estimate=cost(10...  9.07 us
    pallas_call x1, Pallas kernels, local(): pl.pallas_call(functools.partial(span_forward, distances), cost_estimate=...  7.9 us
    all_to_all x1, starting transfers between devices, local(): lax.all_to_all(jnp.broadcast_to(stats[None], (owners, *stats.shape)), 'se...  7.82 us
  transfers between devices with their start and end apart: 37, of which 7 were waited for; matrix products, arithmetic and copies ran while one was open for 4% of the time, Pallas kernels for 11%

profile of v8, /device:TPU:1, one launch (start us, length us, event | category | flops | bytes accessed | tf_op | source)
XLA Modules:
  0.0 167.4 jit_solution(16193678259657391242)
XLA Ops:
  7.2 1.9 %slice.49 = bf16[9,128,256]{2,1,0:T(8,128)(2,1)} slice(bf16[12,128,256]{2,1,0:T(8,128)(2,1)} %bitcast.19), slice={[0:9], [0:128], [0:256]} | slice | bytes 1179648 | tf_op jit(solution)/shard_map/slice | solution.py:336
  9.2 1.6 slice.50
  10.8 4.3 %shard_map.77.refs_1_ = bf16[16,256,256]{2,1,0:T(8,128)(2,1)} custom-call(s32[1]{0:T(128)} %bitcast.3.core, bf16[256,8192]{1,0:T(8,128)(2,1)} %columns.1), custom_call_target="tpu_custom_call" | custom-call | tf_op jit(solution)/shard_map/pallas_call | solution.py:316
  15.2 3.8 %collective-permute-start.1 = (bf16[384,256]{1,0:T(8,128)(2,1)}, bf16[384,256]{1,0:T(8,128)(2,1)S(1)}, u32[]{:S(2)}, u32[]{:S(2)}) collective-permute-start(bf16[384,256]{1,0:T(8,128)(2,1)} %shard_map.78.rest_0_), channel_id=1, source_target_pairs={{0,16},{4,20},{8,24},{12,28},{16,32},{20,36},{24,40},{28,44},{32,4... | collective-permute-start | bytes 589832 | tf_op jit(solution)/shard_map/ppermute | solution.py:329
  19.0 3.1 %collective-permute-start.2 = (bf16[384,256]{1,0:T(8,128)(2,1)}, bf16[384,256]{1,0:T(8,128)(2,1)S(1)}, u32[]{:S(2)}, u32[]{:S(2)}) collective-permute-start(bf16[384,256]{1,0:T(8,128)(2,1)} %shard_map.78.rest_0_), channel_id=1, source_target_pairs={{0,48},{4,52},{8,56},{12,60},{16,0},{20,4},{24,8},{28,12},{32,16},... | collective-permute-start | bytes 589832 | tf_op jit(solution)/shard_map/ppermute | solution.py:329
  23.8 4.3 %collective-permute-done.1.refs_1_.rest_3_ = bf16[384,256]{1,0:T(8,128)(2,1)S(1)} collective-permute-done((bf16[384,256]{1,0:T(8,128)(2,1)}, bf16[384,256]{1,0:T(8,128)(2,1)S(1)}, u32[]{:S(2)}, u32[]{:S(2)}) %collective-permute-start.1) | collective-permute-done | bytes 196640 | tf_op jit(solution)/shard_map/ppermute | solution.py:329
  28.1 7.1 %collective-permute-done.2.refs_2_.rest_4_ = bf16[384,256]{1,0:T(8,128)(2,1)S(1)} collective-permute-done((bf16[384,256]{1,0:T(8,128)(2,1)}, bf16[384,256]{1,0:T(8,128)(2,1)S(1)}, u32[]{:S(2)}, u32[]{:S(2)}) %collective-permute-start.2) | collective-permute-done | bytes 196640 | tf_op jit(solution)/shard_map/ppermute | solution.py:329
  35.9 17.6 %all-gather.2 = s32[16,2,12]{2,1,0:T(2,128)S(1)} all-gather(s32[1,2,12]{2,1,0:T(2,128)} %bitcast.23), channel_id=3, replica_groups=mesh['grp'=4,'seq'=16,'tp'=4] {'seq'}, dimensions={0}, use_global_device_ids=true | all-gather | bytes 1632 | tf_op jit(solution)/shard_map/all_gather | solution.py:345
  55.1 6.8 %all-to-all-start = ((bf16[16,256,256]{2,1,0:T(8,128)(2,1)}), bf16[16,256,256]{2,1,0:T(8,128)(2,1)S(1)}, u32[]{:S(2)}, u32[]{:S(2)}) async-start(bf16[16,256,256]{2,1,0:T(8,128)(2,1)} %shard_map.77.refs_1_), calls=%async_computation | async-start | bytes 4194304 | tf_op jit(solution)/shard_map/all_to_all | solution.py:326
  61.9 1.7 %collective-permute-start.3 = (bf16[384,256]{1,0:T(8,128)(2,1)S(1)}, bf16[384,256]{1,0:T(8,128)(2,1)S(1)}, u32[]{:S(2)}, u32[]{:S(2)}) collective-permute-start(bf16[384,256]{1,0:T(8,128)(2,1)S(1)} %copy-done.3), channel_id=1, source_target_pairs={{0,8},{4,12},{8,16},{12,20},{16,24},{20,28},{24,32},{28,36},{32,40... | collective-permute-start | bytes 589832 | tf_op jit(solution)/shard_map/ppermute | solution.py:329
  65.8 2.2 %collective-permute-start = (s32[2]{0:T(128)S(1)}, s32[2]{0:T(128)S(1)}, u32[]{:S(2)}, u32[]{:S(2)}) collective-permute-start(s32[2]{0:T(128)S(1)} %slice_reduce_fusion), channel_id=1, source_target_pairs={{0,4},{4,8},{8,12},{12,16},{16,20},{20,24},{24,28},{28,32},{32,36}... | collective-permute-start | bytes 32 | tf_op jit(solution)/shard_map/ppermute | solution.py:358
  68.3 3.9 %collective-permute-done = s32[2]{0:T(128)S(1)} collective-permute-done((s32[2]{0:T(128)S(1)}, s32[2]{0:T(128)S(1)}, u32[]{:S(2)}, u32[]{:S(2)}) %collective-permute-start) | collective-permute-done | bytes 40 | tf_op jit(solution)/shard_map/ppermute | solution.py:358
  72.2 1.8 %collective-permute-done.3.rest_1_ = bf16[384,256]{1,0:T(8,128)(2,1)S(1)} collective-permute-done((bf16[384,256]{1,0:T(8,128)(2,1)S(1)}, bf16[384,256]{1,0:T(8,128)(2,1)S(1)}, u32[]{:S(2)}, u32[]{:S(2)}) %collective-permute-start.3) | collective-permute-done | bytes 196640 | tf_op jit(solution)/shard_map/ppermute | solution.py:329
  74.4 3.2 %collective-permute-start.8 = (bf16[192,256]{1,0:T(8,128)(2,1)S(1)}, bf16[192,256]{1,0:T(8,128)(2,1)S(1)}, u32[]{:S(2)}, u32[]{:S(2)}) collective-permute-start(bf16[192,256]{1,0:T(8,128)(2,1)S(1)} %slice.54), channel_id=1, source_target_pairs={{0,48},{4,52},{8,56},{12,60},{16,0},{20,4},{24,8},{28,12},{32,16},... | collective-permute-start | bytes 294920 | tf_op jit(solution)/shard_map/ppermute | solution.py:329
  78.3 2.1 %collective-permute-start.12 = (bf16[384,256]{1,0:T(8,128)(2,1)S(1)}, bf16[384,256]{1,0:T(8,128)(2,1)S(1)}, u32[]{:S(2)}, u32[]{:S(2)}) collective-permute-start(bf16[384,256]{1,0:T(8,128)(2,1)S(1)} %copy-done.6), channel_id=1, source_target_pairs={{0,4},{4,0},{8,12},{12,8},{16,20},{20,16},{24,28},{28,24},{32,36},... | collective-permute-start | bytes 589832 | tf_op jit(solution)/shard_map/ppermute | solution.py:332
  80.4 8.0 %collective-permute-done.7.rest_7_ = bf16[192,256]{1,0:T(8,128)(2,1)S(1)} collective-permute-done((bf16[192,256]{1,0:T(8,128)(2,1)S(1)}, bf16[192,256]{1,0:T(8,128)(2,1)S(1)}, u32[]{:S(2)}, u32[]{:S(2)}) %collective-permute-start.7) | collective-permute-done | bytes 98336 | tf_op jit(solution)/shard_map/ppermute | solution.py:329
  88.4 1.6 collective-permute-start.16
  102.6 7.9 %shard_map.81 = (bf16[192,256]{1,0:T(8,128)(2,1)S(1)}, bf16[192,256]{1,0:T(8,128)(2,1)S(1)}, f32[3,4,128]{2,1,0:T(4,128)S(1)}) custom-call(s32[14]{0:T(128)S(1)} %copy-done.14, bf16[384,256]{1,0:T(8,128)(2,1)S(1)} %copy-done.9, bf16[384,256]{1,0:T(8,128)(2,1)S(1)} %copy-done.10, bf16[16,9,128,256]{3,2,1,0:T(8,128)(2,1)} %shard_map.80.store, ...), custom_call_target="tpu_custom_call" | custom-call | flops 5000000000 | bytes 8388608 | tf_op jit(solution)/shard_map/pallas_call | solution.py:366
  111.1 1.3 copy-done
  113.9 2.5 %collective-permute-start.26 = (bf16[192,256]{1,0:T(8,128)(2,1)S(1)}, bf16[192,256]{1,0:T(8,128)(2,1)S(1)}, u32[]{:S(2)}, u32[]{:S(2)}) collective-permute-start(bf16[192,256]{1,0:T(8,128)(2,1)S(1)} %get-tuple-element.8), channel_id=1, source_target_pairs={{0,2},{1,3},{2,0},{3,1},{4,6},{5,7},{6,4},{7,5},{8,10},{9,11},{10,... | collective-permute-start | bytes 294920 | tf_op jit(solution)/shard_map/ppermute | solution.py:254
  118.8 2.5 %collective-permute-start.19 = (bf16[192,256]{1,0:T(8,128)(2,1)S(1)}, bf16[192,256]{1,0:T(8,128)(2,1)S(1)}, u32[]{:S(2)}, u32[]{:S(2)}) collective-permute-start(bf16[192,256]{1,0:T(8,128)(2,1)S(1)} %get-tuple-element.7), channel_id=1, source_target_pairs={{0,128},{64,192},{128,0},{192,64},{1,129},{65,193},{129,1},{193,65... | collective-permute-start | bytes 294920 | tf_op jit(solution)/shard_map/ppermute | solution.py:254
  121.3 2.3 %collective-permute-start.20 = (bf16[192,256]{1,0:T(8,128)(2,1)S(1)}, bf16[192,256]{1,0:T(8,128)(2,1)S(1)}, u32[]{:S(2)}, u32[]{:S(2)}) collective-permute-start(bf16[192,256]{1,0:T(8,128)(2,1)S(1)} %get-tuple-element.7), channel_id=1, source_target_pairs={{0,192},{64,0},{128,64},{192,128},{1,193},{65,1},{129,65},{193,129... | collective-permute-start | bytes 294920 | tf_op jit(solution)/shard_map/ppermute | solution.py:254
  123.7 2.7 %collective-permute-start.30 = (bf16[192,1024]{1,0:T(8,128)(2,1)S(1)}, bf16[192,1024]{1,0:T(8,128)(2,1)S(1)}, u32[]{:S(2)}, u32[]{:S(2)}) collective-permute-start(bf16[192,1024]{1,0:T(8,128)(2,1)S(1)} %constant_dynamic-update-slice_fusion.4.refs_3_), channel_id=1, source_target_pairs={{0,192},{64,0},{128,64},{192,128},{1,193},{65,1},{129,65},{193,129... | collective-permute-start | bytes 1179656 | tf_op jit(solution)/shard_map/ppermute | solution.py:254
  126.6 2.5 %collective-permute-start.23 = (bf16[192,1024]{1,0:T(8,128)(2,1)S(1)}, bf16[192,1024]{1,0:T(8,128)(2,1)S(1)}, u32[]{:S(2)}, u32[]{:S(2)}) collective-permute-start(bf16[192,1024]{1,0:T(8,128)(2,1)S(1)} %constant_dynamic-update-slice_fusion.refs_0_), channel_id=1, source_target_pairs={{0,3},{1,0},{2,1},{3,2},{4,7},{5,4},{6,5},{7,6},{8,11},{9,8},{10,9... | collective-permute-start | bytes 1179656 | tf_op jit(solution)/shard_map/ppermute | solution.py:254
  129.8 7.8 %all-to-all-start.1 = ((f32[16,3,4,128]{3,2,1,0:T(4,128)}), f32[16,3,4,128]{3,2,1,0:T(4,128)S(1)}, u32[]{:S(2)}, u32[]{:S(2)}) async-start(f32[16,3,4,128]{3,2,1,0:T(4,128)} %broadcast_in_dim.19), calls=%async_computation.1 | async-start | bytes 196608 | tf_op jit(solution)/shard_map/all_to_all | solution.py:412
  137.7 1.6 collective-permute-start.29
  139.3 1.4 collective-permute-start.31
  140.9 2.7 %collective-permute-start.24 = (bf16[192,512]{1,0:T(8,128)(2,1)S(1)}, bf16[192,512]{1,0:T(8,128)(2,1)S(1)}, u32[]{:S(2)}, u32[]{:S(2)}) collective-permute-start(bf16[192,512]{1,0:T(8,128)(2,1)S(1)} %slice.56), channel_id=1, source_target_pairs={{0,3},{1,0},{2,1},{3,2},{4,7},{5,4},{6,5},{7,6},{8,11},{9,8},{10,9... | collective-permute-start | bytes 589832 | tf_op jit(solution)/shard_map/ppermute | solution.py:254
  143.7 1.6 copy-done.1
  145.2 3.1 %shard_map.83.refs_6_ = f32[2,384,256]{2,1,0:T(8,128)S(1)} custom-call(bf16[192,1024]{1,0:T(8,128)(2,1)S(1)} %constant_dynamic-update-slice_fusion.refs_0_, bf16[192,1024]{1,0:T(8,128)(2,1)S(1)} %collective-permute-done.21.refs_1_, bf16[192,1024]{1,0:T(8,128)(2,1)S(1)} %collective-permute-done.23.refs_2_, ...), custom_call_target="tpu_custom_call" | custom-call | flops 3000000000 | bytes 8388608 | tf_op jit(solution)/shard_map/pallas_call | solution.py:392
  148.5 3.0 %shard_map.84 = (bf16[384,512]{1,0:T(8,128)(2,1)}, f32[8,128]{1,0:T(8,128)S(1)}) custom-call(bf16[192,512]{1,0:T(8,128)(2,1)S(1)} %collective-permute-done.22.refs_0_, bf16[192,512]{1,0:T(8,128)(2,1)S(1)} %collective-permute-done.24.refs_1_, bf16[192,512]{1,0:T(8,128)(2,1)S(1)} %collective-permute-done.29.refs_2_, ...), custom_call_target="tpu_custom_call" | custom-call | flops 2000000000 | bytes 8388608 | tf_op jit(solution)/shard_map/pallas_call | solution.py:400
  151.5 9.1 %shard_map.86 = bf16[2,6,128,256]{3,2,1,0:T(8,128)(2,1)} custom-call(s32[32]{0:T(128)S(1)} %copy-done.13, bf16[6144,512]{1,0:T(8,128)(2,1)} %all-gather.6.cloned.1.call-done.rows, bf16[2,6,128,256]{3,2,1,0:T(8,128)(2,1)S(1)} %copy-done.4, f32[48,4,128]{2,1,0:T(4,128)S(1)} %bitcast.21, f32[8,128]{1,0:T(8,128)S(1)} %get-tuple-element.11.rest_0_), custom_call_target="tpu_custom_call" | custom-call | flops 10000000000 | bytes 8388608 | tf_op jit(solution)/shard_map/pallas_call | solution.py:415
  (162 shorter events, 25.6 us)
Async XLA Ops:
  7.2 88.5 %all-gather.8.cloned.1.call-start = ((), (), s32[]{:S(2)}) async-start(), calls=%async_computation.3 | async-start | bytes 10027008 | tf_op jit(solution)/shard_map/all_gather | solution.py:336
  9.2 142.3 %all-gather.6.cloned.1.call-start = ((), (), s32[]{:S(2)}) async-start(), calls=%async_computation.2 | async-start | bytes 6684672 | tf_op jit(solution)/shard_map/all_gather | solution.py:363
  15.2 12.9 %collective-permute-start.1 = (bf16[384,256]{1,0:T(8,128)(2,1)}, bf16[384,256]{1,0:T(8,128)(2,1)S(1)}, u32[]{:S(2)}, u32[]{:S(2)}) collective-permute-start(bf16[384,256]{1,0:T(8,128)(2,1)} %shard_map.78.rest_0_), channel_id=1, source_target_pairs={{0,16},{4,20},{8,24},{12,28},{16,32},{20,36},{24,40},{28,44},{32,4... | collective-permute-start | bytes 589832 | tf_op jit(solution)/shard_map/ppermute | solution.py:329
  19.0 16.2 %collective-permute-start.2 = (bf16[384,256]{1,0:T(8,128)(2,1)}, bf16[384,256]{1,0:T(8,128)(2,1)S(1)}, u32[]{:S(2)}, u32[]{:S(2)}) collective-permute-start(bf16[384,256]{1,0:T(8,128)(2,1)} %shard_map.78.rest_0_), channel_id=1, source_target_pairs={{0,48},{4,52},{8,56},{12,60},{16,0},{20,4},{24,8},{28,12},{32,16},... | collective-permute-start | bytes 589832 | tf_op jit(solution)/shard_map/ppermute | solution.py:329
  55.1 56.1 %all-to-all-start = ((bf16[16,256,256]{2,1,0:T(8,128)(2,1)}), bf16[16,256,256]{2,1,0:T(8,128)(2,1)S(1)}, u32[]{:S(2)}, u32[]{:S(2)}) async-start(bf16[16,256,256]{2,1,0:T(8,128)(2,1)} %shard_map.77.refs_1_), calls=%async_computation | async-start | bytes 4194304 | tf_op jit(solution)/shard_map/all_to_all | solution.py:326
  61.9 12.2 %collective-permute-start.3 = (bf16[384,256]{1,0:T(8,128)(2,1)S(1)}, bf16[384,256]{1,0:T(8,128)(2,1)S(1)}, u32[]{:S(2)}, u32[]{:S(2)}) collective-permute-start(bf16[384,256]{1,0:T(8,128)(2,1)S(1)} %copy-done.3), channel_id=1, source_target_pairs={{0,8},{4,12},{8,16},{12,20},{16,24},{20,28},{24,32},{28,36},{32,40... | collective-permute-start | bytes 589832 | tf_op jit(solution)/shard_map/ppermute | solution.py:329
  63.6 10.8 %collective-permute-start.4 = (bf16[384,256]{1,0:T(8,128)(2,1)S(1)}, bf16[384,256]{1,0:T(8,128)(2,1)S(1)}, u32[]{:S(2)}, u32[]{:S(2)}) collective-permute-start(bf16[384,256]{1,0:T(8,128)(2,1)S(1)} %copy-done.3), channel_id=1, source_target_pairs={{0,56},{4,60},{8,0},{12,4},{16,8},{20,12},{24,16},{28,20},{32,24},... | collective-permute-start | bytes 589832 | tf_op jit(solution)/shard_map/ppermute | solution.py:329
  64.6 13.0 %collective-permute-start.9 = (bf16[384,256]{1,0:T(8,128)(2,1)S(1)}, bf16[384,256]{1,0:T(8,128)(2,1)S(1)}, u32[]{:S(2)}, u32[]{:S(2)}) collective-permute-start(bf16[384,256]{1,0:T(8,128)(2,1)S(1)} %copy-done.3), channel_id=1, source_target_pairs={{0,4},{4,0},{8,12},{12,8},{16,20},{20,16},{24,28},{28,24},{32,36},... | collective-permute-start | bytes 589832 | tf_op jit(solution)/shard_map/ppermute | solution.py:332
  65.8 6.4 %collective-permute-start = (s32[2]{0:T(128)S(1)}, s32[2]{0:T(128)S(1)}, u32[]{:S(2)}, u32[]{:S(2)}) collective-permute-start(s32[2]{0:T(128)S(1)} %slice_reduce_fusion), channel_id=1, source_target_pairs={{0,4},{4,8},{8,12},{12,16},{16,20},{20,24},{24,28},{28,32},{32,36}... | collective-permute-start | bytes 32 | tf_op jit(solution)/shard_map/ppermute | solution.py:358
  68.1 23.2 %collective-permute-start.5 = (bf16[384,256]{1,0:T(8,128)(2,1)S(1)}, bf16[384,256]{1,0:T(8,128)(2,1)}, u32[]{:S(2)}, u32[]{:S(2)}) collective-permute-start(bf16[384,256]{1,0:T(8,128)(2,1)S(1)} %copy-done.6), channel_id=1, source_target_pairs={{0,8},{4,12},{8,16},{12,20},{16,24},{20,28},{24,32},{28,36},{32,40... | collective-permute-start | bytes 589832 | tf_op jit(solution)/shard_map/ppermute | solution.py:329
  72.2 19.6 %collective-permute-start.6 = (bf16[384,256]{1,0:T(8,128)(2,1)S(1)}, bf16[384,256]{1,0:T(8,128)(2,1)}, u32[]{:S(2)}, u32[]{:S(2)}) collective-permute-start(bf16[384,256]{1,0:T(8,128)(2,1)S(1)} %copy-done.8), channel_id=1, source_target_pairs={{0,56},{4,60},{8,0},{12,4},{16,8},{20,12},{24,16},{28,20},{32,24},... | collective-permute-start | bytes 589832 | tf_op jit(solution)/shard_map/ppermute | solution.py:329
  74.1 14.3 %collective-permute-start.7 = (bf16[192,256]{1,0:T(8,128)(2,1)S(1)}, bf16[192,256]{1,0:T(8,128)(2,1)S(1)}, u32[]{:S(2)}, u32[]{:S(2)}) collective-permute-start(bf16[192,256]{1,0:T(8,128)(2,1)S(1)} %slice.53), channel_id=1, source_target_pairs={{0,16},{4,20},{8,24},{12,28},{16,32},{20,36},{24,40},{28,44},{32,4... | collective-permute-start | bytes 294920 | tf_op jit(solution)/shard_map/ppermute | solution.py:329
  74.4 16.3 %collective-permute-start.8 = (bf16[192,256]{1,0:T(8,128)(2,1)S(1)}, bf16[192,256]{1,0:T(8,128)(2,1)S(1)}, u32[]{:S(2)}, u32[]{:S(2)}) collective-permute-start(bf16[192,256]{1,0:T(8,128)(2,1)S(1)} %slice.54), channel_id=1, source_target_pairs={{0,48},{4,52},{8,56},{12,60},{16,0},{20,4},{24,8},{28,12},{32,16},... | collective-permute-start | bytes 294920 | tf_op jit(solution)/shard_map/ppermute | solution.py:329
  78.3 15.4 %collective-permute-start.12 = (bf16[384,256]{1,0:T(8,128)(2,1)S(1)}, bf16[384,256]{1,0:T(8,128)(2,1)S(1)}, u32[]{:S(2)}, u32[]{:S(2)}) collective-permute-start(bf16[384,256]{1,0:T(8,128)(2,1)S(1)} %copy-done.6), channel_id=1, source_target_pairs={{0,4},{4,0},{8,12},{12,8},{16,20},{20,16},{24,28},{28,24},{32,36},... | collective-permute-start | bytes 589832 | tf_op jit(solution)/shard_map/ppermute | solution.py:332
  91.3 4.3 %collective-permute-start.13 = (bf16[384,256]{1,0:T(8,128)(2,1)S(1)}, bf16[384,256]{1,0:T(8,128)(2,1)}, u32[]{:S(2)}, u32[]{:S(2)}) collective-permute-start(bf16[384,256]{1,0:T(8,128)(2,1)S(1)} %copy-done.8), channel_id=1, source_target_pairs={{0,4},{4,0},{8,12},{12,8},{16,20},{20,16},{24,28},{28,24},{32,36},... | collective-permute-start | bytes 589832 | tf_op jit(solution)/shard_map/ppermute | solution.py:332
  91.8 3.8 %collective-permute-start.10 = (bf16[384,256]{1,0:T(8,128)(2,1)S(1)}, bf16[384,256]{1,0:T(8,128)(2,1)}, u32[]{:S(2)}, u32[]{:S(2)}) collective-permute-start(bf16[384,256]{1,0:T(8,128)(2,1)S(1)} %collective-permute-done.3.rest_1_), channel_id=1, source_target_pairs={{0,4},{4,0},{8,12},{12,8},{16,20},{20,16},{24,28},{28,24},{32,36},... | collective-permute-start | bytes 589832 | tf_op jit(solution)/shard_map/ppermute | solution.py:332
  112.5 31.2 %collective-permute-start.32 = (bf16[16,256,256]{2,1,0:T(8,128)(2,1)}, bf16[16,256,256]{2,1,0:T(8,128)(2,1)}, u32[]{:S(2)}, u32[]{:S(2)}) collective-permute-start(bf16[16,256,256]{2,1,0:T(8,128)(2,1)} %shard_map.82.refs_6_.refs_4_), channel_id=1, source_target_pairs={{0,4},{4,0},{8,12},{12,8},{16,20},{20,16},{24,28},{28,24},{32,36},... | collective-permute-start | bytes 6291464 | tf_op jit(solution)/shard_map/ppermute | solution.py:332
  112.7 6.0 %collective-permute-start.25 = (bf16[192,256]{1,0:T(8,128)(2,1)S(1)}, bf16[192,256]{1,0:T(8,128)(2,1)S(1)}, u32[]{:S(2)}, u32[]{:S(2)}) collective-permute-start(bf16[192,256]{1,0:T(8,128)(2,1)S(1)} %get-tuple-element.8), channel_id=1, source_target_pairs={{0,1},{1,2},{2,3},{3,0},{4,5},{5,6},{6,7},{7,4},{8,9},{9,10},{10,1... | collective-permute-start | bytes 294920 | tf_op jit(solution)/shard_map/ppermute | solution.py:254
  113.9 7.4 %collective-permute-start.26 = (bf16[192,256]{1,0:T(8,128)(2,1)S(1)}, bf16[192,256]{1,0:T(8,128)(2,1)S(1)}, u32[]{:S(2)}, u32[]{:S(2)}) collective-permute-start(bf16[192,256]{1,0:T(8,128)(2,1)S(1)} %get-tuple-element.8), channel_id=1, source_target_pairs={{0,2},{1,3},{2,0},{3,1},{4,6},{5,7},{6,4},{7,5},{8,10},{9,11},{10,... | collective-permute-start | bytes 294920 | tf_op jit(solution)/shard_map/ppermute | solution.py:254
  116.4 7.2 %collective-permute-start.27 = (bf16[192,256]{1,0:T(8,128)(2,1)S(1)}, bf16[192,256]{1,0:T(8,128)(2,1)S(1)}, u32[]{:S(2)}, u32[]{:S(2)}) collective-permute-start(bf16[192,256]{1,0:T(8,128)(2,1)S(1)} %get-tuple-element.8), channel_id=1, source_target_pairs={{0,3},{1,0},{2,1},{3,2},{4,7},{5,4},{6,5},{7,6},{8,11},{9,8},{10,9... | collective-permute-start | bytes 294920 | tf_op jit(solution)/shard_map/ppermute | solution.py:254
  117.5 6.2 %collective-permute-start.18 = (bf16[192,256]{1,0:T(8,128)(2,1)S(1)}, bf16[192,256]{1,0:T(8,128)(2,1)S(1)}, u32[]{:S(2)}, u32[]{:S(2)}) collective-permute-start(bf16[192,256]{1,0:T(8,128)(2,1)S(1)} %get-tuple-element.7), channel_id=1, source_target_pairs={{0,64},{64,128},{128,192},{192,0},{1,65},{65,129},{129,193},{193,1... | collective-permute-start | bytes 294920 | tf_op jit(solution)/shard_map/ppermute | solution.py:254
  118.8 7.6 %collective-permute-start.19 = (bf16[192,256]{1,0:T(8,128)(2,1)S(1)}, bf16[192,256]{1,0:T(8,128)(2,1)S(1)}, u32[]{:S(2)}, u32[]{:S(2)}) collective-permute-start(bf16[192,256]{1,0:T(8,128)(2,1)S(1)} %get-tuple-element.7), channel_id=1, source_target_pairs={{0,128},{64,192},{128,0},{192,64},{1,129},{65,193},{129,1},{193,65... | collective-permute-start | bytes 294920 | tf_op jit(solution)/shard_map/ppermute | solution.py:254
  121.3 5.1 %collective-permute-start.20 = (bf16[192,256]{1,0:T(8,128)(2,1)S(1)}, bf16[192,256]{1,0:T(8,128)(2,1)S(1)}, u32[]{:S(2)}, u32[]{:S(2)}) collective-permute-start(bf16[192,256]{1,0:T(8,128)(2,1)S(1)} %get-tuple-element.7), channel_id=1, source_target_pairs={{0,192},{64,0},{128,64},{192,128},{1,193},{65,1},{129,65},{193,129... | collective-permute-start | bytes 294920 | tf_op jit(solution)/shard_map/ppermute | solution.py:254
  123.6 14.1 %collective-permute-start.28 = (bf16[192,1024]{1,0:T(8,128)(2,1)S(1)}, bf16[192,1024]{1,0:T(8,128)(2,1)S(1)}, u32[]{:S(2)}, u32[]{:S(2)}) collective-permute-start(bf16[192,1024]{1,0:T(8,128)(2,1)S(1)} %constant_dynamic-update-slice_fusion.4.refs_3_), channel_id=1, source_target_pairs={{0,64},{64,128},{128,192},{192,0},{1,65},{65,129},{129,193},{193,1... | collective-permute-start | bytes 1179656 | tf_op jit(solution)/shard_map/ppermute | solution.py:254
  123.7 15.6 %collective-permute-start.30 = (bf16[192,1024]{1,0:T(8,128)(2,1)S(1)}, bf16[192,1024]{1,0:T(8,128)(2,1)S(1)}, u32[]{:S(2)}, u32[]{:S(2)}) collective-permute-start(bf16[192,1024]{1,0:T(8,128)(2,1)S(1)} %constant_dynamic-update-slice_fusion.4.refs_3_), channel_id=1, source_target_pairs={{0,192},{64,0},{128,64},{192,128},{1,193},{65,1},{129,65},{193,129... | collective-permute-start | bytes 1179656 | tf_op jit(solution)/shard_map/ppermute | solution.py:254
  126.4 14.4 %collective-permute-start.21 = (bf16[192,1024]{1,0:T(8,128)(2,1)S(1)}, bf16[192,1024]{1,0:T(8,128)(2,1)S(1)}, u32[]{:S(2)}, u32[]{:S(2)}) collective-permute-start(bf16[192,1024]{1,0:T(8,128)(2,1)S(1)} %constant_dynamic-update-slice_fusion.refs_0_), channel_id=1, source_target_pairs={{0,1},{1,2},{2,3},{3,0},{4,5},{5,6},{6,7},{7,4},{8,9},{9,10},{10,1... | collective-permute-start | bytes 1179656 | tf_op jit(solution)/shard_map/ppermute | solution.py:254
  126.6 14.3 %collective-permute-start.23 = (bf16[192,1024]{1,0:T(8,128)(2,1)S(1)}, bf16[192,1024]{1,0:T(8,128)(2,1)S(1)}, u32[]{:S(2)}, u32[]{:S(2)}) collective-permute-start(bf16[192,1024]{1,0:T(8,128)(2,1)S(1)} %constant_dynamic-update-slice_fusion.refs_0_), channel_id=1, source_target_pairs={{0,3},{1,0},{2,1},{3,2},{4,7},{5,4},{6,5},{7,6},{8,11},{9,8},{10,9... | collective-permute-start | bytes 1179656 | tf_op jit(solution)/shard_map/ppermute | solution.py:254
  129.8 21.6 %all-to-all-start.1 = ((f32[16,3,4,128]{3,2,1,0:T(4,128)}), f32[16,3,4,128]{3,2,1,0:T(4,128)S(1)}, u32[]{:S(2)}, u32[]{:S(2)}) async-start(f32[16,3,4,128]{3,2,1,0:T(4,128)} %broadcast_in_dim.19), calls=%async_computation.1 | async-start | bytes 196608 | tf_op jit(solution)/shard_map/all_to_all | solution.py:412
  137.7 10.7 %collective-permute-start.29 = (bf16[192,512]{1,0:T(8,128)(2,1)S(1)}, bf16[192,512]{1,0:T(8,128)(2,1)S(1)}, u32[]{:S(2)}, u32[]{:S(2)}) collective-permute-start(bf16[192,512]{1,0:T(8,128)(2,1)S(1)} %slice.57), channel_id=1, source_target_pairs={{0,64},{64,128},{128,192},{192,0},{1,65},{65,129},{129,193},{193,1... | collective-permute-start | bytes 589832 | tf_op jit(solution)/shard_map/ppermute | solution.py:254
  139.3 9.1 %collective-permute-start.31 = (bf16[192,512]{1,0:T(8,128)(2,1)S(1)}, bf16[192,512]{1,0:T(8,128)(2,1)S(1)}, u32[]{:S(2)}, u32[]{:S(2)}) collective-permute-start(bf16[192,512]{1,0:T(8,128)(2,1)S(1)} %slice.58), channel_id=1, source_target_pairs={{0,192},{64,0},{128,64},{192,128},{1,193},{65,1},{129,65},{193,129... | collective-permute-start | bytes 589832 | tf_op jit(solution)/shard_map/ppermute | solution.py:254
  140.8 7.6 %collective-permute-start.22 = (bf16[192,512]{1,0:T(8,128)(2,1)S(1)}, bf16[192,512]{1,0:T(8,128)(2,1)S(1)}, u32[]{:S(2)}, u32[]{:S(2)}) collective-permute-start(bf16[192,512]{1,0:T(8,128)(2,1)S(1)} %slice.55), channel_id=1, source_target_pairs={{0,1},{1,2},{2,3},{3,0},{4,5},{5,6},{6,7},{7,4},{8,9},{9,10},{10,1... | collective-permute-start | bytes 589832 | tf_op jit(solution)/shard_map/ppermute | solution.py:254
  140.9 7.5 %collective-permute-start.24 = (bf16[192,512]{1,0:T(8,128)(2,1)S(1)}, bf16[192,512]{1,0:T(8,128)(2,1)S(1)}, u32[]{:S(2)}, u32[]{:S(2)}) collective-permute-start(bf16[192,512]{1,0:T(8,128)(2,1)S(1)} %slice.56), channel_id=1, source_target_pairs={{0,3},{1,0},{2,1},{3,2},{4,7},{5,4},{6,5},{7,6},{8,11},{9,8},{10,9... | collective-permute-start | bytes 589832 | tf_op jit(solution)/shard_map/ppermute | solution.py:254
  (36 other events, 241.9 us)
Sparse Core Ops, SparseCore 0:
  10.4 79.5 all-gather.7
  91.8 47.0 all-gather.5

commit v9 on v7

--- a/solution.py
+++ b/solution.py
@@ -365,7 +365,7 @@
         jnp.broadcast_to(stats[None], (owners, *stats.shape)), "seq", split_axis=0, concat_axis=0, tiled=True
     ).reshape(owners * span_count // 2, *stats.shape[1:])
     neighbour_gradient = pl.pallas_call(
-        functools.partial(pair_backward, 4),
+        functools.partial(pair_backward, 8),
         cost_estimate=cost(10),
         out_shape=jax.ShapeDtypeStruct(neighbour_states.shape, jnp.bfloat16),
         in_specs=[SMEM, ANY, VMEM, VMEM, VMEM],

time: 155 us -> 155 us (level)
  no operation moved by 1% of the time
where the time goes in v9:
time: 155 us; the launch traced here: 154 us
  waiting for transfers between devices  44.2 us (29%)
  starting transfers between devices  36.1 us (23%)
  Pallas kernels  24.2 us (16%)
  blocking collectives  23.3 us (15%)
  between operations  14.3 us (9%)
  local copies, waits for them, and re-layouts  11 us (7%)
    all_to_all x1, waiting for transfers between devices, local(): weight = lax.all_to_all(cut, FEATS, split_axis=0, concat_axis=0, tiled=True)  27 us
    all_gather x1, blocking collectives, local(): lax.all_gather(jnp.stack([retrieved.reshape(request_count), valid_blocks....  23.3 us
    ppermute x14, starting transfers between devices, shifted(): lax.ppermute(value, axis, [(source, (source + steps) % count) for source...  20.8 us
    all_gather x1, waiting for transfers between devices, local(): store = lax.all_gather(neighbour_states, 'seq', axis=0)  14.4 us
    pallas_call x1, Pallas kernels, local(): pl.pallas_call(functools.partial(pair_backward, 8), cost_estimate=cost(10...  9.21 us
    all_to_all x1, starting transfers between devices, local(): weight = lax.all_to_all(cut, FEATS, split_axis=0, concat_axis=0, tiled=True)  7.72 us
    all_to_all x1, starting transfers between devices, local(): lax.all_to_all(jnp.broadcast_to(stats[None], (owners, *stats.shape)), 'se...  7.32 us
    unnamed x28, local copies, waits for them, and re-layouts  6.23 us
  transfers between devices with their start and end apart: 19, of which 3 were waited for; matrix products, arithmetic and copies ran while one was open for 7% of the time, Pallas kernels for 10%

profile of v9, /device:TPU:1, one launch (start us, length us, event | category | flops | bytes accessed | tf_op | source)
XLA Modules:
  0.0 154.5 jit_solution(7907271647192813340)
XLA Ops:
  7.2 0.7 all-gather.8.cloned.1.call-update
  7.9 4.4 %shard_map.77 = bf16[16,256,256]{2,1,0:T(8,128)(2,1)} custom-call(s32[1]{0:T(128)} %bitcast.6.core, bf16[256,8192]{1,0:T(8,128)(2,1)} %columns.1), custom_call_target="tpu_custom_call" | custom-call | tf_op jit(solution)/shard_map/pallas_call | solution.py:285
  12.3 7.7 %all-to-all-start = ((bf16[16,256,256]{2,1,0:T(8,128)(2,1)}), bf16[16,256,256]{2,1,0:T(8,128)(2,1)S(1)}, u32[]{:S(2)}, u32[]{:S(2)}) async-start(bf16[16,256,256]{2,1,0:T(8,128)(2,1)} %shard_map.77), calls=%async_computation | async-start | bytes 4194304 | tf_op jit(solution)/shard_map/all_to_all | solution.py:295
  20.1 0.8 pad_maximum_fusion.refs_0_
  20.9 27.0 %all-to-all-done.refs_3_.refs_6_.refs_4_.refs_1_ = bf16[16,256,256]{2,1,0:T(8,128)(2,1)S(1)} async-done(((bf16[16,256,256]{2,1,0:T(8,128)(2,1)}), bf16[16,256,256]{2,1,0:T(8,128)(2,1)S(1)}, u32[]{:S(2)}, u32[]{:S(2)}) %all-to-all-start) | async-done | bytes 2097184 | tf_op jit(solution)/shard_map/all_to_all | solution.py:295
  47.9 1.3 copy-done
  49.6 23.3 %all-gather.2 = s32[16,2,12]{2,1,0:T(2,128)S(1)} all-gather(s32[1,2,12]{2,1,0:T(2,128)S(1)} %add_bitcast_fusion), channel_id=2, replica_groups=mesh['grp'=4,'seq'=16,'tp'=4] {'seq'}, dimensions={0}, use_global_device_ids=true | all-gather | bytes 1632 | tf_op jit(solution)/shard_map/all_gather | solution.py:297
  75.4 14.4 %all-gather.8.cloned.1.call-done = bf16[32,6,128,256]{3,2,1,0:T(8,128)(2,1)} async-done(((bf16[2,6,128,256]{3,2,1,0:T(8,128)(2,1)}), bf16[32,6,128,256]{3,2,1,0:T(8,128)(2,1)}) %all-gather.8.cloned.1.call-update) | async-done | bytes 12582928 | tf_op jit(solution)/shard_map/all_gather | solution.py:315
  89.8 0.7 copy-done.6
  90.5 4.3 %shard_map.79 = (bf16[192,256]{1,0:T(8,128)(2,1)S(1)}, bf16[192,256]{1,0:T(8,128)(2,1)S(1)}, f32[3,4,128]{2,1,0:T(4,128)S(1)}) custom-call(s32[14]{0:T(128)S(1)} %copy-done.6, bf16[384,256]{1,0:T(8,128)(2,1)S(1)} %copy-done.3, bf16[384,256]{1,0:T(8,128)(2,1)S(1)} %copy-done.4, bf16[16,2,6,128,256]{4,3,2,1,0:T(8,128)(2,1)} %shard_map.78.store), custom_call_target="tpu_custom_call" | custom-call | flops 5000000000 | bytes 8388608 | tf_op jit(solution)/shard_map/pallas_call | solution.py:322
  94.8 1.3 collective-permute-start.7
  96.1 2.4 %collective-permute-start.8 = (bf16[192,256]{1,0:T(8,128)(2,1)S(1)}, bf16[192,256]{1,0:T(8,128)(2,1)S(1)}, u32[]{:S(2)}, u32[]{:S(2)}) collective-permute-start(bf16[192,256]{1,0:T(8,128)(2,1)S(1)} %get-tuple-element.8), channel_id=1, source_target_pairs={{0,2},{1,3},{2,0},{3,1},{4,6},{5,7},{6,4},{7,5},{8,10},{9,11},{10,... | collective-permute-start | bytes 294920 | tf_op jit(solution)/shard_map/ppermute | solution.py:223
  98.5 1.2 collective-permute-start.9
  99.7 1.2 collective-permute-start
  100.8 0.6 constant_dynamic-update-slice_fusion.7
  102.1 2.4 %collective-permute-start.1 = (bf16[192,256]{1,0:T(8,128)(2,1)S(1)}, bf16[192,256]{1,0:T(8,128)(2,1)S(1)}, u32[]{:S(2)}, u32[]{:S(2)}) collective-permute-start(bf16[192,256]{1,0:T(8,128)(2,1)S(1)} %get-tuple-element.7), channel_id=1, source_target_pairs={{0,128},{64,192},{128,0},{192,64},{1,129},{65,193},{129,1},{193,65... | collective-permute-start | bytes 294920 | tf_op jit(solution)/shard_map/ppermute | solution.py:223
  105.2 1.2 collective-permute-start.2
  106.4 0.6 constant_dynamic-update-slice_fusion.5
  107.0 0.6 constant_dynamic-update-slice_fusion.4.refs_3_
  108.0 2.4 %collective-permute-start.12 = (bf16[192,1024]{1,0:T(8,128)(2,1)}, bf16[192,1024]{1,0:T(8,128)(2,1)S(1)}, u32[]{:S(2)}, u32[]{:S(2)}) collective-permute-start(bf16[192,1024]{1,0:T(8,128)(2,1)} %constant_dynamic-update-slice_fusion.4.refs_3_), channel_id=1, source_target_pairs={{0,192},{64,0},{128,64},{192,128},{1,193},{65,1},{129,65},{193,129... | collective-permute-start | bytes 1179656 | tf_op jit(solution)/shard_map/ppermute | solution.py:223
  111.0 0.6 constant_dynamic-update-slice_fusion.1
  111.7 0.6 constant_dynamic-update-slice_fusion.refs_0_
  112.6 2.4 %collective-permute-start.5 = (bf16[192,1024]{1,0:T(8,128)(2,1)}, bf16[192,1024]{1,0:T(8,128)(2,1)}, u32[]{:S(2)}, u32[]{:S(2)}) collective-permute-start(bf16[192,1024]{1,0:T(8,128)(2,1)} %constant_dynamic-update-slice_fusion.refs_0_), channel_id=1, source_target_pairs={{0,3},{1,0},{2,1},{3,2},{4,7},{5,4},{6,5},{7,6},{8,11},{9,8},{10,9... | collective-permute-start | bytes 1179656 | tf_op jit(solution)/shard_map/ppermute | solution.py:223
  115.0 0.7 broadcast_in_dim.19
  115.6 7.3 %all-to-all-start.1 = ((f32[16,3,4,128]{3,2,1,0:T(4,128)}), f32[16,3,4,128]{3,2,1,0:T(4,128)S(1)}, u32[]{:S(2)}, u32[]{:S(2)}) async-start(f32[16,3,4,128]{3,2,1,0:T(4,128)} %broadcast_in_dim.19), calls=%async_computation.1 | async-start | bytes 196608 | tf_op jit(solution)/shard_map/all_to_all | solution.py:364
  123.1 2.9 %collective-permute-start.13 = (bf16[192,512]{1,0:T(8,128)(2,1)S(1)}, bf16[192,512]{1,0:T(8,128)(2,1)S(1)}, u32[]{:S(2)}, u32[]{:S(2)}) collective-permute-start(bf16[192,512]{1,0:T(8,128)(2,1)S(1)} %slice.32), channel_id=1, source_target_pairs={{0,192},{64,0},{128,64},{192,128},{1,193},{65,1},{129,65},{193,129... | collective-permute-start | bytes 589832 | tf_op jit(solution)/shard_map/ppermute | solution.py:223
  126.2 0.9 slice.30
  127.1 2.7 %collective-permute-start.6 = (bf16[192,512]{1,0:T(8,128)(2,1)S(1)}, bf16[192,512]{1,0:T(8,128)(2,1)S(1)}, u32[]{:S(2)}, u32[]{:S(2)}) collective-permute-start(bf16[192,512]{1,0:T(8,128)(2,1)S(1)} %slice.30), channel_id=1, source_target_pairs={{0,3},{1,0},{2,1},{3,2},{4,7},{5,4},{6,5},{7,6},{8,11},{9,8},{10,9... | collective-permute-start | bytes 589832 | tf_op jit(solution)/shard_map/ppermute | solution.py:223
  129.9 3.4 %shard_map.80.refs_6_ = f32[2,384,256]{2,1,0:T(8,128)S(1)} custom-call(bf16[192,1024]{1,0:T(8,128)(2,1)} %constant_dynamic-update-slice_fusion.refs_0_, bf16[192,1024]{1,0:T(8,128)(2,1)S(1)} %collective-permute-done.3.refs_1_, bf16[192,1024]{1,0:T(8,128)(2,1)} %collective-permute-done.5.refs_2_, ...), custom_call_target="tpu_custom_call" | custom-call | flops 3000000000 | bytes 8388608 | tf_op jit(solution)/shard_map/pallas_call | solution.py:344
  133.3 3.0 %shard_map.81 = (bf16[384,512]{1,0:T(8,128)(2,1)}, f32[8,128]{1,0:T(8,128)S(1)}) custom-call(bf16[192,512]{1,0:T(8,128)(2,1)S(1)} %collective-permute-done.4.refs_0_, bf16[192,512]{1,0:T(8,128)(2,1)S(1)} %collective-permute-done.6.refs_1_, bf16[192,512]{1,0:T(8,128)(2,1)S(1)} %collective-permute-done.11.refs_2_, ...), custom_call_target="tpu_custom_call" | custom-call | flops 2000000000 | bytes 8388608 | tf_op jit(solution)/shard_map/pallas_call | solution.py:352
  136.3 2.1 %all-gather.6.cloned.1.call-done.rows = bf16[6144,512]{1,0:T(8,128)(2,1)} async-done(((bf16[384,512]{1,0:T(8,128)(2,1)}), bf16[6144,512]{1,0:T(8,128)(2,1)}) %all-gather.6.cloned.1.call-update) | async-done | bytes 6291472 | tf_op jit(solution)/shard_map/all_gather | solution.py:318
  138.4 9.2 %shard_map.83 = bf16[2,6,128,256]{3,2,1,0:T(8,128)(2,1)} custom-call(s32[32]{0:T(128)S(1)} %copy-done.5, bf16[6144,512]{1,0:T(8,128)(2,1)} %all-gather.6.cloned.1.call-done.rows, bf16[2,6,128,256]{3,2,1,0:T(8,128)(2,1)S(1)} %copy-done.2, f32[48,4,128]{2,1,0:T(4,128)S(1)} %bitcast.19, f32[8,128]{1,0:T(8,128)S(1)} %get-tuple-element.11.rest_0_), custom_call_target="tpu_custom_call" | custom-call | flops 10000000000 | bytes 8388608 | tf_op jit(solution)/shard_map/pallas_call | solution.py:367
  (74 shorter events, 5.8 us)
Async XLA Ops:
  7.2 82.7 %all-gather.8.cloned.1.call-start = ((), (), s32[]{:S(2)}) async-start(), calls=%async_computation.3 | async-start | bytes 13369344 | tf_op jit(solution)/shard_map/all_gather | solution.py:315
  7.9 12.2 %copy-start.3 = (bf16[384,256]{1,0:T(8,128)(2,1)S(1)}, bf16[384,256]{1,0:T(8,128)(2,1)}, u32[]{:S(2)}) copy-start(bf16[384,256]{1,0:T(8,128)(2,1)} %queries.1) | copy-start | bytes 589828
  7.9 12.2 %copy-start.4 = (bf16[384,256]{1,0:T(8,128)(2,1)S(1)}, bf16[384,256]{1,0:T(8,128)(2,1)}, u32[]{:S(2)}) copy-start(bf16[384,256]{1,0:T(8,128)(2,1)} %cotangents.1) | copy-start | bytes 589828
  12.3 36.9 %copy-start.7 = (s32[6,2]{0,1:T(2,128)S(1)}, s32[6,2]{0,1:T(2,128)}, u32[]{:S(2)}) copy-start(s32[6,2]{0,1:T(2,128)} %param.8) | copy-start | bytes 148
  12.3 37.1 %copy-start.8 = (s32[6,2]{0,1:T(2,128)S(1)}, s32[6,2]{0,1:T(2,128)}, u32[]{:S(2)}) copy-start(s32[6,2]{0,1:T(2,128)} %param.9) | copy-start | bytes 148
  12.3 35.6 %all-to-all-start = ((bf16[16,256,256]{2,1,0:T(8,128)(2,1)}), bf16[16,256,256]{2,1,0:T(8,128)(2,1)S(1)}, u32[]{:S(2)}, u32[]{:S(2)}) async-start(bf16[16,256,256]{2,1,0:T(8,128)(2,1)} %shard_map.77), calls=%async_computation | async-start | bytes 4194304 | tf_op jit(solution)/shard_map/all_to_all | solution.py:295
  20.0 118.4 %all-gather.6.cloned.1.call-start = ((), (), s32[]{:S(2)}) async-start(), calls=%async_computation.2 | async-start | bytes 6684672 | tf_op jit(solution)/shard_map/all_gather | solution.py:318
  47.9 1.3 copy-start
  74.5 55.4 %collective-permute-start.14 = (bf16[16,256,256]{2,1,0:T(8,128)(2,1)}, bf16[16,256,256]{2,1,0:T(8,128)(2,1)}, u32[]{:S(2)}, u32[]{:S(2)}) collective-permute-start(bf16[16,256,256]{2,1,0:T(8,128)(2,1)} %copy-done), channel_id=1, source_target_pairs={{0,4},{4,0},{8,12},{12,8},{16,20},{20,16},{24,28},{28,24},{32,36},... | collective-permute-start | bytes 6291464 | tf_op jit(solution)/shard_map/ppermute | solution.py:319
  89.8 0.7 copy-start.6
  90.5 39.4 %copy-start.1 = (bf16[16,256,256]{2,1,0:T(8,128)(2,1)S(1)}, bf16[16,256,256]{2,1,0:T(8,128)(2,1)}, u32[]{:S(2)}) copy-start(bf16[16,256,256]{2,1,0:T(8,128)(2,1)} %copy-done) | copy-start | bytes 6291460
  94.8 7.4 %collective-permute-start.7 = (bf16[192,256]{1,0:T(8,128)(2,1)S(1)}, bf16[192,256]{1,0:T(8,128)(2,1)S(1)}, u32[]{:S(2)}, u32[]{:S(2)}) collective-permute-start(bf16[192,256]{1,0:T(8,128)(2,1)S(1)} %get-tuple-element.8), channel_id=1, source_target_pairs={{0,1},{1,2},{2,3},{3,0},{4,5},{5,6},{6,7},{7,4},{8,9},{9,10},{10,1... | collective-permute-start | bytes 294920 | tf_op jit(solution)/shard_map/ppermute | solution.py:223
  96.1 9.1 %collective-permute-start.8 = (bf16[192,256]{1,0:T(8,128)(2,1)S(1)}, bf16[192,256]{1,0:T(8,128)(2,1)S(1)}, u32[]{:S(2)}, u32[]{:S(2)}) collective-permute-start(bf16[192,256]{1,0:T(8,128)(2,1)S(1)} %get-tuple-element.8), channel_id=1, source_target_pairs={{0,2},{1,3},{2,0},{3,1},{4,6},{5,7},{6,4},{7,5},{8,10},{9,11},{10,... | collective-permute-start | bytes 294920 | tf_op jit(solution)/shard_map/ppermute | solution.py:223
  98.5 8.5 %collective-permute-start.9 = (bf16[192,256]{1,0:T(8,128)(2,1)S(1)}, bf16[192,256]{1,0:T(8,128)(2,1)S(1)}, u32[]{:S(2)}, u32[]{:S(2)}) collective-permute-start(bf16[192,256]{1,0:T(8,128)(2,1)S(1)} %get-tuple-element.8), channel_id=1, source_target_pairs={{0,3},{1,0},{2,1},{3,2},{4,7},{5,4},{6,5},{7,6},{8,11},{9,8},{10,9... | collective-permute-start | bytes 294920 | tf_op jit(solution)/shard_map/ppermute | solution.py:223
  99.7 8.3 %collective-permute-start = (bf16[192,256]{1,0:T(8,128)(2,1)S(1)}, bf16[192,256]{1,0:T(8,128)(2,1)S(1)}, u32[]{:S(2)}, u32[]{:S(2)}) collective-permute-start(bf16[192,256]{1,0:T(8,128)(2,1)S(1)} %get-tuple-element.7), channel_id=1, source_target_pairs={{0,64},{64,128},{128,192},{192,0},{1,65},{65,129},{129,193},{193,1... | collective-permute-start | bytes 294920 | tf_op jit(solution)/shard_map/ppermute | solution.py:223
  102.1 8.9 %collective-permute-start.1 = (bf16[192,256]{1,0:T(8,128)(2,1)S(1)}, bf16[192,256]{1,0:T(8,128)(2,1)S(1)}, u32[]{:S(2)}, u32[]{:S(2)}) collective-permute-start(bf16[192,256]{1,0:T(8,128)(2,1)S(1)} %get-tuple-element.7), channel_id=1, source_target_pairs={{0,128},{64,192},{128,0},{192,64},{1,129},{65,193},{129,1},{193,65... | collective-permute-start | bytes 294920 | tf_op jit(solution)/shard_map/ppermute | solution.py:223
  105.2 6.5 %collective-permute-start.2 = (bf16[192,256]{1,0:T(8,128)(2,1)S(1)}, bf16[192,256]{1,0:T(8,128)(2,1)S(1)}, u32[]{:S(2)}, u32[]{:S(2)}) collective-permute-start(bf16[192,256]{1,0:T(8,128)(2,1)S(1)} %get-tuple-element.7), channel_id=1, source_target_pairs={{0,192},{64,0},{128,64},{192,128},{1,193},{65,1},{129,65},{193,129... | collective-permute-start | bytes 294920 | tf_op jit(solution)/shard_map/ppermute | solution.py:223
  107.7 15.3 %collective-permute-start.10 = (bf16[192,1024]{1,0:T(8,128)(2,1)}, bf16[192,1024]{1,0:T(8,128)(2,1)S(1)}, u32[]{:S(2)}, u32[]{:S(2)}) collective-permute-start(bf16[192,1024]{1,0:T(8,128)(2,1)} %constant_dynamic-update-slice_fusion.4.refs_3_), channel_id=1, source_target_pairs={{0,64},{64,128},{128,192},{192,0},{1,65},{65,129},{129,193},{193,1... | collective-permute-start | bytes 1179656 | tf_op jit(solution)/shard_map/ppermute | solution.py:223
  108.0 15.1 %collective-permute-start.12 = (bf16[192,1024]{1,0:T(8,128)(2,1)}, bf16[192,1024]{1,0:T(8,128)(2,1)S(1)}, u32[]{:S(2)}, u32[]{:S(2)}) collective-permute-start(bf16[192,1024]{1,0:T(8,128)(2,1)} %constant_dynamic-update-slice_fusion.4.refs_3_), channel_id=1, source_target_pairs={{0,192},{64,0},{128,64},{192,128},{1,193},{65,1},{129,65},{193,129... | collective-permute-start | bytes 1179656 | tf_op jit(solution)/shard_map/ppermute | solution.py:223
  112.3 13.8 %collective-permute-start.3 = (bf16[192,1024]{1,0:T(8,128)(2,1)}, bf16[192,1024]{1,0:T(8,128)(2,1)S(1)}, u32[]{:S(2)}, u32[]{:S(2)}) collective-permute-start(bf16[192,1024]{1,0:T(8,128)(2,1)} %constant_dynamic-update-slice_fusion.refs_0_), channel_id=1, source_target_pairs={{0,1},{1,2},{2,3},{3,0},{4,5},{5,6},{6,7},{7,4},{8,9},{9,10},{10,1... | collective-permute-start | bytes 1179656 | tf_op jit(solution)/shard_map/ppermute | solution.py:223
  112.6 13.6 %collective-permute-start.5 = (bf16[192,1024]{1,0:T(8,128)(2,1)}, bf16[192,1024]{1,0:T(8,128)(2,1)}, u32[]{:S(2)}, u32[]{:S(2)}) collective-permute-start(bf16[192,1024]{1,0:T(8,128)(2,1)} %constant_dynamic-update-slice_fusion.refs_0_), channel_id=1, source_target_pairs={{0,3},{1,0},{2,1},{3,2},{4,7},{5,4},{6,5},{7,6},{8,11},{9,8},{10,9... | collective-permute-start | bytes 1179656 | tf_op jit(solution)/shard_map/ppermute | solution.py:223
  115.6 22.7 %all-to-all-start.1 = ((f32[16,3,4,128]{3,2,1,0:T(4,128)}), f32[16,3,4,128]{3,2,1,0:T(4,128)S(1)}, u32[]{:S(2)}, u32[]{:S(2)}) async-start(f32[16,3,4,128]{3,2,1,0:T(4,128)} %broadcast_in_dim.19), calls=%async_computation.1 | async-start | bytes 196608 | tf_op jit(solution)/shard_map/all_to_all | solution.py:364
  123.0 10.2 %collective-permute-start.11 = (bf16[192,512]{1,0:T(8,128)(2,1)S(1)}, bf16[192,512]{1,0:T(8,128)(2,1)S(1)}, u32[]{:S(2)}, u32[]{:S(2)}) collective-permute-start(bf16[192,512]{1,0:T(8,128)(2,1)S(1)} %slice.31), channel_id=1, source_target_pairs={{0,64},{64,128},{128,192},{192,0},{1,65},{65,129},{129,193},{193,1... | collective-permute-start | bytes 589832 | tf_op jit(solution)/shard_map/ppermute | solution.py:223
  123.1 10.1 %collective-permute-start.13 = (bf16[192,512]{1,0:T(8,128)(2,1)S(1)}, bf16[192,512]{1,0:T(8,128)(2,1)S(1)}, u32[]{:S(2)}, u32[]{:S(2)}) collective-permute-start(bf16[192,512]{1,0:T(8,128)(2,1)S(1)} %slice.32), channel_id=1, source_target_pairs={{0,192},{64,0},{128,64},{192,128},{1,193},{65,1},{129,65},{193,129... | collective-permute-start | bytes 589832 | tf_op jit(solution)/shard_map/ppermute | solution.py:223
  126.1 7.2 %collective-permute-start.4 = (bf16[192,512]{1,0:T(8,128)(2,1)S(1)}, bf16[192,512]{1,0:T(8,128)(2,1)S(1)}, u32[]{:S(2)}, u32[]{:S(2)}) collective-permute-start(bf16[192,512]{1,0:T(8,128)(2,1)S(1)} %slice.29), channel_id=1, source_target_pairs={{0,1},{1,2},{2,3},{3,0},{4,5},{5,6},{6,7},{7,4},{8,9},{9,10},{10,1... | collective-permute-start | bytes 589832 | tf_op jit(solution)/shard_map/ppermute | solution.py:223
  127.1 6.2 %collective-permute-start.6 = (bf16[192,512]{1,0:T(8,128)(2,1)S(1)}, bf16[192,512]{1,0:T(8,128)(2,1)S(1)}, u32[]{:S(2)}, u32[]{:S(2)}) collective-permute-start(bf16[192,512]{1,0:T(8,128)(2,1)S(1)} %slice.30), channel_id=1, source_target_pairs={{0,3},{1,0},{2,1},{3,2},{4,7},{5,4},{6,5},{7,6},{8,11},{9,8},{10,9... | collective-permute-start | bytes 589832 | tf_op jit(solution)/shard_map/ppermute | solution.py:223
  133.2 5.2 %copy-start.2 = (bf16[2,6,128,256]{3,2,1,0:T(8,128)(2,1)S(1)}, bf16[2,6,128,256]{3,2,1,0:T(8,128)(2,1)}, u32[]{:S(2)}) copy-start(bf16[2,6,128,256]{3,2,1,0:T(8,128)(2,1)} %states.1) | copy-start | bytes 2359300
  133.2 5.2 %copy-start.5 = (s32[32]{0:T(128)S(1)}, s32[32]{0:T(128)}, u32[]{:S(2)}) copy-start(s32[32]{0:T(128)} %reshape.145.refs_1_.slots) | copy-start | bytes 388
Sparse Core Ops, SparseCore 0:
  9.8 79.9 all-gather.7
  91.7 46.6 all-gather.5

commit v10 on v9

--- a/solution.py
+++ b/solution.py
@@ -313,7 +313,7 @@
     codes = lax.dynamic_slice_in_dim(plain, me * request_count, request_count + KNB, 0)
 
     store = lax.all_gather(neighbour_states, "seq", axis=0)
-    store = tied(store, slots, codes, weight)
+    store = tied(store, slots, weight)
     both = tied(jnp.concatenate([queries, attention_cotangent], axis=1), weight)
     gathered = lax.all_gather(both, "seq", axis=0, tiled=True)
     weight_other = lax.ppermute(weight, "seq", [(source, source ^ 1) for source in range(owners)])

time: 155 us -> 155 us (level)
    unnamed x28 -> x26, local copies, waits for them, and re-layouts: 6.23 us -> 5.58 us
  transfers between devices with their start and end apart: 19 -> 19, of which waited for: 3 -> 3; matrix products, arithmetic and copies ran while one was open for 7% -> 6% of each run, Pallas kernels for 10% -> 10%
where the time goes in v10:
time: 155 us; the launch traced here: 154 us
  waiting for transfers between devices  45.2 us (29%)
  starting transfers between devices  36.2 us (23%)
  Pallas kernels  24.1 us (16%)
  blocking collectives  23.3 us (15%)
  between operations  14.3 us (9%)
  local copies, waits for them, and re-layouts  9.77 us (6%)
    all_to_all x1, waiting for transfers between devices, local(): weight = lax.all_to_all(cut, FEATS, split_axis=0, concat_axis=0, tiled=True)  27 us
    all_gather x1, blocking collectives, local(): lax.all_gather(jnp.stack([retrieved.reshape(request_count), valid_blocks....  23.3 us
    ppermute x14, starting transfers between devices, shifted(): lax.ppermute(value, axis, [(source, (source + steps) % count) for source...  20.8 us
    all_gather x1, waiting for transfers between devices, local(): store = lax.all_gather(neighbour_states, 'seq', axis=0)  14.9 us
    pallas_call x1, Pallas kernels, local(): pl.pallas_call(functools.partial(pair_backward, 8), cost_estimate=cost(10...  9.04 us
    all_to_all x1, starting transfers between devices, local(): weight = lax.all_to_all(cut, FEATS, split_axis=0, concat_axis=0, tiled=True)  7.72 us
    all_to_all x1, starting transfers between devices, local(): lax.all_to_all(jnp.broadcast_to(stats[None], (owners, *stats.shape)), 'se...  7.33 us
    unnamed x26, local copies, waits for them, and re-layouts  5.58 us
  transfers between devices with their start and end apart: 19, of which 3 were waited for; matrix products, arithmetic and copies ran while one was open for 6% of the time, Pallas kernels for 10%

profile of v10, /device:TPU:1, one launch (start us, length us, event | category | flops | bytes accessed | tf_op | source)
XLA Modules:
  0.0 154.3 jit_solution(5167323699190635745)
XLA Ops:
  7.2 0.7 all-gather.8.cloned.1.call-update
  7.9 4.4 %shard_map.77 = bf16[16,256,256]{2,1,0:T(8,128)(2,1)} custom-call(s32[1]{0:T(128)} %bitcast.6.core, bf16[256,8192]{1,0:T(8,128)(2,1)} %columns.1), custom_call_target="tpu_custom_call" | custom-call | tf_op jit(solution)/shard_map/pallas_call | solution.py:285
  12.3 7.7 %all-to-all-start = ((bf16[16,256,256]{2,1,0:T(8,128)(2,1)}), bf16[16,256,256]{2,1,0:T(8,128)(2,1)S(1)}, u32[]{:S(2)}, u32[]{:S(2)}) async-start(bf16[16,256,256]{2,1,0:T(8,128)(2,1)} %shard_map.77), calls=%async_computation | async-start | bytes 4194304 | tf_op jit(solution)/shard_map/all_to_all | solution.py:295
  20.1 0.8 pad_maximum_fusion.refs_0_
  20.9 27.0 %all-to-all-done.refs_2_.refs_6_.refs_4_.refs_1_ = bf16[16,256,256]{2,1,0:T(8,128)(2,1)S(1)} async-done(((bf16[16,256,256]{2,1,0:T(8,128)(2,1)}), bf16[16,256,256]{2,1,0:T(8,128)(2,1)S(1)}, u32[]{:S(2)}, u32[]{:S(2)}) %all-to-all-start) | async-done | bytes 2097184 | tf_op jit(solution)/shard_map/all_to_all | solution.py:295
  47.9 1.3 copy-done
  49.6 23.3 %all-gather.2 = s32[16,2,12]{2,1,0:T(2,128)S(1)} all-gather(s32[1,2,12]{2,1,0:T(2,128)S(1)} %add_bitcast_fusion), channel_id=2, replica_groups=mesh['grp'=4,'seq'=16,'tp'=4] {'seq'}, dimensions={0}, use_global_device_ids=true | all-gather | bytes 1632 | tf_op jit(solution)/shard_map/all_gather | solution.py:297
  75.0 14.9 %all-gather.8.cloned.1.call-done = bf16[32,6,128,256]{3,2,1,0:T(8,128)(2,1)} async-done(((bf16[2,6,128,256]{3,2,1,0:T(8,128)(2,1)}), bf16[32,6,128,256]{3,2,1,0:T(8,128)(2,1)}) %all-gather.8.cloned.1.call-update) | async-done | bytes 12582928 | tf_op jit(solution)/shard_map/all_gather | solution.py:315
  89.8 4.3 %shard_map.79 = (bf16[192,256]{1,0:T(8,128)(2,1)S(1)}, bf16[192,256]{1,0:T(8,128)(2,1)S(1)}, f32[3,4,128]{2,1,0:T(4,128)S(1)}) custom-call(s32[14]{0:T(128)S(1)} %pad_dynamic-slice_fusion.codes, bf16[384,256]{1,0:T(8,128)(2,1)S(1)} %copy-done.3, bf16[384,256]{1,0:T(8,128)(2,1)S(1)} %copy-done.4, bf16[16,2,6,128,256]{4,3,2,1,0:T(8,128)(2,1)} %shard_map.78.store), custom_call_target="tpu_custom_call" | custom-call | flops 5000000000 | bytes 8388608 | tf_op jit(solution)/shard_map/pallas_call | solution.py:322
  94.1 1.3 collective-permute-start
  95.4 2.4 %collective-permute-start.1 = (bf16[192,256]{1,0:T(8,128)(2,1)S(1)}, bf16[192,256]{1,0:T(8,128)(2,1)S(1)}, u32[]{:S(2)}, u32[]{:S(2)}) collective-permute-start(bf16[192,256]{1,0:T(8,128)(2,1)S(1)} %get-tuple-element.7), channel_id=1, source_target_pairs={{0,128},{64,192},{128,0},{192,64},{1,129},{65,193},{129,1},{193,65... | collective-permute-start | bytes 294920 | tf_op jit(solution)/shard_map/ppermute | solution.py:223
  97.8 1.2 collective-permute-start.2
  99.0 1.2 collective-permute-start.7
  100.2 0.6 constant_dynamic-update-slice_fusion.3
  100.8 0.6 constant_dynamic-update-slice_fusion.7
  101.5 2.4 %collective-permute-start.8 = (bf16[192,256]{1,0:T(8,128)(2,1)S(1)}, bf16[192,256]{1,0:T(8,128)(2,1)S(1)}, u32[]{:S(2)}, u32[]{:S(2)}) collective-permute-start(bf16[192,256]{1,0:T(8,128)(2,1)S(1)} %get-tuple-element.8), channel_id=1, source_target_pairs={{0,2},{1,3},{2,0},{3,1},{4,6},{5,7},{6,4},{7,5},{8,10},{9,11},{10,... | collective-permute-start | bytes 294920 | tf_op jit(solution)/shard_map/ppermute | solution.py:223
  103.9 0.6 constant_dynamic-update-slice_fusion.2
  104.6 1.2 collective-permute-start.9
  106.4 0.6 constant_dynamic-update-slice_fusion.refs_0_
  107.3 2.4 %collective-permute-start.5 = (bf16[192,1024]{1,0:T(8,128)(2,1)}, bf16[192,1024]{1,0:T(8,128)(2,1)S(1)}, u32[]{:S(2)}, u32[]{:S(2)}) collective-permute-start(bf16[192,1024]{1,0:T(8,128)(2,1)} %constant_dynamic-update-slice_fusion.refs_0_), channel_id=1, source_target_pairs={{0,3},{1,0},{2,1},{3,2},{4,7},{5,4},{6,5},{7,6},{8,11},{9,8},{10,9... | collective-permute-start | bytes 1179656 | tf_op jit(solution)/shard_map/ppermute | solution.py:223
  110.3 0.6 constant_dynamic-update-slice_fusion.5
  111.0 0.6 constant_dynamic-update-slice_fusion.4.refs_3_
  111.9 2.4 %collective-permute-start.12 = (bf16[192,1024]{1,0:T(8,128)(2,1)}, bf16[192,1024]{1,0:T(8,128)(2,1)}, u32[]{:S(2)}, u32[]{:S(2)}) collective-permute-start(bf16[192,1024]{1,0:T(8,128)(2,1)} %constant_dynamic-update-slice_fusion.4.refs_3_), channel_id=1, source_target_pairs={{0,192},{64,0},{128,64},{192,128},{1,193},{65,1},{129,65},{193,129... | collective-permute-start | bytes 1179656 | tf_op jit(solution)/shard_map/ppermute | solution.py:223
  114.3 0.7 broadcast_in_dim.19
  115.0 7.3 %all-to-all-start.1 = ((f32[16,3,4,128]{3,2,1,0:T(4,128)}), f32[16,3,4,128]{3,2,1,0:T(4,128)S(1)}, u32[]{:S(2)}, u32[]{:S(2)}) async-start(f32[16,3,4,128]{3,2,1,0:T(4,128)} %broadcast_in_dim.19), calls=%async_computation.1 | async-start | bytes 196608 | tf_op jit(solution)/shard_map/all_to_all | solution.py:364
  122.5 2.9 %collective-permute-start.6 = (bf16[192,512]{1,0:T(8,128)(2,1)S(1)}, bf16[192,512]{1,0:T(8,128)(2,1)S(1)}, u32[]{:S(2)}, u32[]{:S(2)}) collective-permute-start(bf16[192,512]{1,0:T(8,128)(2,1)S(1)} %slice.30), channel_id=1, source_target_pairs={{0,3},{1,0},{2,1},{3,2},{4,7},{5,4},{6,5},{7,6},{8,11},{9,8},{10,9... | collective-permute-start | bytes 589832 | tf_op jit(solution)/shard_map/ppermute | solution.py:223
  125.5 0.9 slice.32
  126.5 2.7 %collective-permute-start.13 = (bf16[192,512]{1,0:T(8,128)(2,1)S(1)}, bf16[192,512]{1,0:T(8,128)(2,1)S(1)}, u32[]{:S(2)}, u32[]{:S(2)}) collective-permute-start(bf16[192,512]{1,0:T(8,128)(2,1)S(1)} %slice.32), channel_id=1, source_target_pairs={{0,192},{64,0},{128,64},{192,128},{1,193},{65,1},{129,65},{193,129... | collective-permute-start | bytes 589832 | tf_op jit(solution)/shard_map/ppermute | solution.py:223
  129.2 3.4 %shard_map.80.refs_6_ = f32[2,384,256]{2,1,0:T(8,128)S(1)} custom-call(bf16[192,1024]{1,0:T(8,128)(2,1)} %constant_dynamic-update-slice_fusion.refs_0_, bf16[192,1024]{1,0:T(8,128)(2,1)S(1)} %collective-permute-done.3.refs_1_, bf16[192,1024]{1,0:T(8,128)(2,1)S(1)} %collective-permute-done.5.refs_2_, ...), custom_call_target="tpu_custom_call" | custom-call | flops 3000000000 | bytes 8388608 | tf_op jit(solution)/shard_map/pallas_call | solution.py:344
  132.7 3.0 %shard_map.81 = (bf16[384,512]{1,0:T(8,128)(2,1)}, f32[8,128]{1,0:T(8,128)S(1)}) custom-call(bf16[192,512]{1,0:T(8,128)(2,1)S(1)} %collective-permute-done.4.refs_0_, bf16[192,512]{1,0:T(8,128)(2,1)S(1)} %collective-permute-done.6.refs_1_, bf16[192,512]{1,0:T(8,128)(2,1)S(1)} %collective-permute-done.11.refs_2_, ...), custom_call_target="tpu_custom_call" | custom-call | flops 2000000000 | bytes 8388608 | tf_op jit(solution)/shard_map/pallas_call | solution.py:352
  135.7 2.7 %all-gather.6.cloned.1.call-done.rows = bf16[6144,512]{1,0:T(8,128)(2,1)} async-done(((bf16[384,512]{1,0:T(8,128)(2,1)}), bf16[6144,512]{1,0:T(8,128)(2,1)}) %all-gather.6.cloned.1.call-update) | async-done | bytes 6291472 | tf_op jit(solution)/shard_map/all_gather | solution.py:318
  138.4 9.0 %shard_map.83 = bf16[2,6,128,256]{3,2,1,0:T(8,128)(2,1)} custom-call(s32[32]{0:T(128)S(1)} %copy-done.5, bf16[6144,512]{1,0:T(8,128)(2,1)} %all-gather.6.cloned.1.call-done.rows, bf16[2,6,128,256]{3,2,1,0:T(8,128)(2,1)S(1)} %copy-done.2, f32[48,4,128]{2,1,0:T(4,128)S(1)} %bitcast.19, f32[8,128]{1,0:T(8,128)S(1)} %get-tuple-element.11.rest_0_), custom_call_target="tpu_custom_call" | custom-call | flops 10000000000 | bytes 8388608 | tf_op jit(solution)/shard_map/pallas_call | solution.py:367
  (72 shorter events, 4.7 us)
Async XLA Ops:
  7.2 82.7 %all-gather.8.cloned.1.call-start = ((), (), s32[]{:S(2)}) async-start(), calls=%async_computation.3 | async-start | bytes 13369344 | tf_op jit(solution)/shard_map/all_gather | solution.py:315
  7.9 12.2 %copy-start.3 = (bf16[384,256]{1,0:T(8,128)(2,1)S(1)}, bf16[384,256]{1,0:T(8,128)(2,1)}, u32[]{:S(2)}) copy-start(bf16[384,256]{1,0:T(8,128)(2,1)} %queries.1) | copy-start | bytes 589828
  7.9 12.2 %copy-start.4 = (bf16[384,256]{1,0:T(8,128)(2,1)S(1)}, bf16[384,256]{1,0:T(8,128)(2,1)}, u32[]{:S(2)}) copy-start(bf16[384,256]{1,0:T(8,128)(2,1)} %cotangents.1) | copy-start | bytes 589828
  12.3 36.9 %copy-start.6 = (s32[6,2]{0,1:T(2,128)S(1)}, s32[6,2]{0,1:T(2,128)}, u32[]{:S(2)}) copy-start(s32[6,2]{0,1:T(2,128)} %param.9) | copy-start | bytes 148
  12.3 37.1 %copy-start.7 = (s32[6,2]{0,1:T(2,128)S(1)}, s32[6,2]{0,1:T(2,128)}, u32[]{:S(2)}) copy-start(s32[6,2]{0,1:T(2,128)} %param.8) | copy-start | bytes 148
  12.3 35.6 %all-to-all-start = ((bf16[16,256,256]{2,1,0:T(8,128)(2,1)}), bf16[16,256,256]{2,1,0:T(8,128)(2,1)S(1)}, u32[]{:S(2)}, u32[]{:S(2)}) async-start(bf16[16,256,256]{2,1,0:T(8,128)(2,1)} %shard_map.77), calls=%async_computation | async-start | bytes 4194304 | tf_op jit(solution)/shard_map/all_to_all | solution.py:295
  20.0 118.3 %all-gather.6.cloned.1.call-start = ((), (), s32[]{:S(2)}) async-start(), calls=%async_computation.2 | async-start | bytes 6684672 | tf_op jit(solution)/shard_map/all_gather | solution.py:318
  47.9 1.3 copy-start
  73.6 55.6 %collective-permute-start.14 = (bf16[16,256,256]{2,1,0:T(8,128)(2,1)}, bf16[16,256,256]{2,1,0:T(8,128)(2,1)}, u32[]{:S(2)}, u32[]{:S(2)}) collective-permute-start(bf16[16,256,256]{2,1,0:T(8,128)(2,1)} %copy-done), channel_id=1, source_target_pairs={{0,4},{4,0},{8,12},{12,8},{16,20},{20,16},{24,28},{28,24},{32,36},... | collective-permute-start | bytes 6291464 | tf_op jit(solution)/shard_map/ppermute | solution.py:319
  89.8 39.4 %copy-start.1 = (bf16[16,256,256]{2,1,0:T(8,128)(2,1)S(1)}, bf16[16,256,256]{2,1,0:T(8,128)(2,1)}, u32[]{:S(2)}) copy-start(bf16[16,256,256]{2,1,0:T(8,128)(2,1)} %copy-done) | copy-start | bytes 6291460
  94.1 7.3 %collective-permute-start = (bf16[192,256]{1,0:T(8,128)(2,1)S(1)}, bf16[192,256]{1,0:T(8,128)(2,1)S(1)}, u32[]{:S(2)}, u32[]{:S(2)}) collective-permute-start(bf16[192,256]{1,0:T(8,128)(2,1)S(1)} %get-tuple-element.7), channel_id=1, source_target_pairs={{0,64},{64,128},{128,192},{192,0},{1,65},{65,129},{129,193},{193,1... | collective-permute-start | bytes 294920 | tf_op jit(solution)/shard_map/ppermute | solution.py:223
  95.4 9.2 %collective-permute-start.1 = (bf16[192,256]{1,0:T(8,128)(2,1)S(1)}, bf16[192,256]{1,0:T(8,128)(2,1)S(1)}, u32[]{:S(2)}, u32[]{:S(2)}) collective-permute-start(bf16[192,256]{1,0:T(8,128)(2,1)S(1)} %get-tuple-element.7), channel_id=1, source_target_pairs={{0,128},{64,192},{128,0},{192,64},{1,129},{65,193},{129,1},{193,65... | collective-permute-start | bytes 294920 | tf_op jit(solution)/shard_map/ppermute | solution.py:223
  97.8 8.6 %collective-permute-start.2 = (bf16[192,256]{1,0:T(8,128)(2,1)S(1)}, bf16[192,256]{1,0:T(8,128)(2,1)S(1)}, u32[]{:S(2)}, u32[]{:S(2)}) collective-permute-start(bf16[192,256]{1,0:T(8,128)(2,1)S(1)} %get-tuple-element.7), channel_id=1, source_target_pairs={{0,192},{64,0},{128,64},{192,128},{1,193},{65,1},{129,65},{193,129... | collective-permute-start | bytes 294920 | tf_op jit(solution)/shard_map/ppermute | solution.py:223
  99.0 8.4 %collective-permute-start.7 = (bf16[192,256]{1,0:T(8,128)(2,1)S(1)}, bf16[192,256]{1,0:T(8,128)(2,1)S(1)}, u32[]{:S(2)}, u32[]{:S(2)}) collective-permute-start(bf16[192,256]{1,0:T(8,128)(2,1)S(1)} %get-tuple-element.8), channel_id=1, source_target_pairs={{0,1},{1,2},{2,3},{3,0},{4,5},{5,6},{6,7},{7,4},{8,9},{9,10},{10,1... | collective-permute-start | bytes 294920 | tf_op jit(solution)/shard_map/ppermute | solution.py:223
  101.5 8.9 %collective-permute-start.8 = (bf16[192,256]{1,0:T(8,128)(2,1)S(1)}, bf16[192,256]{1,0:T(8,128)(2,1)S(1)}, u32[]{:S(2)}, u32[]{:S(2)}) collective-permute-start(bf16[192,256]{1,0:T(8,128)(2,1)S(1)} %get-tuple-element.8), channel_id=1, source_target_pairs={{0,2},{1,3},{2,0},{3,1},{4,6},{5,7},{6,4},{7,5},{8,10},{9,11},{10,... | collective-permute-start | bytes 294920 | tf_op jit(solution)/shard_map/ppermute | solution.py:223
  104.6 6.4 %collective-permute-start.9 = (bf16[192,256]{1,0:T(8,128)(2,1)S(1)}, bf16[192,256]{1,0:T(8,128)(2,1)S(1)}, u32[]{:S(2)}, u32[]{:S(2)}) collective-permute-start(bf16[192,256]{1,0:T(8,128)(2,1)S(1)} %get-tuple-element.8), channel_id=1, source_target_pairs={{0,3},{1,0},{2,1},{3,2},{4,7},{5,4},{6,5},{7,6},{8,11},{9,8},{10,9... | collective-permute-start | bytes 294920 | tf_op jit(solution)/shard_map/ppermute | solution.py:223
  107.0 15.3 %collective-permute-start.3 = (bf16[192,1024]{1,0:T(8,128)(2,1)}, bf16[192,1024]{1,0:T(8,128)(2,1)S(1)}, u32[]{:S(2)}, u32[]{:S(2)}) collective-permute-start(bf16[192,1024]{1,0:T(8,128)(2,1)} %constant_dynamic-update-slice_fusion.refs_0_), channel_id=1, source_target_pairs={{0,1},{1,2},{2,3},{3,0},{4,5},{5,6},{6,7},{7,4},{8,9},{9,10},{10,1... | collective-permute-start | bytes 1179656 | tf_op jit(solution)/shard_map/ppermute | solution.py:223
  107.3 15.1 %collective-permute-start.5 = (bf16[192,1024]{1,0:T(8,128)(2,1)}, bf16[192,1024]{1,0:T(8,128)(2,1)S(1)}, u32[]{:S(2)}, u32[]{:S(2)}) collective-permute-start(bf16[192,1024]{1,0:T(8,128)(2,1)} %constant_dynamic-update-slice_fusion.refs_0_), channel_id=1, source_target_pairs={{0,3},{1,0},{2,1},{3,2},{4,7},{5,4},{6,5},{7,6},{8,11},{9,8},{10,9... | collective-permute-start | bytes 1179656 | tf_op jit(solution)/shard_map/ppermute | solution.py:223
  111.6 13.8 %collective-permute-start.10 = (bf16[192,1024]{1,0:T(8,128)(2,1)}, bf16[192,1024]{1,0:T(8,128)(2,1)S(1)}, u32[]{:S(2)}, u32[]{:S(2)}) collective-permute-start(bf16[192,1024]{1,0:T(8,128)(2,1)} %constant_dynamic-update-slice_fusion.4.refs_3_), channel_id=1, source_target_pairs={{0,64},{64,128},{128,192},{192,0},{1,65},{65,129},{129,193},{193,1... | collective-permute-start | bytes 1179656 | tf_op jit(solution)/shard_map/ppermute | solution.py:223
  111.9 13.6 %collective-permute-start.12 = (bf16[192,1024]{1,0:T(8,128)(2,1)}, bf16[192,1024]{1,0:T(8,128)(2,1)}, u32[]{:S(2)}, u32[]{:S(2)}) collective-permute-start(bf16[192,1024]{1,0:T(8,128)(2,1)} %constant_dynamic-update-slice_fusion.4.refs_3_), channel_id=1, source_target_pairs={{0,192},{64,0},{128,64},{192,128},{1,193},{65,1},{129,65},{193,129... | collective-permute-start | bytes 1179656 | tf_op jit(solution)/shard_map/ppermute | solution.py:223
  115.0 23.4 %all-to-all-start.1 = ((f32[16,3,4,128]{3,2,1,0:T(4,128)}), f32[16,3,4,128]{3,2,1,0:T(4,128)S(1)}, u32[]{:S(2)}, u32[]{:S(2)}) async-start(f32[16,3,4,128]{3,2,1,0:T(4,128)} %broadcast_in_dim.19), calls=%async_computation.1 | async-start | bytes 196608 | tf_op jit(solution)/shard_map/all_to_all | solution.py:364
  122.3 10.3 %collective-permute-start.4 = (bf16[192,512]{1,0:T(8,128)(2,1)S(1)}, bf16[192,512]{1,0:T(8,128)(2,1)S(1)}, u32[]{:S(2)}, u32[]{:S(2)}) collective-permute-start(bf16[192,512]{1,0:T(8,128)(2,1)S(1)} %slice.29), channel_id=1, source_target_pairs={{0,1},{1,2},{2,3},{3,0},{4,5},{5,6},{6,7},{7,4},{8,9},{9,10},{10,1... | collective-permute-start | bytes 589832 | tf_op jit(solution)/shard_map/ppermute | solution.py:223
  122.5 10.2 %collective-permute-start.6 = (bf16[192,512]{1,0:T(8,128)(2,1)S(1)}, bf16[192,512]{1,0:T(8,128)(2,1)S(1)}, u32[]{:S(2)}, u32[]{:S(2)}) collective-permute-start(bf16[192,512]{1,0:T(8,128)(2,1)S(1)} %slice.30), channel_id=1, source_target_pairs={{0,3},{1,0},{2,1},{3,2},{4,7},{5,4},{6,5},{7,6},{8,11},{9,8},{10,9... | collective-permute-start | bytes 589832 | tf_op jit(solution)/shard_map/ppermute | solution.py:223
  125.4 7.3 %collective-permute-start.11 = (bf16[192,512]{1,0:T(8,128)(2,1)S(1)}, bf16[192,512]{1,0:T(8,128)(2,1)S(1)}, u32[]{:S(2)}, u32[]{:S(2)}) collective-permute-start(bf16[192,512]{1,0:T(8,128)(2,1)S(1)} %slice.31), channel_id=1, source_target_pairs={{0,64},{64,128},{128,192},{192,0},{1,65},{65,129},{129,193},{193,1... | collective-permute-start | bytes 589832 | tf_op jit(solution)/shard_map/ppermute | solution.py:223
  126.5 6.2 %collective-permute-start.13 = (bf16[192,512]{1,0:T(8,128)(2,1)S(1)}, bf16[192,512]{1,0:T(8,128)(2,1)S(1)}, u32[]{:S(2)}, u32[]{:S(2)}) collective-permute-start(bf16[192,512]{1,0:T(8,128)(2,1)S(1)} %slice.32), channel_id=1, source_target_pairs={{0,192},{64,0},{128,64},{192,128},{1,193},{65,1},{129,65},{193,129... | collective-permute-start | bytes 589832 | tf_op jit(solution)/shard_map/ppermute | solution.py:223
  132.6 5.8 %copy-start.2 = (bf16[2,6,128,256]{3,2,1,0:T(8,128)(2,1)S(1)}, bf16[2,6,128,256]{3,2,1,0:T(8,128)(2,1)}, u32[]{:S(2)}) copy-start(bf16[2,6,128,256]{3,2,1,0:T(8,128)(2,1)} %states.1) | copy-start | bytes 2359300
  132.6 5.7 %copy-start.5 = (s32[32]{0:T(128)S(1)}, s32[32]{0:T(128)}, u32[]{:S(2)}) copy-start(s32[32]{0:T(128)} %reshape.145.refs_1_.slots) | copy-start | bytes 388
Sparse Core Ops, SparseCore 0:
  9.8 79.9 all-gather.7
  91.7 46.6 all-gather.5
